TPU v7x, 32 devices: a whole 2x2x4 slice. The times are simulated.
32 devices in a mesh: seq: 4 (over z), tp: 8 (over y, x, core).
Axes of the slice: x: 2, y: 2, z: 4, core: 2. Of those that a mesh axis runs over, the one named last changes fastest.
Arguments:
- tokens: bfloat16 [1024, 6144], P(('seq', 'tp')), may hold values from -6 to 6
- proj_weight: bfloat16 [6144, 4, 4096], P(None, None, 'tp'), may hold values from -0.078125 to 0.078125
- out_weight: bfloat16 [4096, 6144], P('tp'), may hold values from -0.09375 to 0.09375
- head_gain: float32 [4096], P('tp'), may hold values from 0.1 to 1.9
- decay_rate: float32 [32], P('tp'), as said below
Outputs:
- layer_out: bfloat16 [1024, 6144], P(('seq', 'tp'))
Inputs may be any that keep to these rules, and one draw needn't show every extreme that they name: `decay_rate`: every rate is positive.
All inputs are finite; a program needn't handle non-finite values.
Results may differ from a plain program's by a relative error of at most 0.015.
Values may be sent and summed in bfloat16 or wider, within the bound.
No kernel may reach another device: no remote copies, remote signals or barrier semaphores. Data moves between devices by JAX's collectives and lax.ppermute only.
A program may use at most 128 MiB of HBM per device.

v0:
```python
import jax
import jax.numpy as jnp
from jax import lax
from jax.sharding import PartitionSpec as P

HD = 128
BLOCK = 256


def entering(value, axis, combine, identity):
    count, position = (lax.axis_size(axis), lax.axis_index(axis))
    everything = jax.tree.map(
        lambda part, kind: lax.all_gather(part.astype(kind), axis),
        value,
        (jnp.bfloat16, jnp.bfloat16),
    )
    start = jax.tree.map(
        lambda part, zero: jnp.broadcast_to(jnp.asarray(zero, part.dtype), part.shape),
        value,
        identity,
    )

    def turn(k, before):
        reached = k < position
        new = combine(
            before, jax.tree.map(lambda part, own: part[k].astype(own.dtype), everything, value)
        )
        return jax.tree.map(lambda a, b: jnp.where(reached, a, b), new, before)

    return lax.fori_loop(0, count, turn, start)


def attend(q_head, k_head, v_head, rate, start_state):
    count = q_head.shape[0] // BLOCK
    place = jnp.arange(BLOCK).astype(jnp.float32)
    diff = place[:, None] - place[None, :]
    causal = jnp.where(diff >= 0, jnp.exp(-rate * jnp.maximum(diff, 0.0)), 0.0)
    in_decay = jnp.exp(-rate * (place + 1.0))
    out_decay = jnp.exp(-rate * (BLOCK - 1.0 - place))
    block_decay = jnp.exp(-rate * BLOCK)
    q_blocks = q_head.reshape(count, BLOCK, q_head.shape[1])
    k_blocks = k_head.reshape(count, BLOCK, k_head.shape[1])
    v_blocks = v_head.reshape(count, BLOCK, v_head.shape[1])

    def advance(state, block):
        q_blk, k_blk, v_blk = block
        scores = jnp.dot(q_blk, k_blk.T, preferred_element_type=jnp.float32)
        weighted = (scores * causal).astype(jnp.bfloat16)
        inner = jnp.dot(weighted, v_blk, preferred_element_type=jnp.float32)
        carried = (
            jnp.dot(q_blk.astype(jnp.float32), state, precision=lax.Precision.HIGHEST)
            * in_decay[:, None]
        )
        scaled = k_blk.astype(jnp.float32) * out_decay[:, None]
        update = jnp.dot(scaled.T, v_blk.astype(jnp.float32), precision=lax.Precision.HIGHEST)
        return (block_decay * state + update, inner + carried)

    final_state, outputs = lax.scan(advance, start_state, (q_blocks, k_blocks, v_blocks))
    return (outputs.reshape(q_head.shape[0], q_head.shape[1]), final_state)


def per_device(tokens, proj_weight, out_weight, head_gain, decay_rate):
    heads_here = decay_rate.shape[0]
    width = head_gain.shape[0]
    flat = proj_weight.reshape(proj_weight.shape[0], 4 * width)
    mixed = jnp.dot(
        lax.all_gather(tokens, "tp", axis=0, tiled=True), flat, preferred_element_type=jnp.float32
    )
    local_rows = mixed.shape[0]
    q_all = jax.nn.silu(mixed[:, :width]).astype(jnp.bfloat16).reshape(local_rows, heads_here, HD)
    k_all = (
        jax.nn.silu(mixed[:, width : 2 * width])
        .astype(jnp.bfloat16)
        .reshape(local_rows, heads_here, HD)
    )
    v_all = (
        jax.nn.silu(mixed[:, 2 * width : 3 * width])
        .astype(jnp.bfloat16)
        .reshape(local_rows, heads_here, HD)
    )
    gate = mixed[:, 3 * width :].reshape(local_rows, heads_here, HD)
    zero_state = jnp.zeros((HD, HD), jnp.float32)
    outputs, local_states = jax.vmap(attend, in_axes=(1, 1, 1, 0, None), out_axes=(1, 0))(
        q_all, k_all, v_all, decay_rate, zero_state
    )
    zero_states = jnp.zeros((heads_here, HD, HD), jnp.float32)
    span_decay = jnp.exp(-decay_rate * local_rows)

    def combine(earlier, later):
        return (later[1][:, None, None] * earlier[0] + later[0], earlier[1] * later[1])

    incoming, unused = entering(
        (local_states, span_decay), "seq", combine, (zero_states, jnp.ones_like(span_decay))
    )
    place = jnp.arange(local_rows).astype(jnp.float32)
    lift = jnp.exp(-decay_rate[None, :] * (place[:, None] + 1.0))
    extra = jnp.einsum(
        "thd,hde->the", q_all.astype(jnp.float32), incoming, precision=lax.Precision.HIGHEST
    )
    attn = outputs + extra * lift[:, :, None]
    square = jnp.mean(attn * attn, axis=-1, keepdims=True)
    normed = (
        attn
        * lax.rsqrt(square + 1e-06)
        * head_gain.reshape(heads_here, HD)[None]
        * jax.nn.sigmoid(gate)
    )
    joined = normed.astype(jnp.bfloat16).reshape(local_rows, width)
    return lax.psum_scatter(
        jnp.dot(joined, out_weight, preferred_element_type=jnp.float32).astype(jnp.bfloat16),
        "tp",
        scatter_dimension=0,
        tiled=True,
    )


def solution(mesh):
    return jax.shard_map(
        per_device,
        mesh=mesh,
        in_specs=(P(("seq", "tp"), None), P(None, None, "tp"), P("tp", None), P("tp"), P("tp")),
        out_specs=P(("seq", "tp"), None),
        check_vma=False,
    )
```

profile of v0, /device:TPU:9, one launch (start us, length us, event | category | flops | bytes accessed | tf_op | source)
XLA Modules:
  0.0 136.2 jit_solution(17524322370440477950)
XLA Ops:
  6.5 0.7 all-gather.4.cloned.1.call-update
  7.3 0.0 reduce-scatter.2.cloned.1.call-start
  7.3 1.2 dynamic-slice.6
  9.2 0.7 broadcast_multiply_fusion
  9.9 0.2 dynamic-update-slice
  10.1 7.2 %all-reduce = bf16[16]{0:T(256)(128)(2,1)S(1)} all-reduce(bf16[16]{0:T(256)(128)(2,1)S(1)} %dynamic-update-slice), channel_id=2, replica_groups=mesh['seq'=4,'tp'=8] {'seq'}, use_global_device_ids=true, to_apply=%add | all-reduce | flops 16 | bytes 64
  17.3 25.0 %copy.28 = bf16[768,8,4,512]{3,1,2,0:T(8,128)(2,1)} copy(bf16[768,8,4,512]{3,2,1,0:T(4,128)(2,1)} %bitcast.70) | data formatting | bytes 50331648
  42.4 0.1 reshape.191
  42.5 0.1 multiply_exponential_fusion
  42.5 0.1 multiply_exponential_fusion.1
  42.6 0.1 subtract_compare_fusion
  42.7 0.1 subtract_maximum_fusion
  42.9 0.3 all-gather.4.cloned.1.call-done
  43.2 12.5 %fusion.35 = f32[256,2048]{1,0:T(8,128)S(1)} fusion(bf16[256,6144]{1,0:T(8,128)(2,1)} %all-gather.4.cloned.1.call-done, bf16[6144,2048]{1,0:T(8,128)(2,1)} %bitcast.71), kind=kOutput, calls=%fused_computation.58 | convolution fusion | flops 6442450944 | bytes 30408704 | tf_op jit(solution)/shard_map/dot_general | solution.py:66
  55.7 0.6 fusion.21
  56.2 0.0 copy-start
  56.2 0.1 copy.22
  56.4 0.4 fusion.6
  56.8 12.5 %all-gather.1 = bf16[16,128,128]{2,1,0:T(8,128)(2,1)S(1)} all-gather(bf16[4,128,128]{2,1,0:T(8,128)(2,1)S(1)} %fusion.6), channel_id=3, replica_groups=mesh['seq'=4,'tp'=8] {'seq'}, dimensions={0}, use_global_device_ids=true | all-gather | bytes 655360 | tf_op jit(solution)/shard_map/all_gather | solution.py:13
  69.3 0.6 while.9
  69.3 0.1 fusion.43
  69.5 0.1 fusion.43
  69.6 0.1 fusion.43
  69.8 0.1 fusion.43
  69.9 0.4 fusion.5
  70.3 0.5 convolution_bitcast_fusion.2
  70.8 0.5 multiply_reduce_fusion
  71.3 0.2 copy.25
  71.5 0.1 multiply_convert_fusion
  71.7 6.3 %convolution_convert_fusion = bf16[256,6144]{1,0:T(8,128)(2,1)} fusion(bf16[256,512]{0,1:T(8,128)(2,1)S(1)} %bitcast.74, bf16[512,6144]{1,0:T(8,128)(2,1)} %param.9), kind=kOutput, calls=%fused_computation.3 | convolution fusion | flops 1612185600 | bytes 9699328 | tf_op jit(solution)/shard_map/dot_general | solution.py:110
  77.9 0.0 reduce-scatter.2.cloned.1.call-update
  78.0 51.4 %reduce-scatter.2.cloned.1.call-done = bf16[32,6144]{1,0:T(8,128)(2,1)} async-done(((bf16[256,6144]{1,0:T(8,128)(2,1)}), bf16[32,6144]{1,0:T(8,128)(2,1)}) %reduce-scatter.2.cloned.1.call-update) | async-done | bytes 393232 | tf_op jit(solution)/shard_map/reduce_scatter | solution.py:109
  (12 shorter events, 0.1 us)
Async XLA Ops:
  6.5 36.6 %all-gather.4.cloned.1.call-start = ((), (), s32[]{:S(2)}) async-start(), calls=%async_computation.1 | async-start | bytes 3538944 | tf_op jit(solution)/shard_map/all_gather | solution.py:67
  7.3 122.1 %reduce-scatter.2.cloned.1.call-start = ((), (), s32[]{:S(2)}) async-start(), calls=%async_computation.2 | async-start | bytes 3538944 | tf_op jit(solution)/shard_map/reduce_scatter | solution.py:109
  56.2 15.3 %copy-start = (f32[512]{0:T(512)S(1)}, f32[512]{0:T(512)}, u32[]{:S(2)}) copy-start(f32[512]{0:T(512)} %param.10) | copy-start | bytes 6148
Sparse Core Ops, SparseCore 0:
  9.2 33.8 all-gather.3
  78.1 51.2 reduce-scatter.1
where the time goes:
time: 138 us; the launch traced here: 136 us
  waiting for transfers between devices  52.5 us (38%)
  local copies, waits for them, and re-layouts  26.9 us (19%)
  matrix products  20.6 us (15%)
  blocking collectives  19.8 us (14%)
  between operations  14.2 us (10%)
  other arithmetic  2.2 us (2%)
    reduce_scatter x1, waiting for transfers between devices, per_device(): lax.psum_scatter(jnp.dot(joined, out_weight, preferred_element_type=jnp.f...  51.4 us
    unnamed x6, local copies, waits for them, and re-layouts  26.5 us
    all_gather x1, blocking collectives, entering(): lax.all_gather(part.astype(kind), axis)  12.5 us
    dot_general x1, matrix products, per_device(): jnp.dot(lax.all_gather(tokens, 'tp', axis=0, tiled=True), flat, preferred...  12.5 us
    unnamed x1, blocking collectives  7.24 us
    dot_general x1, matrix products, per_device(): jnp.dot(joined, out_weight, preferred_element_type=jnp.float32)  6.27 us
  transfers between devices with their start and end apart: 2, of which 2 were waited for; matrix products, arithmetic and copies ran while one was open for 20% of the time, Pallas kernels for 0%

commit v1 on v0

--- a/solution.py
+++ b/solution.py
@@ -1,10 +1,19 @@
+import functools
+
 import jax
 import jax.numpy as jnp
 from jax import lax
+from jax.experimental import pallas as pl
+from jax.experimental.pallas import tpu as pltpu
 from jax.sharding import PartitionSpec as P
 
 HD = 128
 BLOCK = 256
+F32, BF16 = jnp.float32, jnp.bfloat16
+VMEM = pl.BlockSpec(memory_space=pltpu.VMEM)
+SMEM = pl.BlockSpec(memory_space=pltpu.SMEM)
+HBM = pl.BlockSpec(memory_space=pl.ANY)
+MIB = 1 << 20
 
 
 def entering(value, axis, combine, identity):
@@ -59,7 +68,7 @@
     return (outputs.reshape(q_head.shape[0], q_head.shape[1]), final_state)
 
 
-def per_device(tokens, proj_weight, out_weight, head_gain, decay_rate):
+def general_device(tokens, proj_weight, out_weight, head_gain, decay_rate):
     heads_here = decay_rate.shape[0]
     width = head_gain.shape[0]
     flat = proj_weight.reshape(proj_weight.shape[0], 4 * width)
@@ -114,9 +123,378 @@
     )
 
 
+CORE = [(i, i ^ 1) for i in range(8)]
+FIRST = [(i, i ^ (4 if i & 1 else 2)) for i in range(8)]
+SECOND = [(i, i ^ (2 if i & 1 else 4)) for i in range(8)]
+
+
+def hop(value, pairs):
+    return lax.ppermute(value, "tp", pairs)
+
+
+STEP = 256
+
+
+def pinned(value):
+    return pltpu.with_memory_space_constraint(value, pltpu.VMEM)
+
+
+def in_hbm(value):
+    return pltpu.with_memory_space_constraint(value, pltpu.HBM)
+
+
+def chunks_kernel(first, w_hbm, buf, sem):
+    step = buf.shape[1]
+    copies = [
+        pltpu.make_async_copy(w_hbm.at[pl.ds(first + i * step, step)], buf.at[i], sem.at[i])
+        for i in range(buf.shape[0])
+    ]
+    for copy in copies:
+        copy.start()
+    return copies
+
+
+def turn(block, at, kv_ref, qg_ref):
+    width = block.shape[2]
+    turned = jnp.swapaxes(block, 0, 1)
+    kv_ref[at, :width] = turned[1]
+    kv_ref[at, width:] = turned[2]
+    qg_ref[at, :width] = turned[0]
+    qg_ref[at, width:] = turned[3]
+    return turned
+
+
+def slot_places(index, shape, axis):
+    row = lax.broadcasted_iota(jnp.int32, shape, axis)
+    part = shape[axis] // 8
+    core = index & 1
+    near = jnp.where(core == 0, 2, 4)
+    far = 6 - near
+    owners = (
+        index,
+        index ^ 1,
+        index ^ near,
+        index ^ 1 ^ far,
+        index ^ far,
+        index ^ 1 ^ near,
+        index ^ 6,
+        index ^ 7,
+    )
+    place = row
+    for slot, owner in enumerate(owners):
+        place = jnp.where(row // part == slot, row + (owner - slot) * part, place)
+    return place.astype(F32)
+
+
+def prep_kernel(w_hbm, kv_ref, qg_ref, down_ref, across_ref, buf, sem):
+    step = buf.shape[1]
+    copies = chunks_kernel(0, w_hbm, buf, sem)
+    index = lax.axis_index("tp")
+    down_ref[...] = slot_places(index, down_ref.shape, 0)
+    across_ref[...] = slot_places(index, across_ref.shape, 1)
+    for i, copy in enumerate(copies):
+        copy.wait()
+        turn(buf[i], slice(i * step, (i + 1) * step), kv_ref, qg_ref)
+
+
+def prep(proj_weight, rows):
+    depth, kinds, width = proj_weight.shape
+    depth //= 2
+    out = pltpu.VMEM((depth, 2 * width), BF16)
+    return pl.pallas_call(
+        prep_kernel,
+        in_specs=[HBM],
+        out_specs=[VMEM] * 4,
+        out_shape=[out, out, pltpu.VMEM((rows, 1), F32), pltpu.VMEM((1, rows), F32)],
+        scratch_shapes=[
+            pltpu.VMEM((depth // STEP, STEP, kinds, width), BF16),
+            pltpu.SemaphoreType.DMA((depth // STEP,)),
+        ],
+        compiler_params=pltpu.CompilerParams(vmem_limit_bytes=16 * MIB),
+        cost_estimate=pl.CostEstimate(
+            flops=0, bytes_accessed=2 * depth * kinds * width, transcendentals=0
+        ),
+        name="prep",
+    )(in_hbm(proj_weight))
+
+
+def gather_rows(x_refs, x_all):
+    at = 0
+    for ref in x_refs:
+        x_all[at : at + ref.shape[0], :] = ref[...]
+        at += ref.shape[0]
+
+
+def silu(mixed):
+    return (mixed / (1.0 + jnp.exp(-mixed))).astype(BF16)
+
+
+def near_kernel(n_rows, *refs):
+    x_refs = refs[:n_rows]
+    kv0, qg0, w_hbm, kv1, qg1, k_ref, v_ref, q_ref, g_ref, x_all, total, buf, sem = refs[n_rows:]
+    depth, step, width = kv0.shape[0], buf.shape[1], k_ref.shape[1]
+    copies = chunks_kernel(depth, w_hbm, buf, sem)
+    gather_rows(x_refs, x_all)
+    for i, (ref, half) in enumerate(((qg0, 0), (kv0, 0), (kv0, 1), (qg0, 1))):
+        total[i] = jnp.dot(
+            x_all[:, :depth],
+            ref[:, half * width : (half + 1) * width],
+            preferred_element_type=F32,
+        )
+    for c, copy in enumerate(copies):
+        copy.wait()
+        turned = turn(buf[c], slice(c * step, (c + 1) * step), kv1, qg1)
+        x = x_all[:, depth + c * step : depth + (c + 1) * step]
+        for i in range(4):
+            total[i] += jnp.dot(x, turned[i], preferred_element_type=F32)
+    q_ref[...] = silu(total[0])
+    k_ref[...] = silu(total[1])
+    v_ref[...] = silu(total[2])
+    g_ref[...] = 1.0 / (1.0 + jnp.exp(-total[3]))
+
+
+def project_near(rows, kv0, qg0, proj_weight):
+    count = sum(r.shape[0] for r in rows)
+    depth, kinds, width = proj_weight.shape
+    turned = pltpu.VMEM((depth // 2, 2 * width), BF16)
+    half, wide = pltpu.VMEM((count, width), BF16), pltpu.VMEM((count, width), F32)
+    chunks = depth // 2 // STEP
+    return pl.pallas_call(
+        functools.partial(near_kernel, len(rows)),
+        in_specs=[VMEM] * (len(rows) + 2) + [HBM],
+        out_specs=[VMEM] * 6,
+        out_shape=[turned, turned, half, half, half, wide],
+        scratch_shapes=[
+            pltpu.VMEM((count, depth), BF16),
+            pltpu.VMEM((kinds, count, width), F32),
+            pltpu.VMEM((chunks, STEP, kinds, width), BF16),
+            pltpu.SemaphoreType.DMA((chunks,)),
+        ],
+        compiler_params=pltpu.CompilerParams(vmem_limit_bytes=24 * MIB),
+        cost_estimate=pl.CostEstimate(
+            flops=2 * count * depth * kinds * width,
+            bytes_accessed=depth * kinds * width,
+            transcendentals=0,
+        ),
+        name="project_near",
+    )(*rows, pinned(kv0), pinned(qg0), in_hbm(proj_weight))
+
+
+def far_kernel(n_rows, gate, *refs):
+    x_refs = refs[:n_rows]
+    w0, w1, a_ref, b_ref, x_all = refs[n_rows:]
+    depth, width = w0.shape[0], a_ref.shape[1]
+    gather_rows(x_refs, x_all)
+    for half, out in enumerate((a_ref, b_ref)):
+        cols = slice(half * width, (half + 1) * width)
+        mixed = jnp.dot(x_all[:, :depth], w0[:, cols], preferred_element_type=F32) + jnp.dot(
+            x_all[:, depth:], w1[:, cols], preferred_element_type=F32
+        )
+        out[...] = 1.0 / (1.0 + jnp.exp(-mixed)) if gate and half else silu(mixed)
+
+
+def project_far(rows, w0, w1, gate, name):
+    count = sum(r.shape[0] for r in rows)
+    depth, width = rows[0].shape[1], w0.shape[1] // 2
+    return pl.pallas_call(
+        functools.partial(far_kernel, len(rows), gate),
+        in_specs=[VMEM] * (len(rows) + 2),
+        out_specs=[VMEM] * 2,
+        out_shape=[
+            pltpu.VMEM((count, width), BF16),
+            pltpu.VMEM((count, width), F32 if gate else BF16),
+        ],
+        scratch_shapes=[pltpu.VMEM((count, depth), BF16)],
+        compiler_params=pltpu.CompilerParams(vmem_limit_bytes=12 * MIB),
+        cost_estimate=pl.CostEstimate(
+            flops=4 * count * depth * width, bytes_accessed=4 * depth * width, transcendentals=0
+        ),
+        name=name,
+    )(*rows, pinned(w0), pinned(w1))
+
+
+def state_kernel(rate_ref, place_ref, k0, k1, v0, v1, s_ref):
+    for h in range(s_ref.shape[0]):
+        cols = slice(h * HD, (h + 1) * HD)
+        fade = jnp.exp(-rate_ref[h] * (BLOCK - 1.0 - place_ref[...]))
+        k = jnp.concatenate([k0[:, cols], k1[:, cols]], 0).astype(F32) * fade
+        v = jnp.concatenate([v0[:, cols], v1[:, cols]], 0)
+        s_ref[h] = lax.dot_general(
+            k.astype(BF16), v, (((0,), (0,)), ((), ())), preferred_element_type=F32
+        ).astype(BF16)
+
+
+def middle_kernel(n_rows, rate_ref, place_ref, across_ref, *refs):
+    x_refs = refs[:n_rows]
+    (w0, w1, q0, k0, k1, v0, v1, w_hbm, u_hbm) = refs[n_rows : n_rows + 9]
+    (q1, g1, o_ref, w_ref, u_ref, x_all, sem) = refs[n_rows + 9 :]
+    copies = [
+        pltpu.make_async_copy(w_hbm, w_ref, sem.at[0]),
+        pltpu.make_async_copy(u_hbm, u_ref, sem.at[1]),
+    ]
+    for copy in copies:
+        copy.start()
+    far_kernel(n_rows, True, *x_refs, w0, w1, q1, g1, x_all)
+    diff = place_ref[...] - across_ref[...]
+    seen = diff >= 0
+    diff = jnp.maximum(diff, 0.0)
+    for h in range(o_ref.shape[1] // HD):
+        cols = slice(h * HD, (h + 1) * HD)
+        q = jnp.concatenate([q0[:, cols], q1[:, cols]], 0)
+        k = jnp.concatenate([k0[:, cols], k1[:, cols]], 0)
+        v = jnp.concatenate([v0[:, cols], v1[:, cols]], 0)
+        scores = lax.dot_general(q, k, (((1,), (1,)), ((), ())), preferred_element_type=F32)
+        causal = jnp.where(seen, jnp.exp(-rate_ref[h] * diff), 0.0)
+        o_ref[:, cols] = jnp.dot(
+            (scores * causal).astype(BF16), v, preferred_element_type=F32
+        )
+    for copy in copies:
+        copy.wait()
+
+
+def middle(rate, down, across, rows, w0, w1, q0, k0, k1, v0, v1, w, u):
+    count = sum(r.shape[0] for r in rows)
+    depth, width = rows[0].shape[1], w0.shape[1] // 2
+    weight = pltpu.VMEM(w.shape, w.dtype)
+    return pl.pallas_call(
+        functools.partial(middle_kernel, len(rows)),
+        in_specs=[SMEM] + [VMEM] * (len(rows) + 9) + [HBM] * 2,
+        out_specs=[VMEM] * 5,
+        out_shape=[
+            pltpu.VMEM((count, width), BF16),
+            pltpu.VMEM((count, width), F32),
+            pltpu.VMEM((down.shape[0], width), F32),
+            weight,
+            weight,
+        ],
+        scratch_shapes=[pltpu.VMEM((count, depth), BF16), pltpu.SemaphoreType.DMA((2,))],
+        compiler_params=pltpu.CompilerParams(vmem_limit_bytes=12 * MIB),
+        cost_estimate=pl.CostEstimate(
+            flops=4 * count * depth * width, bytes_accessed=8 * depth * width, transcendentals=0
+        ),
+        name="middle",
+    )(rate, down, across, *rows, pinned(w0), pinned(w1), q0, k0, k1, v0, v1, in_hbm(w), in_hbm(u))
+
+
+TO_SUM = (3, 7, 1, 5, 2, 6, 0, 4)
+
+
+def finish_kernel(rate_ref, place_ref, gain_ref, in_ref, q0, q1, g0, g1, s1, s2, s3, y_ref, z_ref):
+    part = in_ref.shape[0] // 8
+    for h in range(in_ref.shape[1] // HD):
+        cols = slice(h * HD, (h + 1) * HD)
+        rate = rate_ref[h]
+        span = jnp.exp(jnp.full((HD, HD), -rate * BLOCK, F32))
+        state = s1[h].astype(F32) + span * (s2[h].astype(F32) + span * s3[h].astype(F32))
+        high = state.astype(BF16)
+        low = (state - high.astype(F32)).astype(BF16)
+        q = jnp.concatenate([q0[:, cols], q1[:, cols]], 0)
+        extra = jnp.dot(q, high, preferred_element_type=F32) + jnp.dot(
+            q, low, preferred_element_type=F32
+        )
+        attn = in_ref[:, cols] + extra * jnp.exp(-rate * (place_ref[...] + 1.0))
+        square = jnp.mean(attn * attn, axis=-1, keepdims=True)
+        gate = jnp.concatenate([g0[:, cols], g1[:, cols]], 0)
+        y = (attn * lax.rsqrt(square + 1e-06) * gain_ref[:, cols] * gate).astype(BF16)
+        for slot, to in enumerate(TO_SUM):
+            to_ref, at = (y_ref, to) if to < 4 else (z_ref, to - 4)
+            to_ref[at * part : (at + 1) * part, cols] = y[slot * part : (slot + 1) * part]
+
+
+def small(kernel, n_smem, out, name, *args):
+    return pl.pallas_call(
+        kernel,
+        in_specs=[SMEM] * n_smem + [VMEM] * (len(args) - n_smem),
+        out_specs=jax.tree.map(lambda _: VMEM, out),
+        out_shape=out,
+        compiler_params=pltpu.CompilerParams(vmem_limit_bytes=12 * MIB),
+        name=name,
+    )(*args)
+
+
+def out_kernel(y_ref, z_ref, w_ref, u_ref, a_ref, b_ref, c_ref, d_ref):
+    rows, width = a_ref.shape
+    step = 1024
+    for at in range(0, width, step):
+        cols = slice(at, at + step)
+        total = jnp.dot(y_ref[...], w_ref[:, cols], preferred_element_type=F32) + jnp.dot(
+            z_ref[...], u_ref[:, cols], preferred_element_type=F32
+        )
+        for i, ref in enumerate((a_ref, b_ref, c_ref, d_ref)):
+            ref[:, cols] = total[i * rows : (i + 1) * rows].astype(ref.dtype)
+
+
+def out_rows(y, z, w, u):
+    rows, depth = y.shape
+    width = w.shape[1]
+    send = jax.ShapeDtypeStruct((rows // 4, width), BF16)
+    keep = jax.ShapeDtypeStruct((rows // 4, width), F32)
+    return pl.pallas_call(
+        out_kernel,
+        in_specs=[VMEM] * 4,
+        out_specs=[VMEM] * 4,
+        out_shape=[send, keep, send, keep],
+        compiler_params=pltpu.CompilerParams(vmem_limit_bytes=16 * MIB),
+        cost_estimate=pl.CostEstimate(
+            flops=4 * rows * depth * width, bytes_accessed=4 * depth * width, transcendentals=0
+        ),
+        name="out_rows",
+    )(y, z, pinned(w), pinned(u))
+
+
+def paired_device(tokens, proj_weight, out_weight, head_gain, decay_rate):
+    rows = tokens.shape[0]
+    heads = decay_rate.shape[0]
+    count = lax.axis_size("seq")
+
+    beside = hop(tokens, CORE)
+    first = hop(tokens, FIRST)
+    second = hop(tokens, SECOND)
+    kv0, qg0, down, across = prep(proj_weight, 8 * rows)
+    far = hop(first, SECOND)
+    first_beside = hop(first, CORE)
+    kv1, qg1, k0, v0, q0, g0 = project_near(
+        [tokens, beside, first, first_beside], kv0, qg0, proj_weight
+    )
+    second_beside = hop(second, CORE)
+    far_beside = hop(far, CORE)
+    w_other = hop(out_weight, CORE)
+    late = [second, second_beside, far, far_beside]
+    k1, v1 = project_far(late, kv0, kv1, False, "project_far_kv")
+
+    states = small(
+        state_kernel,
+        1,
+        jax.ShapeDtypeStruct((heads, HD, HD), BF16),
+        "state",
+        decay_rate, down, k0, k1, v0, v1,
+    )
+    came = [
+        lax.ppermute(states, "seq", [(i, i + k) for i in range(count - k)]) for k in range(1, count)
+    ]
+    q1, g1, inner, w_own, w_other = middle(
+        decay_rate, down, across, late, qg0, qg1, q0, k0, k1, v0, v1, out_weight, w_other
+    )
+    split = jax.ShapeDtypeStruct((4 * rows, heads * HD), BF16)
+    y, y_other = small(
+        finish_kernel,
+        1,
+        [split, split],
+        "finish",
+        decay_rate, down, head_gain[None, :], inner, q0, q1, g0, g1, *came,
+    )
+    z = hop(y_other, CORE)
+    a, b, c, d = out_rows(y, z, w_own, w_other)
+    got_a = hop(a, SECOND)
+    got_c = hop(c, SECOND)
+    got_b = hop((b + got_a.astype(F32)).astype(BF16), FIRST)
+    return (d + got_c.astype(F32) + got_b.astype(F32)).astype(BF16)
+
+
 def solution(mesh):
+    paired = mesh.shape["tp"] == 8 and mesh.shape["seq"] == 4
     return jax.shard_map(
-        per_device,
+        paired_device if paired else general_device,
         mesh=mesh,
         in_specs=(P(("seq", "tp"), None), P(None, None, "tp"), P("tp", None), P("tp"), P("tp")),
         out_specs=P(("seq", "tp"), None),

time: 138 us -> 79.4 us (0.58)
  the two profiles are of different devices: /device:TPU:9 before, /device:TPU:0 now
where the time goes in v1:
time: 79.4 us; the launch traced here: 79.2 us
  waiting for transfers between devices  26.3 us (33%)
  Pallas kernels  24.6 us (31%)
  starting transfers between devices  21.1 us (27%)
  local copies, waits for them, and re-layouts  6.06 us (8%)
  other arithmetic  0.96 us (1%)
    ppermute x12, waiting for transfers between devices, hop(): return lax.ppermute(value, 'tp', pairs)  26.3 us
    ppermute x12, starting transfers between devices, hop(): return lax.ppermute(value, 'tp', pairs)  11.3 us
    ppermute x3, starting transfers between devices, paired_device(): lax.ppermute(states, 'seq', [(i, i + k) for i in range(count - k)])  9.81 us
    pallas_call x1, Pallas kernels, middle(): pl.pallas_call(functools.partial(middle_kernel, len(rows)), in_specs=[SME...  7.13 us
    pallas_call x1, Pallas kernels, project_near(): pl.pallas_call(functools.partial(near_kernel, len(rows)), in_specs=[VMEM]...  6.56 us
    unnamed x12, local copies, waits for them, and re-layouts  6.06 us
    pallas_call x1, Pallas kernels, prep(): pl.pallas_call(prep_kernel, in_specs=[HBM], out_specs=[VMEM] * 4, out_sha...  4.93 us
    pallas_call x2, Pallas kernels, small(): pl.pallas_call(kernel, in_specs=[SMEM] * n_smem + [VMEM] * (len(args) - n...  2.14 us
  transfers between devices with their start and end apart: 15, of which 6 were waited for; matrix products, arithmetic and copies ran while one was open for 0% of the time, Pallas kernels for 27%

profile of v1, /device:TPU:0, one launch (start us, length us, event | category | flops | bytes accessed | tf_op | source)
XLA Modules:
  0.0 79.2 jit_solution(14618105339390782461)
XLA Ops:
  0.0 0.5 collective-permute-start.7
  0.5 2.5 %collective-permute-start.2 = (bf16[32,6144]{1,0:T(8,128)(2,1)}, bf16[32,6144]{1,0:T(8,128)(2,1)S(1)}, u32[]{:S(2)}, u32[]{:S(2)}) collective-permute-start(bf16[32,6144]{1,0:T(8,128)(2,1)} %refs_0_.1), channel_id=1, source_target_pairs={{0,2},{1,5},{2,0},{3,7},{4,6},{5,1},{6,4},{7,3},{8,10},{9,13},{10,... | collective-permute-start | bytes 1179656 | tf_op jit(solution)/shard_map/ppermute | solution.py:132
  3.0 1.5 %collective-permute-start = (bf16[32,6144]{1,0:T(8,128)(2,1)}, bf16[32,6144]{1,0:T(8,128)(2,1)S(1)}, u32[]{:S(2)}, u32[]{:S(2)}) collective-permute-start(bf16[32,6144]{1,0:T(8,128)(2,1)} %refs_0_.1), channel_id=1, source_target_pairs={{0,4},{1,3},{2,6},{3,1},{4,0},{5,7},{6,2},{7,5},{8,12},{9,11},{10,... | collective-permute-start | bytes 1179656 | tf_op jit(solution)/shard_map/ppermute | solution.py:132
  4.5 7.6 %collective-permute-done.2.refs_2_ = bf16[32,6144]{1,0:T(8,128)(2,1)S(1)} collective-permute-done((bf16[32,6144]{1,0:T(8,128)(2,1)}, bf16[32,6144]{1,0:T(8,128)(2,1)S(1)}, u32[]{:S(2)}, u32[]{:S(2)}) %collective-permute-start.2) | collective-permute-done | bytes 393248 | tf_op jit(solution)/shard_map/ppermute | solution.py:132
  12.2 2.6 %collective-permute-start.3 = (bf16[32,6144]{1,0:T(8,128)(2,1)S(1)}, bf16[32,6144]{1,0:T(8,128)(2,1)S(1)}, u32[]{:S(2)}, u32[]{:S(2)}) collective-permute-start(bf16[32,6144]{1,0:T(8,128)(2,1)S(1)} %collective-permute-done.2.refs_2_), channel_id=1, source_target_pairs={{0,4},{1,3},{2,6},{3,1},{4,0},{5,7},{6,2},{7,5},{8,12},{9,11},{10,... | collective-permute-start | bytes 1179656 | tf_op jit(solution)/shard_map/ppermute | solution.py:132
  14.7 0.5 collective-permute-start.6
  15.2 0.0 collective-permute-start.1
  15.2 5.2 %collective-permute-done.3.refs_2_ = bf16[32,6144]{1,0:T(8,128)(2,1)S(1)} collective-permute-done((bf16[32,6144]{1,0:T(8,128)(2,1)S(1)}, bf16[32,6144]{1,0:T(8,128)(2,1)S(1)}, u32[]{:S(2)}, u32[]{:S(2)}) %collective-permute-start.3) | collective-permute-done | bytes 393248 | tf_op jit(solution)/shard_map/ppermute | solution.py:132
  20.5 4.9 %prep.1 = (bf16[3072,1024]{1,0:T(8,128)(2,1)S(1)}, bf16[3072,1024]{1,0:T(8,128)(2,1)S(1)}, f32[256,1]{1,0:T(8,128)S(1)}, f32[1,256]{1,0:T(1,128)S(1)}) custom-call(bf16[6144,4,512]{2,1,0:T(4,128)(2,1)} %refs_6_.1), custom_call_target="tpu_custom_call" | custom-call | bytes 12582912 | tf_op jit(solution)/shard_map/prep/pallas_call | solution.py:204
  25.4 6.6 %project_near.1 = (bf16[3072,1024]{1,0:T(8,128)(2,1)S(1)}, bf16[3072,1024]{1,0:T(8,128)(2,1)S(1)}, bf16[128,512]{1,0:T(8,128)(2,1)S(1)}, bf16[128,512]{1,0:T(8,1...) custom-call(bf16[32,6144]{1,0:T(8,128)(2,1)S(1)} %copy-done.2, ...), custom_call_target="tpu_custom_call" | custom-call | flops 3221225472 | bytes 12582912 | tf_op jit(solution)/shard_map/project_near/pallas_call | solution.py:262
  32.0 0.0 copy-start.3
  32.1 1.9 %project_far_kv.1 = (bf16[128,512]{1,0:T(8,128)(2,1)S(1)}, bf16[128,512]{1,0:T(8,128)(2,1)S(1)}) custom-call(bf16[32,6144]{1,0:T(8,128)(2,1)S(1)} %collective-permute-done.refs_0_, bf16[32,6144]{1,0:T(8,128)(2,1)S(1)} %collective-permute-done.1.refs_1_, bf16[32,6144]{1,0:T(8,128)(2,1)S(1)} %collective-permute-done.3.refs_2_, ...), custom_call_target="tpu_custom_call" | custom-call | flops 1610612736 | bytes 12582912 | tf_op jit(solution)/shard_map/project_far_kv/pallas_call | solution.py:299
  34.0 0.7 copy-done
  34.7 1.0 %state.1 = bf16[4,128,128]{2,1,0:T(8,128)(2,1)S(1)} custom-call(f32[4]{0:T(128)S(1)} %copy-done.3, f32[256,1]{1,0:T(8,128)S(1)} %get-tuple-element.28.place_ref, bf16[128,512]{1,0:T(8,128)(2,1)S(1)} %get-tuple-element.34.refs_7_.k0, bf16[128,512]{1,0:T(8,128)(2,1)S(1)} %get-tuple-element.36.refs_8_.k1, bf16[128,512]{1,0:T(8,128)(2,1)S(1)} %get-tuple-element.37.refs_9_.v0, ...), custom_call_target="tpu_custom_call" | custom-call | tf_op jit(solution)/shard_map/state/pallas_call | solution.py:405
  35.7 5.9 %collective-permute-start.10 = (bf16[4,128,128]{2,1,0:T(8,128)(2,1)S(1)}, bf16[4,128,128]{2,1,0:T(8,128)(2,1)S(1)}, u32[]{:S(2)}, u32[]{:S(2)}) collective-permute-start(bf16[4,128,128]{2,1,0:T(8,128)(2,1)S(1)} %state.1), channel_id=1, source_target_pairs={{0,24},{1,25},{2,26},{3,27},{4,28},{5,29},{6,30},{7,31}} | collective-permute-start | bytes 393224 | tf_op jit(solution)/shard_map/ppermute | solution.py:473
  41.5 1.3 %collective-permute-start.9 = (bf16[4,128,128]{2,1,0:T(8,128)(2,1)S(1)}, bf16[4,128,128]{2,1,0:T(8,128)(2,1)S(1)}, u32[]{:S(2)}, u32[]{:S(2)}) collective-permute-start(bf16[4,128,128]{2,1,0:T(8,128)(2,1)S(1)} %state.1), channel_id=1, source_target_pairs={{0,16},{8,24},{1,17},{9,25},{2,18},{10,26},{3,19},{11,27},{4,20},{... | collective-permute-start | bytes 393224 | tf_op jit(solution)/shard_map/ppermute | solution.py:473
  42.9 2.6 %collective-permute-start.8 = (bf16[4,128,128]{2,1,0:T(8,128)(2,1)S(1)}, bf16[4,128,128]{2,1,0:T(8,128)(2,1)S(1)}, u32[]{:S(2)}, u32[]{:S(2)}) collective-permute-start(bf16[4,128,128]{2,1,0:T(8,128)(2,1)S(1)} %state.1), channel_id=1, source_target_pairs={{0,8},{8,16},{16,24},{1,9},{9,17},{17,25},{2,10},{10,18},{18,26},{... | collective-permute-start | bytes 393224 | tf_op jit(solution)/shard_map/ppermute | solution.py:473
  45.5 2.6 %copy-done.5 = bf16[512,6144]{1,0:T(8,128)(2,1)} copy-done((bf16[512,6144]{1,0:T(8,128)(2,1)}, bf16[512,6144]{1,0:T(8,128)(2,1)S(1)}, u32[]{:S(2)}) %copy-start.5) | copy-done | bytes 6291480
  48.1 2.8 %copy-done.1 = bf16[3072,1024]{1,0:T(8,128)(2,1)S(1)} copy-done((bf16[3072,1024]{1,0:T(8,128)(2,1)S(1)}, bf16[3072,1024]{1,0:T(8,128)(2,1)}, u32[]{:S(2)}) %copy-start.1) | copy-done | bytes 6291480
  50.9 7.1 %middle.1 = (bf16[128,512]{1,0:T(8,128)(2,1)S(1)}, f32[128,512]{1,0:T(8,128)S(1)}, f32[256,512]{1,0:T(8,128)S(1)}, bf16[512,6144]{1,0:T(8,128)(2,1)S(1)}, bf16[512,6144]{1,0:T(8,128)(2,1)S(1)}) custom-call(f32[4]{0:T(128)S(1)} %copy-done.3, f32[256,1]{1,0:T(8,128)S(1)} %get-tuple-element.28.place_ref, f32[1,256]{1,0:T(1,128)S(1)} %get-tuple-element.29.across_ref, ...), custom_call_target="tpu_custom_call" | custom-call | flops 1610612736 | bytes 25165824 | tf_op jit(solution)/shard_map/middle/pallas_call | solution.py:359
  58.1 1.1 %finish.1 = (bf16[128,512]{1,0:T(8,128)(2,1)S(1)}, bf16[128,512]{1,0:T(8,128)(2,1)S(1)}) custom-call(f32[4]{0:T(128)S(1)} %copy-done.3, f32[256,1]{1,0:T(8,128)S(1)} %get-tuple-element.28.place_ref, f32[1,512]{1,0:T(1,128)S(1)} %bitcast.1, f32[256,512]{1,0:T(8,128)S(1)} %get-tuple-element.39.in_ref, bf16[128,512]{1,0:T(8,128)(2,1)S(1)} %get-tuple-element.33.refs_6_.q0, ...), custom_call_target="tpu_custom_call" | custom-call | tf_op jit(solution)/shard_map/finish/pallas_call | solution.py:405
  59.2 0.1 collective-permute-start.11
  59.3 1.3 %collective-permute-done.11.z_ref = bf16[128,512]{1,0:T(8,128)(2,1)S(1)} collective-permute-done((bf16[128,512]{1,0:T(8,128)(2,1)S(1)}, bf16[128,512]{1,0:T(8,128)(2,1)S(1)}, u32[]{:S(2)}, u32[]{:S(2)}) %collective-permute-start.11) | collective-permute-done | bytes 131104 | tf_op jit(solution)/shard_map/ppermute | solution.py:132
  60.7 1.9 %out_rows.1 = (bf16[32,6144]{1,0:T(8,128)(2,1)S(1)}, f32[32,6144]{1,0:T(8,128)S(1)}, bf16[32,6144]{1,0:T(8,128)(2,1)S(1)}, f32[32,6144]{1,0:T(8,128)S(1)}) custom-call(bf16[128,512]{1,0:T(8,128)(2,1)S(1)} %get-tuple-element.43.y_ref, bf16[128,512]{1,0:T(8,128)(2,1)S(1)} %collective-permute-done.11.z_ref, bf16[512,6144]{1,0:T(8,128)(2,1)S(1)} %get-tuple-element.45.w_ref, ...), custom_call_target="tpu_custom_call" | custom-call | flops 1610612736 | bytes 12582912 | tf_op jit(solution)/shard_map/out_rows/pallas_call | solution.py:432
  62.6 2.0 %collective-permute-start.13 = (bf16[32,6144]{1,0:T(8,128)(2,1)S(1)}, bf16[32,6144]{1,0:T(8,128)(2,1)S(1)}, u32[]{:S(2)}, u32[]{:S(2)}) collective-permute-start(bf16[32,6144]{1,0:T(8,128)(2,1)S(1)} %get-tuple-element.50), channel_id=1, source_target_pairs={{0,4},{1,3},{2,6},{3,1},{4,0},{5,7},{6,2},{7,5},{8,12},{9,11},{10,... | collective-permute-start | bytes 1179656 | tf_op jit(solution)/shard_map/ppermute | solution.py:132
  64.6 0.1 collective-permute-start.12
  64.7 5.8 %collective-permute-done.13 = bf16[32,6144]{1,0:T(8,128)(2,1)S(1)} collective-permute-done((bf16[32,6144]{1,0:T(8,128)(2,1)S(1)}, bf16[32,6144]{1,0:T(8,128)(2,1)S(1)}, u32[]{:S(2)}, u32[]{:S(2)}) %collective-permute-start.13) | collective-permute-done | bytes 393248 | tf_op jit(solution)/shard_map/ppermute | solution.py:132
  70.4 0.1 add_convert_fusion.1
  70.5 1.6 %collective-permute-start.14 = (bf16[32,6144]{1,0:T(8,128)(2,1)S(1)}, bf16[32,6144]{1,0:T(8,128)(2,1)S(1)}, u32[]{:S(2)}, u32[]{:S(2)}) collective-permute-start(bf16[32,6144]{1,0:T(8,128)(2,1)S(1)} %add_convert_fusion.1), channel_id=1, source_target_pairs={{0,2},{1,5},{2,0},{3,7},{4,6},{5,1},{6,4},{7,3},{8,10},{9,13},{10,... | collective-permute-start | bytes 1179656 | tf_op jit(solution)/shard_map/ppermute | solution.py:132
  72.1 4.5 %collective-permute-done.12 = bf16[32,6144]{1,0:T(8,128)(2,1)S(1)} collective-permute-done((bf16[32,6144]{1,0:T(8,128)(2,1)S(1)}, bf16[32,6144]{1,0:T(8,128)(2,1)S(1)}, u32[]{:S(2)}, u32[]{:S(2)}) %collective-permute-start.12) | collective-permute-done | bytes 393248 | tf_op jit(solution)/shard_map/ppermute | solution.py:132
  76.6 1.8 %collective-permute-done.14 = bf16[32,6144]{1,0:T(8,128)(2,1)S(1)} collective-permute-done((bf16[32,6144]{1,0:T(8,128)(2,1)S(1)}, bf16[32,6144]{1,0:T(8,128)(2,1)S(1)}, u32[]{:S(2)}, u32[]{:S(2)}) %collective-permute-start.14) | collective-permute-done | bytes 393248 | tf_op jit(solution)/shard_map/ppermute | solution.py:132
  78.4 0.9 %add_convert_fusion = bf16[32,6144]{1,0:T(8,128)(2,1)} fusion(bf16[32,6144]{1,0:T(8,128)(2,1)S(1)} %collective-permute-done.14, f32[32,6144]{1,0:T(8,128)S(1)} %get-tuple-element.47, bf16[32,6144]{1,0:T(8,128)(2,1)S(1)} %collective-permute-done.12), kind=kLoop, calls=%fused_computation | loop fusion | flops 983040 | bytes 1966080 | tf_op jit(solution)/shard_map/convert_element_type | solution.py:491
  (19 shorter events, 0.0 us)
Async XLA Ops:
  0.0 25.4 %copy-start.2 = (bf16[32,6144]{1,0:T(8,128)(2,1)S(1)}, bf16[32,6144]{1,0:T(8,128)(2,1)}, u32[]{:S(2)}) copy-start(bf16[32,6144]{1,0:T(8,128)(2,1)} %refs_0_.1) | copy-start | bytes 1179652
  0.0 45.5 %collective-permute-start.7 = (bf16[512,6144]{1,0:T(8,128)(2,1)}, bf16[512,6144]{1,0:T(8,128)(2,1)S(1)}, u32[]{:S(2)}, u32[]{:S(2)}) collective-permute-start(bf16[512,6144]{1,0:T(8,128)(2,1)} %refs_11_.1), channel_id=1, source_target_pairs={{0,1},{1,0},{2,3},{3,2},{4,5},{5,4},{6,7},{7,6},{8,9},{9,8},{10,11... | collective-permute-start | bytes 18874376 | tf_op jit(solution)/shard_map/ppermute | solution.py:132
  0.5 11.7 %collective-permute-start.2 = (bf16[32,6144]{1,0:T(8,128)(2,1)}, bf16[32,6144]{1,0:T(8,128)(2,1)S(1)}, u32[]{:S(2)}, u32[]{:S(2)}) collective-permute-start(bf16[32,6144]{1,0:T(8,128)(2,1)} %refs_0_.1), channel_id=1, source_target_pairs={{0,2},{1,5},{2,0},{3,7},{4,6},{5,1},{6,4},{7,3},{8,10},{9,13},{10,... | collective-permute-start | bytes 1179656 | tf_op jit(solution)/shard_map/ppermute | solution.py:132
  3.0 12.2 %collective-permute-start = (bf16[32,6144]{1,0:T(8,128)(2,1)}, bf16[32,6144]{1,0:T(8,128)(2,1)S(1)}, u32[]{:S(2)}, u32[]{:S(2)}) collective-permute-start(bf16[32,6144]{1,0:T(8,128)(2,1)} %refs_0_.1), channel_id=1, source_target_pairs={{0,4},{1,3},{2,6},{3,1},{4,0},{5,7},{6,2},{7,5},{8,12},{9,11},{10,... | collective-permute-start | bytes 1179656 | tf_op jit(solution)/shard_map/ppermute | solution.py:132
  12.2 8.3 %collective-permute-start.3 = (bf16[32,6144]{1,0:T(8,128)(2,1)S(1)}, bf16[32,6144]{1,0:T(8,128)(2,1)S(1)}, u32[]{:S(2)}, u32[]{:S(2)}) collective-permute-start(bf16[32,6144]{1,0:T(8,128)(2,1)S(1)} %collective-permute-done.2.refs_2_), channel_id=1, source_target_pairs={{0,4},{1,3},{2,6},{3,1},{4,0},{5,7},{6,2},{7,5},{8,12},{9,11},{10,... | collective-permute-start | bytes 1179656 | tf_op jit(solution)/shard_map/ppermute | solution.py:132
  14.7 10.7 %collective-permute-start.5 = (bf16[32,6144]{1,0:T(8,128)(2,1)}, bf16[32,6144]{1,0:T(8,128)(2,1)S(1)}, u32[]{:S(2)}, u32[]{:S(2)}) collective-permute-start(bf16[32,6144]{1,0:T(8,128)(2,1)} %refs_0_.1), channel_id=1, source_target_pairs={{0,1},{1,0},{2,3},{3,2},{4,5},{5,4},{6,7},{7,6},{8,9},{9,8},{10,11... | collective-permute-start | bytes 1179656 | tf_op jit(solution)/shard_map/ppermute | solution.py:132
  14.7 10.7 %collective-permute-start.6 = (bf16[32,6144]{1,0:T(8,128)(2,1)S(1)}, bf16[32,6144]{1,0:T(8,128)(2,1)S(1)}, u32[]{:S(2)}, u32[]{:S(2)}) collective-permute-start(bf16[32,6144]{1,0:T(8,128)(2,1)S(1)} %collective-permute-done.2.refs_2_), channel_id=1, source_target_pairs={{0,1},{1,0},{2,3},{3,2},{4,5},{5,4},{6,7},{7,6},{8,9},{9,8},{10,11... | collective-permute-start | bytes 1179656 | tf_op jit(solution)/shard_map/ppermute | solution.py:132
  15.2 16.8 %collective-permute-start.1 = (bf16[32,6144]{1,0:T(8,128)(2,1)S(1)}, bf16[32,6144]{1,0:T(8,128)(2,1)S(1)}, u32[]{:S(2)}, u32[]{:S(2)}) collective-permute-start(bf16[32,6144]{1,0:T(8,128)(2,1)S(1)} %collective-permute-done.refs_0_), channel_id=1, source_target_pairs={{0,1},{1,0},{2,3},{3,2},{4,5},{5,4},{6,7},{7,6},{8,9},{9,8},{10,11... | collective-permute-start | bytes 1179656 | tf_op jit(solution)/shard_map/ppermute | solution.py:132
  20.5 11.6 %collective-permute-start.4 = (bf16[32,6144]{1,0:T(8,128)(2,1)S(1)}, bf16[32,6144]{1,0:T(8,128)(2,1)S(1)}, u32[]{:S(2)}, u32[]{:S(2)}) collective-permute-start(bf16[32,6144]{1,0:T(8,128)(2,1)S(1)} %collective-permute-done.3.refs_2_), channel_id=1, source_target_pairs={{0,1},{1,0},{2,3},{3,2},{4,5},{5,4},{6,7},{7,6},{8,9},{9,8},{10,11... | collective-permute-start | bytes 1179656 | tf_op jit(solution)/shard_map/ppermute | solution.py:132
  32.0 2.7 %copy-start = (bf16[3072,1024]{1,0:T(8,128)(2,1)}, bf16[3072,1024]{1,0:T(8,128)(2,1)S(1)}, u32[]{:S(2)}) copy-start(bf16[3072,1024]{1,0:T(8,128)(2,1)S(1)} %get-tuple-element.32.refs_5_) | copy-start | bytes 18874372
  32.0 2.6 %copy-start.3 = (f32[4]{0:T(128)S(1)}, f32[4]{0:T(128)}, u32[]{:S(2)}) copy-start(f32[4]{0:T(128)} %rate_ref.5) | copy-start | bytes 52
  35.7 22.4 %collective-permute-start.10 = (bf16[4,128,128]{2,1,0:T(8,128)(2,1)S(1)}, bf16[4,128,128]{2,1,0:T(8,128)(2,1)S(1)}, u32[]{:S(2)}, u32[]{:S(2)}) collective-permute-start(bf16[4,128,128]{2,1,0:T(8,128)(2,1)S(1)} %state.1), channel_id=1, source_target_pairs={{0,24},{1,25},{2,26},{3,27},{4,28},{5,29},{6,30},{7,31}} | collective-permute-start | bytes 393224 | tf_op jit(solution)/shard_map/ppermute | solution.py:473
  41.5 16.5 %collective-permute-start.9 = (bf16[4,128,128]{2,1,0:T(8,128)(2,1)S(1)}, bf16[4,128,128]{2,1,0:T(8,128)(2,1)S(1)}, u32[]{:S(2)}, u32[]{:S(2)}) collective-permute-start(bf16[4,128,128]{2,1,0:T(8,128)(2,1)S(1)} %state.1), channel_id=1, source_target_pairs={{0,16},{8,24},{1,17},{9,25},{2,18},{10,26},{3,19},{11,27},{4,20},{... | collective-permute-start | bytes 393224 | tf_op jit(solution)/shard_map/ppermute | solution.py:473
  42.9 15.2 %collective-permute-start.8 = (bf16[4,128,128]{2,1,0:T(8,128)(2,1)S(1)}, bf16[4,128,128]{2,1,0:T(8,128)(2,1)S(1)}, u32[]{:S(2)}, u32[]{:S(2)}) collective-permute-start(bf16[4,128,128]{2,1,0:T(8,128)(2,1)S(1)} %state.1), channel_id=1, source_target_pairs={{0,8},{8,16},{16,24},{1,9},{9,17},{17,25},{2,10},{10,18},{18,26},{... | collective-permute-start | bytes 393224 | tf_op jit(solution)/shard_map/ppermute | solution.py:473
  45.5 2.6 %copy-start.5 = (bf16[512,6144]{1,0:T(8,128)(2,1)}, bf16[512,6144]{1,0:T(8,128)(2,1)S(1)}, u32[]{:S(2)}) copy-start(bf16[512,6144]{1,0:T(8,128)(2,1)S(1)} %collective-permute-done.7.refs_12_) | copy-start | bytes 18874372
  48.1 2.8 %copy-start.1 = (bf16[3072,1024]{1,0:T(8,128)(2,1)S(1)}, bf16[3072,1024]{1,0:T(8,128)(2,1)}, u32[]{:S(2)}) copy-start(bf16[3072,1024]{1,0:T(8,128)(2,1)} %copy-done) | copy-start | bytes 18874372
  50.9 7.2 %copy-start.4 = (f32[512]{0:T(512)S(1)}, f32[512]{0:T(512)}, u32[]{:S(2)}) copy-start(f32[512]{0:T(512)} %param.8) | copy-start | bytes 6148
  59.2 1.4 %collective-permute-start.11 = (bf16[128,512]{1,0:T(8,128)(2,1)S(1)}, bf16[128,512]{1,0:T(8,128)(2,1)S(1)}, u32[]{:S(2)}, u32[]{:S(2)}) collective-permute-start(bf16[128,512]{1,0:T(8,128)(2,1)S(1)} %get-tuple-element.44), channel_id=1, source_target_pairs={{0,1},{1,0},{2,3},{3,2},{4,5},{5,4},{6,7},{7,6},{8,9},{9,8},{10,11... | collective-permute-start | bytes 393224 | tf_op jit(solution)/shard_map/ppermute | solution.py:132
  62.6 7.8 %collective-permute-start.13 = (bf16[32,6144]{1,0:T(8,128)(2,1)S(1)}, bf16[32,6144]{1,0:T(8,128)(2,1)S(1)}, u32[]{:S(2)}, u32[]{:S(2)}) collective-permute-start(bf16[32,6144]{1,0:T(8,128)(2,1)S(1)} %get-tuple-element.50), channel_id=1, source_target_pairs={{0,4},{1,3},{2,6},{3,1},{4,0},{5,7},{6,2},{7,5},{8,12},{9,11},{10,... | collective-permute-start | bytes 1179656 | tf_op jit(solution)/shard_map/ppermute | solution.py:132
  64.6 12.0 %collective-permute-start.12 = (bf16[32,6144]{1,0:T(8,128)(2,1)S(1)}, bf16[32,6144]{1,0:T(8,128)(2,1)S(1)}, u32[]{:S(2)}, u32[]{:S(2)}) collective-permute-start(bf16[32,6144]{1,0:T(8,128)(2,1)S(1)} %get-tuple-element.48), channel_id=1, source_target_pairs={{0,4},{1,3},{2,6},{3,1},{4,0},{5,7},{6,2},{7,5},{8,12},{9,11},{10,... | collective-permute-start | bytes 1179656 | tf_op jit(solution)/shard_map/ppermute | solution.py:132
  70.5 7.8 %collective-permute-start.14 = (bf16[32,6144]{1,0:T(8,128)(2,1)S(1)}, bf16[32,6144]{1,0:T(8,128)(2,1)S(1)}, u32[]{:S(2)}, u32[]{:S(2)}) collective-permute-start(bf16[32,6144]{1,0:T(8,128)(2,1)S(1)} %add_convert_fusion.1), channel_id=1, source_target_pairs={{0,2},{1,5},{2,0},{3,7},{4,6},{5,1},{6,4},{7,3},{8,10},{9,13},{10,... | collective-permute-start | bytes 1179656 | tf_op jit(solution)/shard_map/ppermute | solution.py:132

commit v2 on v0

--- a/solution.py
+++ b/solution.py
@@ -1,10 +1,19 @@
+import functools
+
 import jax
 import jax.numpy as jnp
 from jax import lax
+from jax.experimental import pallas as pl
+from jax.experimental.pallas import tpu as pltpu
 from jax.sharding import PartitionSpec as P
 
 HD = 128
 BLOCK = 256
+F32, BF16 = jnp.float32, jnp.bfloat16
+VMEM = pl.BlockSpec(memory_space=pltpu.VMEM)
+SMEM = pl.BlockSpec(memory_space=pltpu.SMEM)
+HBM = pl.BlockSpec(memory_space=pl.ANY)
+MIB = 1 << 20
 
 
 def entering(value, axis, combine, identity):
@@ -59,7 +68,7 @@
     return (outputs.reshape(q_head.shape[0], q_head.shape[1]), final_state)
 
 
-def per_device(tokens, proj_weight, out_weight, head_gain, decay_rate):
+def general_device(tokens, proj_weight, out_weight, head_gain, decay_rate):
     heads_here = decay_rate.shape[0]
     width = head_gain.shape[0]
     flat = proj_weight.reshape(proj_weight.shape[0], 4 * width)
@@ -114,9 +123,426 @@
     )
 
 
+CORE = [(i, i ^ 1) for i in range(8)]
+FIRST = [(i, i ^ (4 if i & 1 else 2)) for i in range(8)]
+SECOND = [(i, i ^ (2 if i & 1 else 4)) for i in range(8)]
+
+
+def hop(value, pairs):
+    return lax.ppermute(value, "tp", pairs)
+
+
+STEP = 256
+SLOTS = 8
+
+
+def pinned(value):
+    return pltpu.with_memory_space_constraint(value, pltpu.VMEM)
+
+
+def in_hbm(value):
+    return pltpu.with_memory_space_constraint(value, pltpu.HBM)
+
+
+def chunks(first, count, w_hbm, buf, sem):
+    slots, step = buf.shape[:2]
+
+    def copy(i):
+        return pltpu.make_async_copy(
+            w_hbm.at[pl.ds(first + i * step, step)], buf.at[i % slots], sem.at[i % slots]
+        )
+
+    for i in range(min(slots, count)):
+        copy(i).start()
+    for i in range(count):
+        copy(i).wait()
+        yield i, buf[i % slots]
+        if i + slots < count:
+            copy(i + slots).start()
+
+
+def turn(block, at, kv_ref, qg_ref):
+    width = block.shape[2]
+    turned = jnp.swapaxes(block, 0, 1)
+    kv_ref[at, :width] = turned[1]
+    kv_ref[at, width:] = turned[2]
+    qg_ref[at, :width] = turned[0]
+    qg_ref[at, width:] = turned[3]
+    return turned
+
+
+def slot_places(index, shape, axis):
+    row = lax.broadcasted_iota(jnp.int32, shape, axis)
+    part = shape[axis] // 8
+    core = index & 1
+    near = jnp.where(core == 0, 2, 4)
+    far = 6 - near
+    owners = (
+        index,
+        index ^ 1,
+        index ^ near,
+        index ^ far,
+        index ^ 1 ^ far,
+        index ^ 1 ^ near,
+        index ^ 6,
+        index ^ 7,
+    )
+    place = row
+    for slot, owner in enumerate(owners):
+        place = jnp.where(row // part == slot, row + (owner - slot) * part, place)
+    return place.astype(F32)
+
+
+def tie_kernel(*refs):
+    pass
+
+
+def tie(values, others):
+    return pl.pallas_call(
+        tie_kernel,
+        in_specs=[HBM] * (len(values) + len(others)),
+        out_specs=[HBM] * len(values),
+        out_shape=[jax.ShapeDtypeStruct(v.shape, v.dtype) for v in values],
+        input_output_aliases={i: i for i in range(len(values))},
+        compiler_params=pltpu.CompilerParams(vmem_limit_bytes=MIB // 4),
+        name="tie",
+    )(*values, *others)
+
+
+def prep_kernel(first, last, started, w_hbm, pass_ref, *refs):
+    refs = refs[2 * started :]
+    kv_ref, qg_ref, *outs = refs[:-3]
+    buf, sem, pass_sem = refs[-3:]
+    step = buf.shape[1]
+    passing = []
+    if len(outs) == 1:
+        passing = [pltpu.make_async_copy(pass_ref, outs[0], pass_sem)]
+    for copy in passing:
+        copy.start()
+    for i, block in chunks(first, (last - first) // step, w_hbm, buf, sem):
+        if i == 0 and len(outs) == 2:
+            index = lax.axis_index("tp")
+            for axis, ref in enumerate(outs):
+                ref[...] = slot_places(index, ref.shape, axis)
+        turn(block, slice(first + i * step, first + (i + 1) * step), kv_ref, qg_ref)
+    for copy in passing:
+        copy.wait()
+
+
+def prep(first, last, proj_weight, turned, passed, outs, name):
+    depth, kinds, width = proj_weight.shape
+    out = pltpu.VMEM((depth, 2 * width), BF16)
+    slots = min(SLOTS, (last - first) // STEP)
+    return pl.pallas_call(
+        functools.partial(prep_kernel, first, last, bool(turned)),
+        in_specs=[HBM, HBM] + [VMEM] * len(turned),
+        out_specs=[VMEM] * (2 + len(outs)),
+        out_shape=[out, out, *outs],
+        scratch_shapes=[
+            pltpu.VMEM((slots, STEP, kinds, width), BF16),
+            pltpu.SemaphoreType.DMA((slots,)),
+            pltpu.SemaphoreType.DMA,
+        ],
+        input_output_aliases={2 + i: i for i in range(len(turned))},
+        compiler_params=pltpu.CompilerParams(vmem_limit_bytes=9 * MIB),
+        cost_estimate=pl.CostEstimate(
+            flops=0, bytes_accessed=4 * (last - first) * kinds * width, transcendentals=0
+        ),
+        name=name,
+    )(in_hbm(proj_weight), passed, *map(pinned, turned))
+
+
+def gather_rows(x_refs, x_all, at):
+    for ref in x_refs:
+        x_all[at : at + ref.shape[0], :] = ref[...]
+        at += ref.shape[0]
+
+
+def silu(mixed):
+    return (mixed / (1.0 + jnp.exp(-mixed))).astype(BF16)
+
+
+def near_kernel(n_rows, first, *refs):
+    x_refs = refs[:n_rows]
+    w_hbm, _, _, kv, qg, x_all, k_ref, v_ref, total, buf, sem = refs[n_rows:]
+    step, (count, width) = buf.shape[1], k_ref.shape
+    depth = kv.shape[0]
+    arriving = chunks(first, (depth - first) // step, w_hbm, buf, sem)
+    for c, block in arriving:
+        if c == 0:
+            gather_rows(x_refs, x_all, 0)
+            for i in range(2):
+                total[i] = jnp.dot(
+                    x_all[:count, :first],
+                    kv[:first, i * width : (i + 1) * width],
+                    preferred_element_type=F32,
+                )
+        at = first + c * step
+        turned = turn(block, slice(at, at + step), kv, qg)
+        for i in range(2):
+            total[i] += jnp.dot(
+                x_all[:count, at : at + step], turned[1 + i], preferred_element_type=F32
+            )
+    k_ref[...] = silu(total[0])
+    v_ref[...] = silu(total[1])
+
+
+def project_near(rows, first, proj_weight, kv, qg):
+    count = sum(r.shape[0] for r in rows)
+    depth, kinds, width = proj_weight.shape
+    turned = pltpu.VMEM(kv.shape, BF16)
+    half = pltpu.VMEM((count, width), BF16)
+    slots = min(SLOTS, (depth - first) // STEP)
+    return pl.pallas_call(
+        functools.partial(near_kernel, len(rows), first),
+        in_specs=[VMEM] * len(rows) + [HBM, VMEM, VMEM],
+        out_specs=[VMEM] * 5,
+        out_shape=[turned, turned, pltpu.VMEM((2 * count, depth), BF16), half, half],
+        scratch_shapes=[
+            pltpu.VMEM((2, count, width), F32),
+            pltpu.VMEM((slots, STEP, kinds, width), BF16),
+            pltpu.SemaphoreType.DMA((slots,)),
+        ],
+        input_output_aliases={len(rows) + 1: 0, len(rows) + 2: 1},
+        compiler_params=pltpu.CompilerParams(vmem_limit_bytes=9 * MIB),
+        cost_estimate=pl.CostEstimate(
+            flops=2 * count * depth * kinds * width,
+            bytes_accessed=4 * depth * kinds * width,
+            transcendentals=0,
+        ),
+        name="project_near",
+    )(*rows, in_hbm(proj_weight), pinned(kv), pinned(qg))
+
+
+def far_kernel(n_rows, rate_ref, place_ref, k0, v0, kv, _, *refs):
+    x_refs = refs[:n_rows]
+    x_all, k_ref, v_ref, s_ref = refs[n_rows:]
+    count, width = k_ref.shape
+    gather_rows(x_refs, x_all, count)
+    for i, ref in enumerate((k_ref, v_ref)):
+        ref[...] = silu(
+            jnp.dot(
+                x_all[count:],
+                kv[:, i * width : (i + 1) * width],
+                preferred_element_type=F32,
+            )
+        )
+    for h in range(s_ref.shape[0]):
+        cols = slice(h * HD, (h + 1) * HD)
+        fade = jnp.exp(-rate_ref[h] * (BLOCK - 1.0 - place_ref[...]))
+        k = jnp.concatenate([k0[:, cols], k_ref[:, cols]], 0).astype(F32) * fade
+        v = jnp.concatenate([v0[:, cols], v_ref[:, cols]], 0)
+        s_ref[h] = lax.dot_general(
+            k.astype(BF16), v, (((0,), (0,)), ((), ())), preferred_element_type=F32
+        ).astype(BF16)
+
+
+def project_far(rate, down, k0, v0, kv, x_all, rows):
+    count = sum(r.shape[0] for r in rows)
+    depth, width = rows[0].shape[1], k0.shape[1]
+    half = pltpu.VMEM((count, width), BF16)
+    return pl.pallas_call(
+        functools.partial(far_kernel, len(rows)),
+        in_specs=[SMEM] + [VMEM] * (5 + len(rows)),
+        out_specs=[VMEM] * 4,
+        out_shape=[
+            pltpu.VMEM(x_all.shape, BF16),
+            half,
+            half,
+            jax.ShapeDtypeStruct((rate.shape[0], HD, HD), BF16),
+        ],
+        input_output_aliases={5: 0},
+        compiler_params=pltpu.CompilerParams(vmem_limit_bytes=2 * MIB),
+        cost_estimate=pl.CostEstimate(
+            flops=4 * count * depth * width, bytes_accessed=4 * depth * width, transcendentals=0
+        ),
+        name="project_far",
+    )(rate, down, k0, v0, pinned(kv), pinned(x_all), *rows)
+
+
+def block_decay(rate):
+    return jnp.exp(jnp.full((HD, HD), -rate * BLOCK, F32))
+
+
+def carry_kernel(rate_ref, own_ref, came_ref, _, o_ref):
+    came = lax.axis_index("seq") > 0
+    for h in range(o_ref.shape[0]):
+        o_ref[h] = (
+            own_ref[h].astype(F32)
+            + jnp.where(came, block_decay(rate_ref[h]) * came_ref[h].astype(F32), 0.0)
+        ).astype(BF16)
+
+
+def gates_kernel(x_all, qg, w_hbm, q_ref, g_ref, w_ref, sem):
+    copy = pltpu.make_async_copy(w_hbm, w_ref, sem)
+    copy.start()
+    width = q_ref.shape[1]
+    q_ref[...] = silu(jnp.dot(x_all[...], qg[:, :width], preferred_element_type=F32))
+    mixed = jnp.dot(x_all[...], qg[:, width:], preferred_element_type=F32)
+    g_ref[...] = 1.0 / (1.0 + jnp.exp(-mixed))
+    copy.wait()
+
+
+def gates(x_all, qg, w):
+    count, depth = x_all.shape
+    width = qg.shape[1] // 2
+    return pl.pallas_call(
+        gates_kernel,
+        in_specs=[VMEM, VMEM, HBM],
+        out_specs=[VMEM] * 3,
+        out_shape=[
+            pltpu.VMEM((count, width), BF16),
+            pltpu.VMEM((count, width), F32),
+            pltpu.VMEM(w.shape, w.dtype),
+        ],
+        scratch_shapes=[pltpu.SemaphoreType.DMA],
+        compiler_params=pltpu.CompilerParams(vmem_limit_bytes=2 * MIB),
+        cost_estimate=pl.CostEstimate(
+            flops=4 * count * depth * width, bytes_accessed=8 * depth * width, transcendentals=0
+        ),
+        name="gates",
+    )(pinned(x_all), pinned(qg), in_hbm(w))
+
+
+def inner_kernel(rate_ref, place_ref, across_ref, q_ref, k0, k1, v0, v1, o_ref):
+    diff = place_ref[...] - across_ref[...]
+    seen = diff >= 0
+    diff = jnp.maximum(diff, 0.0)
+    for h in range(o_ref.shape[1] // HD):
+        cols = slice(h * HD, (h + 1) * HD)
+        k = jnp.concatenate([k0[:, cols], k1[:, cols]], 0)
+        v = jnp.concatenate([v0[:, cols], v1[:, cols]], 0)
+        scores = lax.dot_general(
+            q_ref[:, cols], k, (((1,), (1,)), ((), ())), preferred_element_type=F32
+        )
+        causal = jnp.where(seen, jnp.exp(-rate_ref[h] * diff), 0.0)
+        o_ref[:, cols] = jnp.dot(
+            (scores * causal).astype(BF16), v, preferred_element_type=F32
+        )
+
+
+TO_SUM = (3, 7, 1, 2, 5, 6, 0, 4)
+
+
+def finish_kernel(rate_ref, place_ref, gain_ref, in_ref, q_ref, g_ref, s1, s2, s3, y_ref, z_ref):
+    part = in_ref.shape[0] // 8
+    block = lax.axis_index("seq")
+    for h in range(in_ref.shape[1] // HD):
+        cols = slice(h * HD, (h + 1) * HD)
+        rate = rate_ref[h]
+        fade = block_decay(rate)
+        state = jnp.where(block > 0, s1[h].astype(F32), 0.0) + fade * (
+            jnp.where(block > 1, s2[h].astype(F32), 0.0)
+            + fade * jnp.where(block > 2, s3[h].astype(F32), 0.0)
+        )
+        high = state.astype(BF16)
+        low = (state - high.astype(F32)).astype(BF16)
+        q = q_ref[:, cols]
+        extra = jnp.dot(q, high, preferred_element_type=F32) + jnp.dot(
+            q, low, preferred_element_type=F32
+        )
+        attn = in_ref[:, cols] + extra * jnp.exp(-rate * (place_ref[...] + 1.0))
+        square = jnp.mean(attn * attn, axis=-1, keepdims=True)
+        y = (attn * lax.rsqrt(square + 1e-06) * gain_ref[:, cols] * g_ref[:, cols]).astype(BF16)
+        for slot, to in enumerate(TO_SUM):
+            to_ref, at = (y_ref, to) if to < 4 else (z_ref, to - 4)
+            to_ref[at * part : (at + 1) * part, cols] = y[slot * part : (slot + 1) * part]
+
+
+def small(kernel, n_smem, out, name, *args):
+    return pl.pallas_call(
+        kernel,
+        in_specs=[SMEM] * n_smem + [VMEM] * (len(args) - n_smem),
+        out_specs=jax.tree.map(lambda _: VMEM, out),
+        out_shape=out,
+        compiler_params=pltpu.CompilerParams(vmem_limit_bytes=3 * MIB),
+        name=name,
+    )(*args)
+
+
+def out_kernel(y_ref, z_ref, w_ref, u_ref, a_ref, b_ref, c_ref, d_ref):
+    rows, width = a_ref.shape
+    step = 1024
+    for at in range(0, width, step):
+        cols = slice(at, at + step)
+        total = jnp.dot(y_ref[...], w_ref[:, cols], preferred_element_type=F32) + jnp.dot(
+            z_ref[...], u_ref[:, cols], preferred_element_type=F32
+        )
+        for i, ref in enumerate((a_ref, b_ref, c_ref, d_ref)):
+            ref[:, cols] = total[i * rows : (i + 1) * rows].astype(ref.dtype)
+
+
+def out_rows(y, z, w, u):
+    rows, depth = y.shape
+    width = w.shape[1]
+    send = jax.ShapeDtypeStruct((rows // 4, width), BF16)
+    keep = jax.ShapeDtypeStruct((rows // 4, width), F32)
+    return pl.pallas_call(
+        out_kernel,
+        in_specs=[VMEM] * 4,
+        out_specs=[VMEM] * 4,
+        out_shape=[send, keep, send, keep],
+        compiler_params=pltpu.CompilerParams(vmem_limit_bytes=4 * MIB),
+        cost_estimate=pl.CostEstimate(
+            flops=4 * rows * depth * width, bytes_accessed=4 * depth * width, transcendentals=0
+        ),
+        name="out_rows",
+    )(y, z, pinned(w), pinned(u))
+
+
+def paired_device(tokens, proj_weight, out_weight, head_gain, decay_rate):
+    rows = tokens.shape[0]
+    heads = decay_rate.shape[0]
+
+    cuts = [proj_weight.shape[0] * i // 4 for i in range(5)]
+    w_other = hop(out_weight, CORE)
+    first = hop(tokens, FIRST)
+    copied = jax.ShapeDtypeStruct(tokens.shape, tokens.dtype)
+    *turned, passed = prep(cuts[0], cuts[1], proj_weight, [], tokens, [copied], "prep_a")
+    second = hop(passed, SECOND)
+    beside = hop(tokens, CORE)
+    places = [pltpu.VMEM((8 * rows, 1), F32), pltpu.VMEM((1, 8 * rows), F32)]
+    *turned, down, across = prep(cuts[1], cuts[2], proj_weight, turned, passed, places, "prep_b")
+    (first,) = tie([first], [down])
+    far = hop(first, SECOND)
+    second_beside = hop(first, CORE)
+    turned = prep(cuts[2], cuts[3], proj_weight, turned, first, [], "prep_c")
+    kv, qg, x_all, k0, v0 = project_near(
+        [tokens, beside, first, second], cuts[3], proj_weight, *turned
+    )
+    first_beside = hop(second, CORE)
+    (far,) = tie([far], [k0])
+    far_beside = hop(far, CORE)
+    x_all, k1, v1, states = project_far(
+        decay_rate, down, k0, v0, kv, x_all, [second_beside, first_beside, far, far_beside]
+    )
+
+    came = [
+        lax.ppermute(states, "seq", [(i, (i + k) % 4) for i in range(4)]) for k in (1, 2, 3)
+    ]
+    q, g, w_own = gates(x_all, qg, out_weight)
+    full = jax.ShapeDtypeStruct((8 * rows, heads * HD), F32)
+    inner = small(inner_kernel, 1, full, "inner", decay_rate, down, across, q, k0, k1, v0, v1)
+    split = jax.ShapeDtypeStruct((4 * rows, heads * HD), BF16)
+    y, y_other = small(
+        finish_kernel,
+        1,
+        [split, split],
+        "finish",
+        decay_rate, down, head_gain[None, :], inner, q, g, *came,
+    )
+    z = hop(y_other, CORE)
+    a, b, c, d = out_rows(y, z, w_own, w_other)
+    got_a = hop(a, SECOND)
+    got_c = hop(c, SECOND)
+    got_b = hop((b + got_a.astype(F32)).astype(BF16), FIRST)
+    return (d + got_c.astype(F32) + got_b.astype(F32)).astype(BF16)
+
+
 def solution(mesh):
+    paired = mesh.shape["tp"] == 8 and mesh.shape["seq"] == 4
     return jax.shard_map(
-        per_device,
+        paired_device if paired else general_device,
         mesh=mesh,
         in_specs=(P(("seq", "tp"), None), P(None, None, "tp"), P("tp", None), P("tp"), P("tp")),
         out_specs=P(("seq", "tp"), None),

time: 138 us -> 60.3 us (0.44); the launches traced: 136 us -> 60.1 us
  waiting for transfers between devices: 52.5 us -> 21.7 us
  local copies, waits for them, and re-layouts: 26.9 us -> 1.04 us
  Pallas kernels: 0 us -> 24.2 us
  matrix products: 20.6 us -> 0 us
  blocking collectives: 19.8 us -> 0 us
  between operations: 14.2 us -> 0.14 us
  starting transfers between devices: 0.04 us -> 12.1 us
    reduce_scatter x1 -> x0, waiting for transfers between devices: 51.4 us -> none  [per_device(): lax.psum_scatter(jnp.dot(joined, out_weight, preferred_element_type=jnp.f...]
    unnamed x6, local copies, waits for them, and re-layouts: 26.5 us -> 1.04 us
    pallas_call x0 -> x11, Pallas kernels: none -> 24.2 us  [the longest x3 9.45 us: prep(): pl.pallas_call(functools.partial(prep_kernel, first, last, bool(turned)),...]
    ppermute x0 -> x15, waiting for transfers between devices: none -> 21.7 us  [the longest x12 15.6 us: hop(): return lax.ppermute(value, 'tp', pairs)]
    dot_general x6 -> x0, matrix products: 20.6 us -> none  [the longest x1 12.5 us: per_device(): jnp.dot(lax.all_gather(tokens, 'tp', axis=0, tiled=True), flat, preferred...]
    all_gather x1 -> x0, blocking collectives: 12.5 us -> none  [entering(): lax.all_gather(part.astype(kind), axis)]
    ppermute x0 -> x15, starting transfers between devices: none -> 12.1 us  [the longest x12 8.24 us: hop(): return lax.ppermute(value, 'tp', pairs)]
    unnamed x1 -> x0, blocking collectives: 7.24 us -> none
  transfers between devices with their start and end apart: 2 -> 15, of which waited for: 2 -> 7; matrix products, arithmetic and copies ran while one was open for 20% -> 0% of each run, Pallas kernels for 0% -> 37%
where the time goes in v2:
time: 60.3 us; the launch traced here: 60.1 us
  Pallas kernels  24.2 us (40%)
  waiting for transfers between devices  21.7 us (36%)
  starting transfers between devices  12.1 us (20%)
  local copies, waits for them, and re-layouts  1.04 us (2%)
  other arithmetic  0.93 us (2%)
    ppermute x12, waiting for transfers between devices, hop(): return lax.ppermute(value, 'tp', pairs)  15.6 us
    pallas_call x3, Pallas kernels, prep(): pl.pallas_call(functools.partial(prep_kernel, first, last, bool(turned)),...  9.45 us
    ppermute x12, starting transfers between devices, hop(): return lax.ppermute(value, 'tp', pairs)  8.24 us
    ppermute x3, waiting for transfers between devices, paired_device(): lax.ppermute(states, 'seq', [(i, (i + k) % 4) for i in range(4)])  6.12 us
    pallas_call x1, Pallas kernels, project_near(): pl.pallas_call(functools.partial(near_kernel, len(rows), first), in_specs...  4.33 us
    ppermute x3, starting transfers between devices, paired_device(): lax.ppermute(states, 'seq', [(i, (i + k) % 4) for i in range(4)])  3.82 us
    pallas_call x1, Pallas kernels, gates(): pl.pallas_call(gates_kernel, in_specs=[VMEM, VMEM, HBM], out_specs=[VMEM]...  3.54 us
    pallas_call x1, Pallas kernels, project_far(): pl.pallas_call(functools.partial(far_kernel, len(rows)), in_specs=[SMEM]...  2.69 us
  transfers between devices with their start and end apart: 15, of which 7 were waited for; matrix products, arithmetic and copies ran while one was open for 0% of the time, Pallas kernels for 37%

profile of v2, /device:TPU:9, one launch (start us, length us, event | category | flops | bytes accessed | tf_op | source)
XLA Modules:
  0.0 60.1 jit_solution(17082465783642895293)
XLA Ops:
  0.0 0.7 %collective-permute-start.11 = (bf16[512,6144]{1,0:T(8,128)(2,1)}, bf16[512,6144]{1,0:T(8,128)(2,1)S(1)}, u32[]{:S(2)}, u32[]{:S(2)}) collective-permute-start(bf16[512,6144]{1,0:T(8,128)(2,1)} %w_hbm.7), channel_id=1, source_target_pairs={{0,1},{1,0},{2,3},{3,2},{4,5},{5,4},{6,7},{7,6},{8,9},{9,8},{10,11... | collective-permute-start | bytes 18874376 | tf_op jit(solution)/shard_map/ppermute | solution.py:132
  0.7 1.2 %collective-permute-start.1 = (bf16[32,6144]{1,0:T(8,128)(2,1)}, bf16[32,6144]{1,0:T(8,128)(2,1)S(1)}, u32[]{:S(2)}, u32[]{:S(2)}) collective-permute-start(bf16[32,6144]{1,0:T(8,128)(2,1)} %refs_0_.1), channel_id=1, source_target_pairs={{0,2},{1,5},{2,0},{3,7},{4,6},{5,1},{6,4},{7,3},{8,10},{9,13},{10,... | collective-permute-start | bytes 1179656 | tf_op jit(solution)/shard_map/ppermute | solution.py:132
  1.9 1.0 %copy-done = bf16[32,6144]{1,0:T(8,128)(2,1)S(1)} copy-done((bf16[32,6144]{1,0:T(8,128)(2,1)S(1)}, bf16[32,6144]{1,0:T(8,128)(2,1)}, u32[]{:S(2)}) %copy-start) | copy-done | bytes 393240
  2.9 3.3 %prep_a.1 = (bf16[6144,1024]{1,0:T(8,128)(2,1)S(1)}, bf16[6144,1024]{1,0:T(8,128)(2,1)S(1)}, bf16[32,6144]{1,0:T(8,128)(2,1)S(1)}) custom-call(bf16[6144,4,512]{2,1,0:T(4,128)(2,1)} %refs_4_.1, bf16[32,6144]{1,0:T(8,128)(2,1)S(1)} %copy-done), custom_call_target="tpu_custom_call" | custom-call | bytes 12582912 | tf_op jit(solution)/shard_map/prep_a/pallas_call | solution.py:236
  6.2 1.3 %collective-permute-start.2 = (bf16[32,6144]{1,0:T(8,128)(2,1)S(1)}, bf16[32,6144]{1,0:T(8,128)(2,1)S(1)}, u32[]{:S(2)}, u32[]{:S(2)}) collective-permute-start(bf16[32,6144]{1,0:T(8,128)(2,1)S(1)} %get-tuple-element.32.pass_ref), channel_id=1, source_target_pairs={{0,4},{1,3},{2,6},{3,1},{4,0},{5,7},{6,2},{7,5},{8,12},{9,11},{10,... | collective-permute-start | bytes 1179656 | tf_op jit(solution)/shard_map/ppermute | solution.py:132
  7.5 0.6 collective-permute-start
  8.1 3.1 %prep_b.1 = (bf16[6144,1024]{1,0:T(8,128)(2,1)S(1)}, bf16[6144,1024]{1,0:T(8,128)(2,1)S(1)}, f32[256,1]{1,0:T(8,128)S(1)}, f32[1,256]{1,0:T(1,128)S(1)}) custom-call(bf16[6144,4,512]{2,1,0:T(4,128)(2,1)} %refs_4_.1, bf16[32,6144]{1,0:T(8,128)(2,1)S(1)} %get-tuple-element.32.pass_ref, ...), custom_call_target="tpu_custom_call", output_to_operand_aliasing={{0}: (2, {}), {1}: (3, {})} | custom-call | bytes 12582912 | tf_op jit(solution)/shard_map/prep_b/pallas_call | solution.py:236
  11.2 0.3 collective-permute-start.5
  11.5 0.3 collective-permute-start.3
  11.8 3.1 %prep_c.1 = (bf16[6144,1024]{1,0:T(8,128)(2,1)S(1)}, bf16[6144,1024]{1,0:T(8,128)(2,1)S(1)}) custom-call(bf16[6144,4,512]{2,1,0:T(4,128)(2,1)} %refs_4_.1, bf16[32,6144]{1,0:T(8,128)(2,1)S(1)} %tie.2.pass_ref.refs_2_, bf16[6144,1024]{1,0:T(8,128)(2,1)S(1)} %get-tuple-element.37.refs_0_, ...), custom_call_target="tpu_custom_call", output_to_operand_aliasing={{0}: (2, {}), {1}: (3, {})} | custom-call | bytes 12582912 | tf_op jit(solution)/shard_map/prep_c/pallas_call | solution.py:236
  14.9 0.3 collective-permute-start.4
  15.2 4.3 %project_near.1 = (bf16[6144,1024]{1,0:T(8,128)(2,1)S(1)}, bf16[6144,1024]{1,0:T(8,128)(2,1)S(1)}, bf16[256,6144]{1,0:T(8,128)(2,1)S(1)}, bf16[128,512]{1,0:T(8,128)(2,1)S(1)}, bf16[128,512]{1,0:T(8,128)(2,1)S(1)}) custom-call(bf16[32,6144]{1,0:T(8,128)(2,1)S(1)} %copy-done, ...), custom_call_target="tpu_custom_call", output_to_operand_aliasing={{0}: (5, {}), {1}: (6, {})} | custom-call | flops 3221225472 | bytes 50331648 | tf_op jit(solution)/shard_map/project_near/pallas_call | solution.py:296
  19.6 0.3 collective-permute-start.6
  19.9 1.5 %collective-permute-done.6.refs_3_ = bf16[32,6144]{1,0:T(8,128)(2,1)S(1)} collective-permute-done((bf16[32,6144]{1,0:T(8,128)(2,1)S(1)}, bf16[32,6144]{1,0:T(8,128)(2,1)S(1)}, u32[]{:S(2)}, u32[]{:S(2)}) %collective-permute-start.6) | collective-permute-done | bytes 393248 | tf_op jit(solution)/shard_map/ppermute | solution.py:132
  21.3 2.7 %project_far.1 = (bf16[256,6144]{1,0:T(8,128)(2,1)S(1)}, bf16[128,512]{1,0:T(8,128)(2,1)S(1)}, bf16[128,512]{1,0:T(8,128)(2,1)S(1)}, bf16[4,128,128]{2,1,0:T(8,128)(2,1)S(1)}) custom-call(f32[4]{0:T(128)S(1)} %copy-done.1, f32[256,1]{1,0:T(8,128)S(1)} %get-tuple-element.35.refs_1_.place_ref, ...), custom_call_target="tpu_custom_call", output_to_operand_aliasing={{0}: (5, {})} | custom-call | flops 1610612736 | bytes 12582912 | tf_op jit(solution)/shard_map/project_far/pallas_call | solution.py:344
  24.1 1.4 %collective-permute-start.7 = (bf16[4,128,128]{2,1,0:T(8,128)(2,1)S(1)}, bf16[4,128,128]{2,1,0:T(8,128)(2,1)S(1)}, u32[]{:S(2)}, u32[]{:S(2)}) collective-permute-start(bf16[4,128,128]{2,1,0:T(8,128)(2,1)S(1)} %get-tuple-element.51), channel_id=1, source_target_pairs={{0,8},{8,16},{16,24},{24,0},{1,9},{9,17},{17,25},{25,1},{2,10},{10... | collective-permute-start | bytes 393224 | tf_op jit(solution)/shard_map/ppermute | solution.py:521
  25.4 1.1 %collective-permute-start.8 = (bf16[4,128,128]{2,1,0:T(8,128)(2,1)S(1)}, bf16[4,128,128]{2,1,0:T(8,128)(2,1)S(1)}, u32[]{:S(2)}, u32[]{:S(2)}) collective-permute-start(bf16[4,128,128]{2,1,0:T(8,128)(2,1)S(1)} %get-tuple-element.51), channel_id=1, source_target_pairs={{0,16},{8,24},{16,0},{24,8},{1,17},{9,25},{17,1},{25,9},{2,18},{10... | collective-permute-start | bytes 393224 | tf_op jit(solution)/shard_map/ppermute | solution.py:521
  26.5 1.4 %collective-permute-start.9 = (bf16[4,128,128]{2,1,0:T(8,128)(2,1)S(1)}, bf16[4,128,128]{2,1,0:T(8,128)(2,1)S(1)}, u32[]{:S(2)}, u32[]{:S(2)}) collective-permute-start(bf16[4,128,128]{2,1,0:T(8,128)(2,1)S(1)} %get-tuple-element.51), channel_id=1, source_target_pairs={{0,24},{8,0},{16,8},{24,16},{1,25},{9,1},{17,9},{25,17},{2,26},{10... | collective-permute-start | bytes 393224 | tf_op jit(solution)/shard_map/ppermute | solution.py:521
  27.9 3.5 %gates.1 = (bf16[256,512]{1,0:T(8,128)(2,1)S(1)}, f32[256,512]{1,0:T(8,128)S(1)}, bf16[512,6144]{1,0:T(8,128)(2,1)S(1)}) custom-call(bf16[256,6144]{1,0:T(8,128)(2,1)S(1)} %get-tuple-element.45.x_all, bf16[6144,1024]{1,0:T(8,128)(2,1)S(1)} %get-tuple-element.46.qg, bf16[512,6144]{1,0:T(8,128)(2,1)} %w_hbm.7), custom_call_target="tpu_custom_call" | custom-call | flops 3221225472 | bytes 25165824 | tf_op jit(solution)/shard_map/gates/pallas_call | solution.py:389
  31.4 1.2 %inner.1.in_ref = f32[256,512]{1,0:T(8,128)S(1)} custom-call(f32[4]{0:T(128)S(1)} %copy-done.1, f32[256,1]{1,0:T(8,128)S(1)} %get-tuple-element.35.refs_1_.place_ref, f32[1,256]{1,0:T(1,128)S(1)} %get-tuple-element.36.across_ref, bf16[256,512]{1,0:T(8,128)(2,1)S(1)} %get-tuple-element.47.q_ref, bf16[128,512]{1,0:T(8,128)(2,1)S(1)} %get-tuple-element.41.refs_1_.k0, ...), custom_call_target="tpu_custom_call" | custom-call | tf_op jit(solution)/shard_map/inner/pallas_call | solution.py:453
  32.7 3.8 %collective-permute-done.8.s2 = bf16[4,128,128]{2,1,0:T(8,128)(2,1)S(1)} collective-permute-done((bf16[4,128,128]{2,1,0:T(8,128)(2,1)S(1)}, bf16[4,128,128]{2,1,0:T(8,128)(2,1)S(1)}, u32[]{:S(2)}, u32[]{:S(2)}) %collective-permute-start.8) | collective-permute-done | bytes 131104 | tf_op jit(solution)/shard_map/ppermute | solution.py:521
  36.5 2.3 %collective-permute-done.9.s3 = bf16[4,128,128]{2,1,0:T(8,128)(2,1)S(1)} collective-permute-done((bf16[4,128,128]{2,1,0:T(8,128)(2,1)S(1)}, bf16[4,128,128]{2,1,0:T(8,128)(2,1)S(1)}, u32[]{:S(2)}, u32[]{:S(2)}) %collective-permute-start.9) | collective-permute-done | bytes 131104 | tf_op jit(solution)/shard_map/ppermute | solution.py:521
  38.8 1.1 %finish.1 = (bf16[128,512]{1,0:T(8,128)(2,1)S(1)}, bf16[128,512]{1,0:T(8,128)(2,1)S(1)}) custom-call(f32[4]{0:T(128)S(1)} %copy-done.1, f32[256,1]{1,0:T(8,128)S(1)} %get-tuple-element.35.refs_1_.place_ref, f32[1,512]{1,0:T(1,128)S(1)} %bitcast.1, f32[256,512]{1,0:T(8,128)S(1)} %inner.1.in_ref, bf16[256,512]{1,0:T(8,128)(2,1)S(1)} %get-tuple-element.47.q_ref, ...), custom_call_target="tpu_custom_call" | custom-call | tf_op jit(solution)/shard_map/finish/pallas_call | solution.py:453
  39.9 0.6 collective-permute-start.10
  40.5 1.0 %collective-permute-done.10.z_ref = bf16[128,512]{1,0:T(8,128)(2,1)S(1)} collective-permute-done((bf16[128,512]{1,0:T(8,128)(2,1)S(1)}, bf16[128,512]{1,0:T(8,128)(2,1)S(1)}, u32[]{:S(2)}, u32[]{:S(2)}) %collective-permute-start.10) | collective-permute-done | bytes 131104 | tf_op jit(solution)/shard_map/ppermute | solution.py:132
  41.5 1.8 %out_rows.1 = (bf16[32,6144]{1,0:T(8,128)(2,1)S(1)}, f32[32,6144]{1,0:T(8,128)S(1)}, bf16[32,6144]{1,0:T(8,128)(2,1)S(1)}, f32[32,6144]{1,0:T(8,128)S(1)}) custom-call(bf16[128,512]{1,0:T(8,128)(2,1)S(1)} %get-tuple-element.52.y_ref, bf16[128,512]{1,0:T(8,128)(2,1)S(1)} %collective-permute-done.10.z_ref, bf16[512,6144]{1,0:T(8,128)(2,1)S(1)} %get-tuple-element.54.w_ref, ...), custom_call_target="tpu_custom_call" | custom-call | flops 1610612736 | bytes 12582912 | tf_op jit(solution)/shard_map/out_rows/pallas_call | solution.py:480
  43.3 1.3 %collective-permute-start.13 = (bf16[32,6144]{1,0:T(8,128)(2,1)S(1)}, bf16[32,6144]{1,0:T(8,128)(2,1)S(1)}, u32[]{:S(2)}, u32[]{:S(2)}) collective-permute-start(bf16[32,6144]{1,0:T(8,128)(2,1)S(1)} %get-tuple-element.58), channel_id=1, source_target_pairs={{0,4},{1,3},{2,6},{3,1},{4,0},{5,7},{6,2},{7,5},{8,12},{9,11},{10,... | collective-permute-start | bytes 1179656 | tf_op jit(solution)/shard_map/ppermute | solution.py:132
  44.8 5.5 %collective-permute-done.13 = bf16[32,6144]{1,0:T(8,128)(2,1)S(1)} collective-permute-done((bf16[32,6144]{1,0:T(8,128)(2,1)S(1)}, bf16[32,6144]{1,0:T(8,128)(2,1)S(1)}, u32[]{:S(2)}, u32[]{:S(2)}) %collective-permute-start.13) | collective-permute-done | bytes 393248 | tf_op jit(solution)/shard_map/ppermute | solution.py:132
  50.4 1.2 %collective-permute-start.14 = (bf16[32,6144]{1,0:T(8,128)(2,1)S(1)}, bf16[32,6144]{1,0:T(8,128)(2,1)S(1)}, u32[]{:S(2)}, u32[]{:S(2)}) collective-permute-start(bf16[32,6144]{1,0:T(8,128)(2,1)S(1)} %add_convert_fusion.1), channel_id=1, source_target_pairs={{0,2},{1,5},{2,0},{3,7},{4,6},{5,1},{6,4},{7,3},{8,10},{9,13},{10,... | collective-permute-start | bytes 1179656 | tf_op jit(solution)/shard_map/ppermute | solution.py:132
  51.5 3.0 %collective-permute-done.12 = bf16[32,6144]{1,0:T(8,128)(2,1)S(1)} collective-permute-done((bf16[32,6144]{1,0:T(8,128)(2,1)S(1)}, bf16[32,6144]{1,0:T(8,128)(2,1)S(1)}, u32[]{:S(2)}, u32[]{:S(2)}) %collective-permute-start.12) | collective-permute-done | bytes 393248 | tf_op jit(solution)/shard_map/ppermute | solution.py:132
  54.5 4.7 %collective-permute-done.14 = bf16[32,6144]{1,0:T(8,128)(2,1)S(1)} collective-permute-done((bf16[32,6144]{1,0:T(8,128)(2,1)S(1)}, bf16[32,6144]{1,0:T(8,128)(2,1)S(1)}, u32[]{:S(2)}, u32[]{:S(2)}) %collective-permute-start.14) | collective-permute-done | bytes 393248 | tf_op jit(solution)/shard_map/ppermute | solution.py:132
  59.2 0.9 %add_convert_fusion = bf16[32,6144]{1,0:T(8,128)(2,1)} fusion(bf16[32,6144]{1,0:T(8,128)(2,1)S(1)} %collective-permute-done.14, f32[32,6144]{1,0:T(8,128)S(1)} %get-tuple-element.55, bf16[32,6144]{1,0:T(8,128)(2,1)S(1)} %collective-permute-done.12), kind=kLoop, calls=%fused_computation | loop fusion | flops 983040 | bytes 1966080 | tf_op jit(solution)/shard_map/convert_element_type | solution.py:539
  (17 shorter events, 0.4 us)
Async XLA Ops:
  0.0 41.5 %collective-permute-start.11 = (bf16[512,6144]{1,0:T(8,128)(2,1)}, bf16[512,6144]{1,0:T(8,128)(2,1)S(1)}, u32[]{:S(2)}, u32[]{:S(2)}) collective-permute-start(bf16[512,6144]{1,0:T(8,128)(2,1)} %w_hbm.7), channel_id=1, source_target_pairs={{0,1},{1,0},{2,3},{3,2},{4,5},{5,4},{6,7},{7,6},{8,9},{9,8},{10,11... | collective-permute-start | bytes 18874376 | tf_op jit(solution)/shard_map/ppermute | solution.py:132
  0.7 10.5 %collective-permute-start.1 = (bf16[32,6144]{1,0:T(8,128)(2,1)}, bf16[32,6144]{1,0:T(8,128)(2,1)S(1)}, u32[]{:S(2)}, u32[]{:S(2)}) collective-permute-start(bf16[32,6144]{1,0:T(8,128)(2,1)} %refs_0_.1), channel_id=1, source_target_pairs={{0,2},{1,5},{2,0},{3,7},{4,6},{5,1},{6,4},{7,3},{8,10},{9,13},{10,... | collective-permute-start | bytes 1179656 | tf_op jit(solution)/shard_map/ppermute | solution.py:132
  1.9 1.0 %copy-start = (bf16[32,6144]{1,0:T(8,128)(2,1)S(1)}, bf16[32,6144]{1,0:T(8,128)(2,1)}, u32[]{:S(2)}) copy-start(bf16[32,6144]{1,0:T(8,128)(2,1)} %refs_0_.1) | copy-start | bytes 1179652
  6.2 8.6 %collective-permute-start.2 = (bf16[32,6144]{1,0:T(8,128)(2,1)S(1)}, bf16[32,6144]{1,0:T(8,128)(2,1)S(1)}, u32[]{:S(2)}, u32[]{:S(2)}) collective-permute-start(bf16[32,6144]{1,0:T(8,128)(2,1)S(1)} %get-tuple-element.32.pass_ref), channel_id=1, source_target_pairs={{0,4},{1,3},{2,6},{3,1},{4,0},{5,7},{6,2},{7,5},{8,12},{9,11},{10,... | collective-permute-start | bytes 1179656 | tf_op jit(solution)/shard_map/ppermute | solution.py:132
  7.5 7.7 %collective-permute-start = (bf16[32,6144]{1,0:T(8,128)(2,1)S(1)}, bf16[32,6144]{1,0:T(8,128)(2,1)S(1)}, u32[]{:S(2)}, u32[]{:S(2)}) collective-permute-start(bf16[32,6144]{1,0:T(8,128)(2,1)S(1)} %copy-done), channel_id=1, source_target_pairs={{0,1},{1,0},{2,3},{3,2},{4,5},{5,4},{6,7},{7,6},{8,9},{9,8},{10,11... | collective-permute-start | bytes 1179656 | tf_op jit(solution)/shard_map/ppermute | solution.py:132
  11.2 8.4 %collective-permute-start.5 = (bf16[32,6144]{1,0:T(8,128)(2,1)S(1)}, bf16[32,6144]{1,0:T(8,128)(2,1)S(1)}, u32[]{:S(2)}, u32[]{:S(2)}) collective-permute-start(bf16[32,6144]{1,0:T(8,128)(2,1)S(1)} %tie.2.pass_ref.refs_2_), channel_id=1, source_target_pairs={{0,4},{1,3},{2,6},{3,1},{4,0},{5,7},{6,2},{7,5},{8,12},{9,11},{10,... | collective-permute-start | bytes 1179656 | tf_op jit(solution)/shard_map/ppermute | solution.py:132
  11.5 8.4 %collective-permute-start.3 = (bf16[32,6144]{1,0:T(8,128)(2,1)S(1)}, bf16[32,6144]{1,0:T(8,128)(2,1)S(1)}, u32[]{:S(2)}, u32[]{:S(2)}) collective-permute-start(bf16[32,6144]{1,0:T(8,128)(2,1)S(1)} %tie.2.pass_ref.refs_2_), channel_id=1, source_target_pairs={{0,1},{1,0},{2,3},{3,2},{4,5},{5,4},{6,7},{7,6},{8,9},{9,8},{10,11... | collective-permute-start | bytes 1179656 | tf_op jit(solution)/shard_map/ppermute | solution.py:132
  14.9 5.0 %collective-permute-start.4 = (bf16[32,6144]{1,0:T(8,128)(2,1)S(1)}, bf16[32,6144]{1,0:T(8,128)(2,1)S(1)}, u32[]{:S(2)}, u32[]{:S(2)}) collective-permute-start(bf16[32,6144]{1,0:T(8,128)(2,1)S(1)} %collective-permute-done.2.refs_3_), channel_id=1, source_target_pairs={{0,1},{1,0},{2,3},{3,2},{4,5},{5,4},{6,7},{7,6},{8,9},{9,8},{10,11... | collective-permute-start | bytes 1179656 | tf_op jit(solution)/shard_map/ppermute | solution.py:132
  15.2 6.2 %copy-start.1 = (f32[4]{0:T(128)S(1)}, f32[4]{0:T(128)}, u32[]{:S(2)}) copy-start(f32[4]{0:T(128)} %rate_ref.5) | copy-start | bytes 52
  19.6 1.8 %collective-permute-start.6 = (bf16[32,6144]{1,0:T(8,128)(2,1)S(1)}, bf16[32,6144]{1,0:T(8,128)(2,1)S(1)}, u32[]{:S(2)}, u32[]{:S(2)}) collective-permute-start(bf16[32,6144]{1,0:T(8,128)(2,1)S(1)} %tie.3.refs_2_), channel_id=1, source_target_pairs={{0,1},{1,0},{2,3},{3,2},{4,5},{5,4},{6,7},{7,6},{8,9},{9,8},{10,11... | collective-permute-start | bytes 1179656 | tf_op jit(solution)/shard_map/ppermute | solution.py:132
  24.0 14.8 %copy-start.2 = (f32[512]{0:T(512)S(1)}, f32[512]{0:T(512)}, u32[]{:S(2)}) copy-start(f32[512]{0:T(512)} %param.8) | copy-start | bytes 6148
  24.1 8.6 %collective-permute-start.7 = (bf16[4,128,128]{2,1,0:T(8,128)(2,1)S(1)}, bf16[4,128,128]{2,1,0:T(8,128)(2,1)S(1)}, u32[]{:S(2)}, u32[]{:S(2)}) collective-permute-start(bf16[4,128,128]{2,1,0:T(8,128)(2,1)S(1)} %get-tuple-element.51), channel_id=1, source_target_pairs={{0,8},{8,16},{16,24},{24,0},{1,9},{9,17},{17,25},{25,1},{2,10},{10... | collective-permute-start | bytes 393224 | tf_op jit(solution)/shard_map/ppermute | solution.py:521
  25.4 11.1 %collective-permute-start.8 = (bf16[4,128,128]{2,1,0:T(8,128)(2,1)S(1)}, bf16[4,128,128]{2,1,0:T(8,128)(2,1)S(1)}, u32[]{:S(2)}, u32[]{:S(2)}) collective-permute-start(bf16[4,128,128]{2,1,0:T(8,128)(2,1)S(1)} %get-tuple-element.51), channel_id=1, source_target_pairs={{0,16},{8,24},{16,0},{24,8},{1,17},{9,25},{17,1},{25,9},{2,18},{10... | collective-permute-start | bytes 393224 | tf_op jit(solution)/shard_map/ppermute | solution.py:521
  26.5 12.3 %collective-permute-start.9 = (bf16[4,128,128]{2,1,0:T(8,128)(2,1)S(1)}, bf16[4,128,128]{2,1,0:T(8,128)(2,1)S(1)}, u32[]{:S(2)}, u32[]{:S(2)}) collective-permute-start(bf16[4,128,128]{2,1,0:T(8,128)(2,1)S(1)} %get-tuple-element.51), channel_id=1, source_target_pairs={{0,24},{8,0},{16,8},{24,16},{1,25},{9,1},{17,9},{25,17},{2,26},{10... | collective-permute-start | bytes 393224 | tf_op jit(solution)/shard_map/ppermute | solution.py:521
  39.9 1.5 %collective-permute-start.10 = (bf16[128,512]{1,0:T(8,128)(2,1)S(1)}, bf16[128,512]{1,0:T(8,128)(2,1)S(1)}, u32[]{:S(2)}, u32[]{:S(2)}) collective-permute-start(bf16[128,512]{1,0:T(8,128)(2,1)S(1)} %get-tuple-element.53), channel_id=1, source_target_pairs={{0,1},{1,0},{2,3},{3,2},{4,5},{5,4},{6,7},{7,6},{8,9},{9,8},{10,11... | collective-permute-start | bytes 393224 | tf_op jit(solution)/shard_map/ppermute | solution.py:132
  43.3 7.0 %collective-permute-start.13 = (bf16[32,6144]{1,0:T(8,128)(2,1)S(1)}, bf16[32,6144]{1,0:T(8,128)(2,1)S(1)}, u32[]{:S(2)}, u32[]{:S(2)}) collective-permute-start(bf16[32,6144]{1,0:T(8,128)(2,1)S(1)} %get-tuple-element.58), channel_id=1, source_target_pairs={{0,4},{1,3},{2,6},{3,1},{4,0},{5,7},{6,2},{7,5},{8,12},{9,11},{10,... | collective-permute-start | bytes 1179656 | tf_op jit(solution)/shard_map/ppermute | solution.py:132
  44.6 9.9 %collective-permute-start.12 = (bf16[32,6144]{1,0:T(8,128)(2,1)S(1)}, bf16[32,6144]{1,0:T(8,128)(2,1)S(1)}, u32[]{:S(2)}, u32[]{:S(2)}) collective-permute-start(bf16[32,6144]{1,0:T(8,128)(2,1)S(1)} %get-tuple-element.56), channel_id=1, source_target_pairs={{0,4},{1,3},{2,6},{3,1},{4,0},{5,7},{6,2},{7,5},{8,12},{9,11},{10,... | collective-permute-start | bytes 1179656 | tf_op jit(solution)/shard_map/ppermute | solution.py:132
  50.4 8.9 %collective-permute-start.14 = (bf16[32,6144]{1,0:T(8,128)(2,1)S(1)}, bf16[32,6144]{1,0:T(8,128)(2,1)S(1)}, u32[]{:S(2)}, u32[]{:S(2)}) collective-permute-start(bf16[32,6144]{1,0:T(8,128)(2,1)S(1)} %add_convert_fusion.1), channel_id=1, source_target_pairs={{0,2},{1,5},{2,0},{3,7},{4,6},{5,1},{6,4},{7,3},{8,10},{9,13},{10,... | collective-permute-start | bytes 1179656 | tf_op jit(solution)/shard_map/ppermute | solution.py:132

commit v3 on v2

--- a/solution.py
+++ b/solution.py
@@ -152,13 +152,16 @@
             w_hbm.at[pl.ds(first + i * step, step)], buf.at[i % slots], sem.at[i % slots]
         )
 
+    def arriving():
+        for i in range(count):
+            copy(i).wait()
+            yield i, buf[i % slots]
+            if i + slots < count:
+                copy(i + slots).start()
+
     for i in range(min(slots, count)):
         copy(i).start()
-    for i in range(count):
-        copy(i).wait()
-        yield i, buf[i % slots]
-        if i + slots < count:
-            copy(i + slots).start()
+    return arriving()
 
 
 def turn(block, at, kv_ref, qg_ref):
@@ -219,11 +222,12 @@
         passing = [pltpu.make_async_copy(pass_ref, outs[0], pass_sem)]
     for copy in passing:
         copy.start()
-    for i, block in chunks(first, (last - first) // step, w_hbm, buf, sem):
-        if i == 0 and len(outs) == 2:
-            index = lax.axis_index("tp")
-            for axis, ref in enumerate(outs):
-                ref[...] = slot_places(index, ref.shape, axis)
+    arriving = chunks(first, (last - first) // step, w_hbm, buf, sem)
+    if len(outs) == 2:
+        index = lax.axis_index("tp")
+        for axis, ref in enumerate(outs):
+            ref[...] = slot_places(index, ref.shape, axis)
+    for i, block in arriving:
         turn(block, slice(first + i * step, first + (i + 1) * step), kv_ref, qg_ref)
     for copy in passing:
         copy.wait()
@@ -244,12 +248,12 @@
             pltpu.SemaphoreType.DMA,
         ],
         input_output_aliases={2 + i: i for i in range(len(turned))},
-        compiler_params=pltpu.CompilerParams(vmem_limit_bytes=9 * MIB),
+        compiler_params=pltpu.CompilerParams(vmem_limit_bytes=11 * MIB),
         cost_estimate=pl.CostEstimate(
             flops=0, bytes_accessed=4 * (last - first) * kinds * width, transcendentals=0
         ),
         name=name,
-    )(in_hbm(proj_weight), passed, *map(pinned, turned))
+    )(in_hbm(proj_weight), in_hbm(passed), *map(pinned, turned))
 
 
 def gather_rows(x_refs, x_all, at):
@@ -268,15 +272,14 @@
     step, (count, width) = buf.shape[1], k_ref.shape
     depth = kv.shape[0]
     arriving = chunks(first, (depth - first) // step, w_hbm, buf, sem)
+    gather_rows(x_refs, x_all, 0)
+    for i in range(2):
+        total[i] = jnp.dot(
+            x_all[:count, :first],
+            kv[:first, i * width : (i + 1) * width],
+            preferred_element_type=F32,
+        )
     for c, block in arriving:
-        if c == 0:
-            gather_rows(x_refs, x_all, 0)
-            for i in range(2):
-                total[i] = jnp.dot(
-                    x_all[:count, :first],
-                    kv[:first, i * width : (i + 1) * width],
-                    preferred_element_type=F32,
-                )
         at = first + c * step
         turned = turn(block, slice(at, at + step), kv, qg)
         for i in range(2):
@@ -304,7 +307,7 @@
             pltpu.SemaphoreType.DMA((slots,)),
         ],
         input_output_aliases={len(rows) + 1: 0, len(rows) + 2: 1},
-        compiler_params=pltpu.CompilerParams(vmem_limit_bytes=9 * MIB),
+        compiler_params=pltpu.CompilerParams(vmem_limit_bytes=11 * MIB),
         cost_estimate=pl.CostEstimate(
             flops=2 * count * depth * kinds * width,
             bytes_accessed=4 * depth * kinds * width,
@@ -460,34 +463,58 @@
     )(*args)
 
 
-def out_kernel(y_ref, z_ref, w_ref, u_ref, a_ref, b_ref, c_ref, d_ref):
+def out_own_kernel(y_ref, w_ref, o_ref):
+    step = 1024
+    for at in range(0, o_ref.shape[1], step):
+        cols = slice(at, at + step)
+        o_ref[:, cols] = jnp.dot(y_ref[...], w_ref[:, cols], preferred_element_type=F32)
+
+
+def out_own(y, w):
+    rows, depth = y.shape
+    width = w.shape[1]
+    return pl.pallas_call(
+        out_own_kernel,
+        in_specs=[VMEM] * 2,
+        out_specs=VMEM,
+        out_shape=pltpu.VMEM((rows, width), F32),
+        compiler_params=pltpu.CompilerParams(vmem_limit_bytes=4 * MIB),
+        cost_estimate=pl.CostEstimate(
+            flops=2 * rows * depth * width, bytes_accessed=2 * depth * width, transcendentals=0
+        ),
+        name="out_own",
+    )(y, pinned(w))
+
+
+def out_kernel(own_ref, z_ref, u_ref, a_ref, b_ref, c_ref, d_ref):
     rows, width = a_ref.shape
     step = 1024
     for at in range(0, width, step):
         cols = slice(at, at + step)
-        total = jnp.dot(y_ref[...], w_ref[:, cols], preferred_element_type=F32) + jnp.dot(
+        total = own_ref[:, cols] + jnp.dot(
             z_ref[...], u_ref[:, cols], preferred_element_type=F32
         )
         for i, ref in enumerate((a_ref, b_ref, c_ref, d_ref)):
             ref[:, cols] = total[i * rows : (i + 1) * rows].astype(ref.dtype)
 
 
-def out_rows(y, z, w, u):
-    rows, depth = y.shape
-    width = w.shape[1]
+def out_rows(own, z, u):
+    rows, width = own.shape
     send = jax.ShapeDtypeStruct((rows // 4, width), BF16)
     keep = jax.ShapeDtypeStruct((rows // 4, width), F32)
     return pl.pallas_call(
         out_kernel,
-        in_specs=[VMEM] * 4,
+        in_specs=[VMEM] * 3,
         out_specs=[VMEM] * 4,
         out_shape=[send, keep, send, keep],
         compiler_params=pltpu.CompilerParams(vmem_limit_bytes=4 * MIB),
         cost_estimate=pl.CostEstimate(
-            flops=4 * rows * depth * width, bytes_accessed=4 * depth * width, transcendentals=0
+            flops=2 * rows * z.shape[1] * width,
+            bytes_accessed=2 * z.shape[1] * width,
+            transcendentals=0,
         ),
         name="out_rows",
-    )(y, z, pinned(w), pinned(u))
+    )(pinned(own), z, pinned(u))
 
 
 def paired_device(tokens, proj_weight, out_weight, head_gain, decay_rate):
@@ -502,11 +529,11 @@
     second = hop(passed, SECOND)
     beside = hop(tokens, CORE)
     places = [pltpu.VMEM((8 * rows, 1), F32), pltpu.VMEM((1, 8 * rows), F32)]
-    *turned, down, across = prep(cuts[1], cuts[2], proj_weight, turned, passed, places, "prep_b")
+    *turned, down, across = prep(cuts[1], cuts[2], proj_weight, turned, tokens, places, "prep_b")
     (first,) = tie([first], [down])
     far = hop(first, SECOND)
     second_beside = hop(first, CORE)
-    turned = prep(cuts[2], cuts[3], proj_weight, turned, first, [], "prep_c")
+    turned = prep(cuts[2], cuts[3], proj_weight, turned, tokens, [], "prep_c")
     kv, qg, x_all, k0, v0 = project_near(
         [tokens, beside, first, second], cuts[3], proj_weight, *turned
     )
@@ -532,11 +559,12 @@
         decay_rate, down, head_gain[None, :], inner, q, g, *came,
     )
     z = hop(y_other, CORE)
-    a, b, c, d = out_rows(y, z, w_own, w_other)
+    a, b, c, d = out_rows(out_own(y, w_own), z, w_other)
     got_a = hop(a, SECOND)
     got_c = hop(c, SECOND)
     got_b = hop((b + got_a.astype(F32)).astype(BF16), FIRST)
-    return (d + got_c.astype(F32) + got_b.astype(F32)).astype(BF16)
+    summed = lax.optimization_barrier(d + got_c.astype(F32))
+    return (summed + got_b.astype(F32)).astype(BF16)
 
 
 def solution(mesh):

time: 60.3 us -> 58.7 us (0.973)
  local copies, waits for them, and re-layouts: 1.04 us -> 0.02 us
    unnamed x6 -> x8, local copies, waits for them, and re-layouts: 1.04 us -> 0.02 us
    pallas_call x1, Pallas kernels: 4.33 us -> 3.65 us  [project_near(): pl.pallas_call(functools.partial(near_kernel, len(rows), first), in_specs...]
    pallas_call x1 -> x2, Pallas kernels: 1.8 us -> 1.99 us  [the longest x1 1 us: out_rows(): pl.pallas_call(out_kernel, in_specs=[VMEM] * 3, out_specs=[VMEM] * 4, out...]
  transfers between devices with their start and end apart: 15 -> 15, of which waited for: 7 -> 6; matrix products, arithmetic and copies ran while one was open for 0% -> 0% of each run, Pallas kernels for 37% -> 39%
where the time goes in v3:
time: 58.7 us; the launch traced here: 58.5 us
  Pallas kernels  23.7 us (40%)
  waiting for transfers between devices  21.6 us (37%)
  starting transfers between devices  12.1 us (21%)
  other arithmetic  0.95 us (2%)
    ppermute x12, waiting for transfers between devices, hop(): return lax.ppermute(value, 'tp', pairs)  15.3 us
    pallas_call x3, Pallas kernels, prep(): pl.pallas_call(functools.partial(prep_kernel, first, last, bool(turned)),...  9.44 us
    ppermute x12, starting transfers between devices, hop(): return lax.ppermute(value, 'tp', pairs)  8.28 us
    ppermute x3, waiting for transfers between devices, paired_device(): lax.ppermute(states, 'seq', [(i, (i + k) % 4) for i in range(4)])  6.27 us
    ppermute x3, starting transfers between devices, paired_device(): lax.ppermute(states, 'seq', [(i, (i + k) % 4) for i in range(4)])  3.82 us
    pallas_call x1, Pallas kernels, project_near(): pl.pallas_call(functools.partial(near_kernel, len(rows), first), in_specs...  3.65 us
    pallas_call x1, Pallas kernels, gates(): pl.pallas_call(gates_kernel, in_specs=[VMEM, VMEM, HBM], out_specs=[VMEM]...  3.53 us
    pallas_call x1, Pallas kernels, project_far(): pl.pallas_call(functools.partial(far_kernel, len(rows)), in_specs=[SMEM]...  2.69 us
  transfers between devices with their start and end apart: 15, of which 6 were waited for; matrix products, arithmetic and copies ran while one was open for 0% of the time, Pallas kernels for 39%

profile of v3, /device:TPU:9, one launch (start us, length us, event | category | flops | bytes accessed | tf_op | source)
XLA Modules:
  0.0 58.5 jit_solution(475987145427904340)
XLA Ops:
  0.0 0.7 %collective-permute-start.11 = (bf16[512,6144]{1,0:T(8,128)(2,1)}, bf16[512,6144]{1,0:T(8,128)(2,1)S(1)}, u32[]{:S(2)}, u32[]{:S(2)}) collective-permute-start(bf16[512,6144]{1,0:T(8,128)(2,1)} %w_hbm.7), channel_id=1, source_target_pairs={{0,1},{1,0},{2,3},{3,2},{4,5},{5,4},{6,7},{7,6},{8,9},{9,8},{10,11... | collective-permute-start | bytes 18874376 | tf_op jit(solution)/shard_map/ppermute | solution.py:132
  0.7 1.2 %collective-permute-start.1 = (bf16[32,6144]{1,0:T(8,128)(2,1)}, bf16[32,6144]{1,0:T(8,128)(2,1)S(1)}, u32[]{:S(2)}, u32[]{:S(2)}) collective-permute-start(bf16[32,6144]{1,0:T(8,128)(2,1)} %refs_0_.1), channel_id=1, source_target_pairs={{0,2},{1,5},{2,0},{3,7},{4,6},{5,1},{6,4},{7,3},{8,10},{9,13},{10,... | collective-permute-start | bytes 1179656 | tf_op jit(solution)/shard_map/ppermute | solution.py:132
  1.9 3.2 %prep_a.1 = (bf16[6144,1024]{1,0:T(8,128)(2,1)S(1)}, bf16[6144,1024]{1,0:T(8,128)(2,1)S(1)}, bf16[32,6144]{1,0:T(8,128)(2,1)S(1)}) custom-call(bf16[6144,4,512]{2,1,0:T(4,128)(2,1)} %refs_4_.1, bf16[32,6144]{1,0:T(8,128)(2,1)} %refs_0_.1), custom_call_target="tpu_custom_call" | custom-call | bytes 12582912 | tf_op jit(solution)/shard_map/prep_a/pallas_call | solution.py:240
  5.1 1.3 %collective-permute-start.2 = (bf16[32,6144]{1,0:T(8,128)(2,1)S(1)}, bf16[32,6144]{1,0:T(8,128)(2,1)S(1)}, u32[]{:S(2)}, u32[]{:S(2)}) collective-permute-start(bf16[32,6144]{1,0:T(8,128)(2,1)S(1)} %get-tuple-element.36), channel_id=1, source_target_pairs={{0,4},{1,3},{2,6},{3,1},{4,0},{5,7},{6,2},{7,5},{8,12},{9,11},{10,... | collective-permute-start | bytes 1179656 | tf_op jit(solution)/shard_map/ppermute | solution.py:132
  6.4 0.6 %collective-permute-start = (bf16[32,6144]{1,0:T(8,128)(2,1)S(1)}, bf16[32,6144]{1,0:T(8,128)(2,1)S(1)}, u32[]{:S(2)}, u32[]{:S(2)}) collective-permute-start(bf16[32,6144]{1,0:T(8,128)(2,1)S(1)} %copy-done), channel_id=1, source_target_pairs={{0,1},{1,0},{2,3},{3,2},{4,5},{5,4},{6,7},{7,6},{8,9},{9,8},{10,11... | collective-permute-start | bytes 1179656 | tf_op jit(solution)/shard_map/ppermute | solution.py:132
  7.0 3.1 %prep_b.1 = (bf16[6144,1024]{1,0:T(8,128)(2,1)S(1)}, bf16[6144,1024]{1,0:T(8,128)(2,1)S(1)}, f32[256,1]{1,0:T(8,128)S(1)}, f32[1,256]{1,0:T(1,128)S(1)}) custom-call(bf16[6144,4,512]{2,1,0:T(4,128)(2,1)} %refs_4_.1, bf16[32,6144]{1,0:T(8,128)(2,1)} %refs_0_.1, ...), custom_call_target="tpu_custom_call", output_to_operand_aliasing={{0}: (2, {}), {1}: (3, {})} | custom-call | bytes 12582912 | tf_op jit(solution)/shard_map/prep_b/pallas_call | solution.py:240
  10.2 0.3 collective-permute-start.5
  10.5 3.1 %prep_c.1 = (bf16[6144,1024]{1,0:T(8,128)(2,1)S(1)}, bf16[6144,1024]{1,0:T(8,128)(2,1)S(1)}) custom-call(bf16[6144,4,512]{2,1,0:T(4,128)(2,1)} %refs_4_.1, bf16[32,6144]{1,0:T(8,128)(2,1)} %refs_0_.1, bf16[6144,1024]{1,0:T(8,128)(2,1)S(1)} %get-tuple-element.37.refs_0_, ...), custom_call_target="tpu_custom_call", output_to_operand_aliasing={{0}: (2, {}), {1}: (3, {})} | custom-call | bytes 12582912 | tf_op jit(solution)/shard_map/prep_c/pallas_call | solution.py:240
  13.6 1.2 %collective-permute-start.3 = (bf16[32,6144]{1,0:T(8,128)(2,1)S(1)}, bf16[32,6144]{1,0:T(8,128)(2,1)S(1)}, u32[]{:S(2)}, u32[]{:S(2)}) collective-permute-start(bf16[32,6144]{1,0:T(8,128)(2,1)S(1)} %tie.2.refs_2_), channel_id=1, source_target_pairs={{0,1},{1,0},{2,3},{3,2},{4,5},{5,4},{6,7},{7,6},{8,9},{9,8},{10,11... | collective-permute-start | bytes 1179656 | tf_op jit(solution)/shard_map/ppermute | solution.py:132
  14.8 0.1 collective-permute-start.4
  14.9 3.7 %project_near.1 = (bf16[6144,1024]{1,0:T(8,128)(2,1)S(1)}, bf16[6144,1024]{1,0:T(8,128)(2,1)S(1)}, bf16[256,6144]{1,0:T(8,128)(2,1)S(1)}, bf16[128,512]{1,0:T(8,128)(2,1)S(1)}, bf16[128,512]{1,0:T(8,128)(2,1)S(1)}) custom-call(bf16[32,6144]{1,0:T(8,128)(2,1)S(1)} %copy-done.1, ...), custom_call_target="tpu_custom_call", output_to_operand_aliasing={{0}: (5, {}), {1}: (6, {})} | custom-call | flops 3221225472 | bytes 50331648 | tf_op jit(solution)/shard_map/project_near/pallas_call | solution.py:299
  18.6 0.5 collective-permute-start.6
  19.1 1.3 %collective-permute-done.6.refs_3_ = bf16[32,6144]{1,0:T(8,128)(2,1)S(1)} collective-permute-done((bf16[32,6144]{1,0:T(8,128)(2,1)S(1)}, bf16[32,6144]{1,0:T(8,128)(2,1)S(1)}, u32[]{:S(2)}, u32[]{:S(2)}) %collective-permute-start.6) | collective-permute-done | bytes 393248 | tf_op jit(solution)/shard_map/ppermute | solution.py:132
  20.5 2.7 %project_far.1 = (bf16[256,6144]{1,0:T(8,128)(2,1)S(1)}, bf16[128,512]{1,0:T(8,128)(2,1)S(1)}, bf16[128,512]{1,0:T(8,128)(2,1)S(1)}, bf16[4,128,128]{2,1,0:T(8,128)(2,1)S(1)}) custom-call(f32[4]{0:T(128)S(1)} %copy-done.2, f32[256,1]{1,0:T(8,128)S(1)} %get-tuple-element.34.refs_1_.place_ref, ...), custom_call_target="tpu_custom_call", output_to_operand_aliasing={{0}: (5, {})} | custom-call | flops 1610612736 | bytes 12582912 | tf_op jit(solution)/shard_map/project_far/pallas_call | solution.py:347
  23.2 1.4 %collective-permute-start.7 = (bf16[4,128,128]{2,1,0:T(8,128)(2,1)S(1)}, bf16[4,128,128]{2,1,0:T(8,128)(2,1)S(1)}, u32[]{:S(2)}, u32[]{:S(2)}) collective-permute-start(bf16[4,128,128]{2,1,0:T(8,128)(2,1)S(1)} %get-tuple-element.51), channel_id=1, source_target_pairs={{0,8},{8,16},{16,24},{24,0},{1,9},{9,17},{17,25},{25,1},{2,10},{10... | collective-permute-start | bytes 393224 | tf_op jit(solution)/shard_map/ppermute | solution.py:548
  24.5 1.2 %collective-permute-start.8 = (bf16[4,128,128]{2,1,0:T(8,128)(2,1)S(1)}, bf16[4,128,128]{2,1,0:T(8,128)(2,1)S(1)}, u32[]{:S(2)}, u32[]{:S(2)}) collective-permute-start(bf16[4,128,128]{2,1,0:T(8,128)(2,1)S(1)} %get-tuple-element.51), channel_id=1, source_target_pairs={{0,16},{8,24},{16,0},{24,8},{1,17},{9,25},{17,1},{25,9},{2,18},{10... | collective-permute-start | bytes 393224 | tf_op jit(solution)/shard_map/ppermute | solution.py:548
  25.7 1.3 %collective-permute-start.9 = (bf16[4,128,128]{2,1,0:T(8,128)(2,1)S(1)}, bf16[4,128,128]{2,1,0:T(8,128)(2,1)S(1)}, u32[]{:S(2)}, u32[]{:S(2)}) collective-permute-start(bf16[4,128,128]{2,1,0:T(8,128)(2,1)S(1)} %get-tuple-element.51), channel_id=1, source_target_pairs={{0,24},{8,0},{16,8},{24,16},{1,25},{9,1},{17,9},{25,17},{2,26},{10... | collective-permute-start | bytes 393224 | tf_op jit(solution)/shard_map/ppermute | solution.py:548
  27.0 3.5 %gates.1 = (bf16[256,512]{1,0:T(8,128)(2,1)S(1)}, f32[256,512]{1,0:T(8,128)S(1)}, bf16[512,6144]{1,0:T(8,128)(2,1)S(1)}) custom-call(bf16[256,6144]{1,0:T(8,128)(2,1)S(1)} %get-tuple-element.45.x_all, bf16[6144,1024]{1,0:T(8,128)(2,1)S(1)} %get-tuple-element.46.qg, bf16[512,6144]{1,0:T(8,128)(2,1)} %w_hbm.7), custom_call_target="tpu_custom_call" | custom-call | flops 3221225472 | bytes 25165824 | tf_op jit(solution)/shard_map/gates/pallas_call | solution.py:392
  30.6 1.2 %inner.1.in_ref = f32[256,512]{1,0:T(8,128)S(1)} custom-call(f32[4]{0:T(128)S(1)} %copy-done.2, f32[256,1]{1,0:T(8,128)S(1)} %get-tuple-element.34.refs_1_.place_ref, f32[1,256]{1,0:T(1,128)S(1)} %get-tuple-element.35.across_ref, bf16[256,512]{1,0:T(8,128)(2,1)S(1)} %get-tuple-element.47.q_ref, bf16[128,512]{1,0:T(8,128)(2,1)S(1)} %get-tuple-element.41.refs_1_.k0, ...), custom_call_target="tpu_custom_call" | custom-call | tf_op jit(solution)/shard_map/inner/pallas_call | solution.py:456
  31.8 3.7 %collective-permute-done.8.s2 = bf16[4,128,128]{2,1,0:T(8,128)(2,1)S(1)} collective-permute-done((bf16[4,128,128]{2,1,0:T(8,128)(2,1)S(1)}, bf16[4,128,128]{2,1,0:T(8,128)(2,1)S(1)}, u32[]{:S(2)}, u32[]{:S(2)}) %collective-permute-start.8) | collective-permute-done | bytes 131104 | tf_op jit(solution)/shard_map/ppermute | solution.py:548
  35.5 2.6 %collective-permute-done.9.s3 = bf16[4,128,128]{2,1,0:T(8,128)(2,1)S(1)} collective-permute-done((bf16[4,128,128]{2,1,0:T(8,128)(2,1)S(1)}, bf16[4,128,128]{2,1,0:T(8,128)(2,1)S(1)}, u32[]{:S(2)}, u32[]{:S(2)}) %collective-permute-start.9) | collective-permute-done | bytes 131104 | tf_op jit(solution)/shard_map/ppermute | solution.py:548
  38.1 1.1 %finish.1 = (bf16[128,512]{1,0:T(8,128)(2,1)S(1)}, bf16[128,512]{1,0:T(8,128)(2,1)S(1)}) custom-call(f32[4]{0:T(128)S(1)} %copy-done.2, f32[256,1]{1,0:T(8,128)S(1)} %get-tuple-element.34.refs_1_.place_ref, f32[1,512]{1,0:T(1,128)S(1)} %bitcast.1, f32[256,512]{1,0:T(8,128)S(1)} %inner.1.in_ref, bf16[256,512]{1,0:T(8,128)(2,1)S(1)} %get-tuple-element.47.q_ref, ...), custom_call_target="tpu_custom_call" | custom-call | tf_op jit(solution)/shard_map/finish/pallas_call | solution.py:456
  39.2 0.6 collective-permute-start.10
  39.8 1.0 %out_own.1.own_ref = f32[128,6144]{1,0:T(8,128)S(1)} custom-call(bf16[128,512]{1,0:T(8,128)(2,1)S(1)} %get-tuple-element.52.y_ref, bf16[512,6144]{1,0:T(8,128)(2,1)S(1)} %get-tuple-element.53.w_ref), custom_call_target="tpu_custom_call" | custom-call | flops 805306368 | bytes 6291456 | tf_op jit(solution)/shard_map/out_own/pallas_call | solution.py:476
  40.8 1.0 %out_rows.1 = (bf16[32,6144]{1,0:T(8,128)(2,1)S(1)}, f32[32,6144]{1,0:T(8,128)S(1)}, bf16[32,6144]{1,0:T(8,128)(2,1)S(1)}, f32[32,6144]{1,0:T(8,128)S(1)}) custom-call(f32[128,6144]{1,0:T(8,128)S(1)} %out_own.1.own_ref, bf16[128,512]{1,0:T(8,128)(2,1)S(1)} %collective-permute-done.10.z_ref, bf16[512,6144]{1,0:T(8,128)(2,1)S(1)} %collective-permute-done.11.u_ref), custom_call_target="tpu_custom_call" | custom-call | flops 805306368 | bytes 6291456 | tf_op jit(solution)/shard_map/out_rows/pallas_call | solution.py:505
  41.8 1.1 %collective-permute-start.13 = (bf16[32,6144]{1,0:T(8,128)(2,1)S(1)}, bf16[32,6144]{1,0:T(8,128)(2,1)S(1)}, u32[]{:S(2)}, u32[]{:S(2)}) collective-permute-start(bf16[32,6144]{1,0:T(8,128)(2,1)S(1)} %get-tuple-element.58), channel_id=1, source_target_pairs={{0,4},{1,3},{2,6},{3,1},{4,0},{5,7},{6,2},{7,5},{8,12},{9,11},{10,... | collective-permute-start | bytes 1179656 | tf_op jit(solution)/shard_map/ppermute | solution.py:132
  42.9 0.4 collective-permute-start.12
  43.3 5.5 %collective-permute-done.13 = bf16[32,6144]{1,0:T(8,128)(2,1)S(1)} collective-permute-done((bf16[32,6144]{1,0:T(8,128)(2,1)S(1)}, bf16[32,6144]{1,0:T(8,128)(2,1)S(1)}, u32[]{:S(2)}, u32[]{:S(2)}) %collective-permute-start.13) | collective-permute-done | bytes 393248 | tf_op jit(solution)/shard_map/ppermute | solution.py:132
  48.9 0.2 collective-permute-start.14
  49.1 3.9 %collective-permute-done.12 = bf16[32,6144]{1,0:T(8,128)(2,1)S(1)} collective-permute-done((bf16[32,6144]{1,0:T(8,128)(2,1)S(1)}, bf16[32,6144]{1,0:T(8,128)(2,1)S(1)}, u32[]{:S(2)}, u32[]{:S(2)}) %collective-permute-start.12) | collective-permute-done | bytes 393248 | tf_op jit(solution)/shard_map/ppermute | solution.py:132
  53.1 4.6 %collective-permute-done.14 = bf16[32,6144]{1,0:T(8,128)(2,1)S(1)} collective-permute-done((bf16[32,6144]{1,0:T(8,128)(2,1)S(1)}, bf16[32,6144]{1,0:T(8,128)(2,1)S(1)}, u32[]{:S(2)}, u32[]{:S(2)}) %collective-permute-start.14) | collective-permute-done | bytes 393248 | tf_op jit(solution)/shard_map/ppermute | solution.py:132
  57.7 0.8 %add_convert_fusion = bf16[32,6144]{1,0:T(8,128)(2,1)} fusion(f32[32,6144]{1,0:T(8,128)S(1)} %convert_add_fusion, bf16[32,6144]{1,0:T(8,128)(2,1)S(1)} %collective-permute-done.14), kind=kLoop, calls=%fused_computation | loop fusion | flops 589824 | bytes 1572864 | tf_op jit(solution)/shard_map/convert_element_type | solution.py:567
  (21 shorter events, 0.2 us)
Async XLA Ops:
  0.0 6.4 %copy-start = (bf16[32,6144]{1,0:T(8,128)(2,1)S(1)}, bf16[32,6144]{1,0:T(8,128)(2,1)}, u32[]{:S(2)}) copy-start(bf16[32,6144]{1,0:T(8,128)(2,1)} %refs_0_.1) | copy-start | bytes 1179652
  0.0 40.8 %collective-permute-start.11 = (bf16[512,6144]{1,0:T(8,128)(2,1)}, bf16[512,6144]{1,0:T(8,128)(2,1)S(1)}, u32[]{:S(2)}, u32[]{:S(2)}) collective-permute-start(bf16[512,6144]{1,0:T(8,128)(2,1)} %w_hbm.7), channel_id=1, source_target_pairs={{0,1},{1,0},{2,3},{3,2},{4,5},{5,4},{6,7},{7,6},{8,9},{9,8},{10,11... | collective-permute-start | bytes 18874376 | tf_op jit(solution)/shard_map/ppermute | solution.py:132
  0.7 9.5 %collective-permute-start.1 = (bf16[32,6144]{1,0:T(8,128)(2,1)}, bf16[32,6144]{1,0:T(8,128)(2,1)S(1)}, u32[]{:S(2)}, u32[]{:S(2)}) collective-permute-start(bf16[32,6144]{1,0:T(8,128)(2,1)} %refs_0_.1), channel_id=1, source_target_pairs={{0,2},{1,5},{2,0},{3,7},{4,6},{5,1},{6,4},{7,3},{8,10},{9,13},{10,... | collective-permute-start | bytes 1179656 | tf_op jit(solution)/shard_map/ppermute | solution.py:132
  5.1 9.7 %collective-permute-start.2 = (bf16[32,6144]{1,0:T(8,128)(2,1)S(1)}, bf16[32,6144]{1,0:T(8,128)(2,1)S(1)}, u32[]{:S(2)}, u32[]{:S(2)}) collective-permute-start(bf16[32,6144]{1,0:T(8,128)(2,1)S(1)} %get-tuple-element.36), channel_id=1, source_target_pairs={{0,4},{1,3},{2,6},{3,1},{4,0},{5,7},{6,2},{7,5},{8,12},{9,11},{10,... | collective-permute-start | bytes 1179656 | tf_op jit(solution)/shard_map/ppermute | solution.py:132
  6.4 8.5 %collective-permute-start = (bf16[32,6144]{1,0:T(8,128)(2,1)S(1)}, bf16[32,6144]{1,0:T(8,128)(2,1)S(1)}, u32[]{:S(2)}, u32[]{:S(2)}) collective-permute-start(bf16[32,6144]{1,0:T(8,128)(2,1)S(1)} %copy-done), channel_id=1, source_target_pairs={{0,1},{1,0},{2,3},{3,2},{4,5},{5,4},{6,7},{7,6},{8,9},{9,8},{10,11... | collective-permute-start | bytes 1179656 | tf_op jit(solution)/shard_map/ppermute | solution.py:132
  10.2 8.4 %collective-permute-start.5 = (bf16[32,6144]{1,0:T(8,128)(2,1)S(1)}, bf16[32,6144]{1,0:T(8,128)(2,1)S(1)}, u32[]{:S(2)}, u32[]{:S(2)}) collective-permute-start(bf16[32,6144]{1,0:T(8,128)(2,1)S(1)} %tie.2.refs_2_), channel_id=1, source_target_pairs={{0,4},{1,3},{2,6},{3,1},{4,0},{5,7},{6,2},{7,5},{8,12},{9,11},{10,... | collective-permute-start | bytes 1179656 | tf_op jit(solution)/shard_map/ppermute | solution.py:132
  10.5 4.5 %copy-start.1 = (bf16[32,6144]{1,0:T(8,128)(2,1)S(1)}, bf16[32,6144]{1,0:T(8,128)(2,1)}, u32[]{:S(2)}) copy-start(bf16[32,6144]{1,0:T(8,128)(2,1)} %refs_0_.1) | copy-start | bytes 1179652
  13.6 5.5 %collective-permute-start.3 = (bf16[32,6144]{1,0:T(8,128)(2,1)S(1)}, bf16[32,6144]{1,0:T(8,128)(2,1)S(1)}, u32[]{:S(2)}, u32[]{:S(2)}) collective-permute-start(bf16[32,6144]{1,0:T(8,128)(2,1)S(1)} %tie.2.refs_2_), channel_id=1, source_target_pairs={{0,1},{1,0},{2,3},{3,2},{4,5},{5,4},{6,7},{7,6},{8,9},{9,8},{10,11... | collective-permute-start | bytes 1179656 | tf_op jit(solution)/shard_map/ppermute | solution.py:132
  14.8 4.3 %collective-permute-start.4 = (bf16[32,6144]{1,0:T(8,128)(2,1)S(1)}, bf16[32,6144]{1,0:T(8,128)(2,1)S(1)}, u32[]{:S(2)}, u32[]{:S(2)}) collective-permute-start(bf16[32,6144]{1,0:T(8,128)(2,1)S(1)} %collective-permute-done.2.refs_3_), channel_id=1, source_target_pairs={{0,1},{1,0},{2,3},{3,2},{4,5},{5,4},{6,7},{7,6},{8,9},{9,8},{10,11... | collective-permute-start | bytes 1179656 | tf_op jit(solution)/shard_map/ppermute | solution.py:132
  14.9 5.5 %copy-start.2 = (f32[4]{0:T(128)S(1)}, f32[4]{0:T(128)}, u32[]{:S(2)}) copy-start(f32[4]{0:T(128)} %rate_ref.5) | copy-start | bytes 52
  18.6 1.9 %collective-permute-start.6 = (bf16[32,6144]{1,0:T(8,128)(2,1)S(1)}, bf16[32,6144]{1,0:T(8,128)(2,1)S(1)}, u32[]{:S(2)}, u32[]{:S(2)}) collective-permute-start(bf16[32,6144]{1,0:T(8,128)(2,1)S(1)} %tie.3.refs_2_), channel_id=1, source_target_pairs={{0,1},{1,0},{2,3},{3,2},{4,5},{5,4},{6,7},{7,6},{8,9},{9,8},{10,11... | collective-permute-start | bytes 1179656 | tf_op jit(solution)/shard_map/ppermute | solution.py:132
  23.2 14.9 %copy-start.3 = (f32[512]{0:T(512)S(1)}, f32[512]{0:T(512)}, u32[]{:S(2)}) copy-start(f32[512]{0:T(512)} %param.8) | copy-start | bytes 6148
  23.2 8.6 %collective-permute-start.7 = (bf16[4,128,128]{2,1,0:T(8,128)(2,1)S(1)}, bf16[4,128,128]{2,1,0:T(8,128)(2,1)S(1)}, u32[]{:S(2)}, u32[]{:S(2)}) collective-permute-start(bf16[4,128,128]{2,1,0:T(8,128)(2,1)S(1)} %get-tuple-element.51), channel_id=1, source_target_pairs={{0,8},{8,16},{16,24},{24,0},{1,9},{9,17},{17,25},{25,1},{2,10},{10... | collective-permute-start | bytes 393224 | tf_op jit(solution)/shard_map/ppermute | solution.py:548
  24.5 10.9 %collective-permute-start.8 = (bf16[4,128,128]{2,1,0:T(8,128)(2,1)S(1)}, bf16[4,128,128]{2,1,0:T(8,128)(2,1)S(1)}, u32[]{:S(2)}, u32[]{:S(2)}) collective-permute-start(bf16[4,128,128]{2,1,0:T(8,128)(2,1)S(1)} %get-tuple-element.51), channel_id=1, source_target_pairs={{0,16},{8,24},{16,0},{24,8},{1,17},{9,25},{17,1},{25,9},{2,18},{10... | collective-permute-start | bytes 393224 | tf_op jit(solution)/shard_map/ppermute | solution.py:548
  25.7 12.4 %collective-permute-start.9 = (bf16[4,128,128]{2,1,0:T(8,128)(2,1)S(1)}, bf16[4,128,128]{2,1,0:T(8,128)(2,1)S(1)}, u32[]{:S(2)}, u32[]{:S(2)}) collective-permute-start(bf16[4,128,128]{2,1,0:T(8,128)(2,1)S(1)} %get-tuple-element.51), channel_id=1, source_target_pairs={{0,24},{8,0},{16,8},{24,16},{1,25},{9,1},{17,9},{25,17},{2,26},{10... | collective-permute-start | bytes 393224 | tf_op jit(solution)/shard_map/ppermute | solution.py:548
  39.2 1.6 %collective-permute-start.10 = (bf16[128,512]{1,0:T(8,128)(2,1)S(1)}, bf16[128,512]{1,0:T(8,128)(2,1)S(1)}, u32[]{:S(2)}, u32[]{:S(2)}) collective-permute-start(bf16[128,512]{1,0:T(8,128)(2,1)S(1)} %get-tuple-element.54), channel_id=1, source_target_pairs={{0,1},{1,0},{2,3},{3,2},{4,5},{5,4},{6,7},{7,6},{8,9},{9,8},{10,11... | collective-permute-start | bytes 393224 | tf_op jit(solution)/shard_map/ppermute | solution.py:132
  41.8 7.0 %collective-permute-start.13 = (bf16[32,6144]{1,0:T(8,128)(2,1)S(1)}, bf16[32,6144]{1,0:T(8,128)(2,1)S(1)}, u32[]{:S(2)}, u32[]{:S(2)}) collective-permute-start(bf16[32,6144]{1,0:T(8,128)(2,1)S(1)} %get-tuple-element.58), channel_id=1, source_target_pairs={{0,4},{1,3},{2,6},{3,1},{4,0},{5,7},{6,2},{7,5},{8,12},{9,11},{10,... | collective-permute-start | bytes 1179656 | tf_op jit(solution)/shard_map/ppermute | solution.py:132
  42.9 10.1 %collective-permute-start.12 = (bf16[32,6144]{1,0:T(8,128)(2,1)S(1)}, bf16[32,6144]{1,0:T(8,128)(2,1)S(1)}, u32[]{:S(2)}, u32[]{:S(2)}) collective-permute-start(bf16[32,6144]{1,0:T(8,128)(2,1)S(1)} %get-tuple-element.56), channel_id=1, source_target_pairs={{0,4},{1,3},{2,6},{3,1},{4,0},{5,7},{6,2},{7,5},{8,12},{9,11},{10,... | collective-permute-start | bytes 1179656 | tf_op jit(solution)/shard_map/ppermute | solution.py:132
  48.9 8.8 %collective-permute-start.14 = (bf16[32,6144]{1,0:T(8,128)(2,1)S(1)}, bf16[32,6144]{1,0:T(8,128)(2,1)S(1)}, u32[]{:S(2)}, u32[]{:S(2)}) collective-permute-start(bf16[32,6144]{1,0:T(8,128)(2,1)S(1)} %add_convert_fusion.1), channel_id=1, source_target_pairs={{0,2},{1,5},{2,0},{3,7},{4,6},{5,1},{6,4},{7,3},{8,10},{9,13},{10,... | collective-permute-start | bytes 1179656 | tf_op jit(solution)/shard_map/ppermute | solution.py:132

commit v4 on v3

--- a/solution.py
+++ b/solution.py
@@ -218,14 +218,14 @@
     buf, sem, pass_sem = refs[-3:]
     step = buf.shape[1]
     passing = []
-    if len(outs) == 1:
+    if outs:
         passing = [pltpu.make_async_copy(pass_ref, outs[0], pass_sem)]
     for copy in passing:
         copy.start()
     arriving = chunks(first, (last - first) // step, w_hbm, buf, sem)
-    if len(outs) == 2:
+    if outs:
         index = lax.axis_index("tp")
-        for axis, ref in enumerate(outs):
+        for axis, ref in enumerate(outs[1:]):
             ref[...] = slot_places(index, ref.shape, axis)
     for i, block in arriving:
         turn(block, slice(first + i * step, first + (i + 1) * step), kv_ref, qg_ref)
@@ -521,21 +521,23 @@
     rows = tokens.shape[0]
     heads = decay_rate.shape[0]
 
-    cuts = [proj_weight.shape[0] * i // 4 for i in range(5)]
+    cuts = [proj_weight.shape[0] // STEP * part // 8 * STEP for part in (0, 3, 6)]
     w_other = hop(out_weight, CORE)
     first = hop(tokens, FIRST)
-    copied = jax.ShapeDtypeStruct(tokens.shape, tokens.dtype)
-    *turned, passed = prep(cuts[0], cuts[1], proj_weight, [], tokens, [copied], "prep_a")
+    outs = [
+        jax.ShapeDtypeStruct(tokens.shape, tokens.dtype),
+        pltpu.VMEM((8 * rows, 1), F32),
+        pltpu.VMEM((1, 8 * rows), F32),
+    ]
+    *turned, passed, down, across = prep(0, cuts[1], proj_weight, [], tokens, outs, "prep_a")
     second = hop(passed, SECOND)
     beside = hop(tokens, CORE)
-    places = [pltpu.VMEM((8 * rows, 1), F32), pltpu.VMEM((1, 8 * rows), F32)]
-    *turned, down, across = prep(cuts[1], cuts[2], proj_weight, turned, tokens, places, "prep_b")
     (first,) = tie([first], [down])
     far = hop(first, SECOND)
     second_beside = hop(first, CORE)
-    turned = prep(cuts[2], cuts[3], proj_weight, turned, tokens, [], "prep_c")
+    turned = prep(cuts[1], cuts[2], proj_weight, turned, tokens, [], "prep_b")
     kv, qg, x_all, k0, v0 = project_near(
-        [tokens, beside, first, second], cuts[3], proj_weight, *turned
+        [passed, beside, first, second], cuts[2], proj_weight, *turned
     )
     first_beside = hop(second, CORE)
     (far,) = tie([far], [k0])
@@ -545,8 +547,9 @@
     )
 
     came = [
-        lax.ppermute(states, "seq", [(i, (i + k) % 4) for i in range(4)]) for k in (1, 2, 3)
+        lax.ppermute(states, "seq", [(i, (i + k) % 4) for i in range(4)]) for k in (1, 2)
     ]
+    came.append(lax.ppermute(states, "seq", [(0, 3)]))
     q, g, w_own = gates(x_all, qg, out_weight)
     full = jax.ShapeDtypeStruct((8 * rows, heads * HD), F32)
     inner = small(inner_kernel, 1, full, "inner", decay_rate, down, across, q, k0, k1, v0, v1)

time: 58.7 us -> 57.8 us (0.985)
  the two profiles are of different devices: /device:TPU:9 before, /device:TPU:0 now
where the time goes in v4:
time: 57.8 us; the launch traced here: 57.6 us
  Pallas kernels  22.8 us (39%)
  starting transfers between devices  18.8 us (33%)
  waiting for transfers between devices  14.9 us (26%)
  other arithmetic  0.95 us (2%)
    ppermute x12, waiting for transfers between devices, hop(): return lax.ppermute(value, 'tp', pairs)  14.1 us
    ppermute x12, starting transfers between devices, hop(): return lax.ppermute(value, 'tp', pairs)  11.4 us
    pallas_call x2, Pallas kernels, prep(): pl.pallas_call(functools.partial(prep_kernel, first, last, bool(turned)),...  8.58 us
    ppermute x2, starting transfers between devices, paired_device(): lax.ppermute(states, 'seq', [(i, (i + k) % 4) for i in range(4)])  3.99 us
    pallas_call x1, Pallas kernels, project_near(): pl.pallas_call(functools.partial(near_kernel, len(rows), first), in_specs...  3.65 us
    pallas_call x1, Pallas kernels, gates(): pl.pallas_call(gates_kernel, in_specs=[VMEM, VMEM, HBM], out_specs=[VMEM]...  3.54 us
    ppermute x1, starting transfers between devices, paired_device(): came.append(lax.ppermute(states, 'seq', [(0, 3)]))  3.43 us
    pallas_call x1, Pallas kernels, project_far(): pl.pallas_call(functools.partial(far_kernel, len(rows)), in_specs=[SMEM]...  2.68 us
  transfers between devices with their start and end apart: 15, of which 6 were waited for; matrix products, arithmetic and copies ran while one was open for 0% of the time, Pallas kernels for 38%

profile of v4, /device:TPU:0, one launch (start us, length us, event | category | flops | bytes accessed | tf_op | source)
XLA Modules:
  0.0 57.6 jit_solution(13450543282155480909)
XLA Ops:
  0.0 0.5 collective-permute-start.11
  0.5 2.5 %collective-permute-start.1 = (bf16[32,6144]{1,0:T(8,128)(2,1)}, bf16[32,6144]{1,0:T(8,128)(2,1)S(1)}, u32[]{:S(2)}, u32[]{:S(2)}) collective-permute-start(bf16[32,6144]{1,0:T(8,128)(2,1)} %pass_ref.3), channel_id=1, source_target_pairs={{0,2},{1,5},{2,0},{3,7},{4,6},{5,1},{6,4},{7,3},{8,10},{9,13},{10,... | collective-permute-start | bytes 1179656 | tf_op jit(solution)/shard_map/ppermute | solution.py:132
  3.0 4.3 %prep_a.1 = (bf16[6144,1024]{1,0:T(8,128)(2,1)S(1)}, bf16[6144,1024]{1,0:T(8,128)(2,1)S(1)}, bf16[32,6144]{1,0:T(8,128)(2,1)S(1)}, f32[256,1]{1,0:T(8,128)S(1)}, f32[1,256]{1,0:T(1,128)S(1)}) custom-call(bf16[6144,4,512]{2,1,0:T(4,128)(2,1)} %refs_4_.1, bf16[32,6144]{1,0:T(8,128)(2,1)} %pass_ref.3), custom_call_target="tpu_custom_call" | custom-call | bytes 18874368 | tf_op jit(solution)/shard_map/prep_a/pallas_call | solution.py:240
  7.4 1.6 %collective-permute-start.2 = (bf16[32,6144]{1,0:T(8,128)(2,1)S(1)}, bf16[32,6144]{1,0:T(8,128)(2,1)S(1)}, u32[]{:S(2)}, u32[]{:S(2)}) collective-permute-start(bf16[32,6144]{1,0:T(8,128)(2,1)S(1)} %get-tuple-element.32.refs_0_), channel_id=1, source_target_pairs={{0,4},{1,3},{2,6},{3,1},{4,0},{5,7},{6,2},{7,5},{8,12},{9,11},{10,... | collective-permute-start | bytes 1179656 | tf_op jit(solution)/shard_map/ppermute | solution.py:132
  9.0 2.5 %collective-permute-start.5 = (bf16[32,6144]{1,0:T(8,128)(2,1)S(1)}, bf16[32,6144]{1,0:T(8,128)(2,1)S(1)}, u32[]{:S(2)}, u32[]{:S(2)}) collective-permute-start(bf16[32,6144]{1,0:T(8,128)(2,1)S(1)} %tie.2.refs_2_), channel_id=1, source_target_pairs={{0,4},{1,3},{2,6},{3,1},{4,0},{5,7},{6,2},{7,5},{8,12},{9,11},{10,... | collective-permute-start | bytes 1179656 | tf_op jit(solution)/shard_map/ppermute | solution.py:132
  11.5 4.2 %prep_b.1 = (bf16[6144,1024]{1,0:T(8,128)(2,1)S(1)}, bf16[6144,1024]{1,0:T(8,128)(2,1)S(1)}) custom-call(bf16[6144,4,512]{2,1,0:T(4,128)(2,1)} %refs_4_.1, bf16[32,6144]{1,0:T(8,128)(2,1)} %pass_ref.3, bf16[6144,1024]{1,0:T(8,128)(2,1)S(1)} %get-tuple-element.33.refs_0_, ...), custom_call_target="tpu_custom_call", output_to_operand_aliasing={{0}: (2, {}), {1}: (3, {})} | custom-call | bytes 18874368 | tf_op jit(solution)/shard_map/prep_b/pallas_call | solution.py:240
  15.7 0.1 collective-permute-start.3
  15.8 0.5 collective-permute-start.4
  16.3 3.7 %project_near.1 = (bf16[6144,1024]{1,0:T(8,128)(2,1)S(1)}, bf16[6144,1024]{1,0:T(8,128)(2,1)S(1)}, bf16[256,6144]{1,0:T(8,128)(2,1)S(1)}, bf16[128,512]{1,0:T(8,128)(2,1)S(1)}, bf16[128,512]{1,0:T(8,128)(2,1)S(1)}) custom-call(bf16[32,6144]{1,0:T(8,128)(2,1)S(1)} %get-tuple-element.32.refs_0_, ...), custom_call_target="tpu_custom_call", output_to_operand_aliasing={{0}: (5, {}), {1}: (6, {})} | custom-call | flops 3221225472 | bytes 50331648 | tf_op jit(solution)/shard_map/project_near/pallas_call | solution.py:299
  20.0 0.1 collective-permute-start.6
  20.1 1.6 %collective-permute-done.6.refs_3_ = bf16[32,6144]{1,0:T(8,128)(2,1)S(1)} collective-permute-done((bf16[32,6144]{1,0:T(8,128)(2,1)S(1)}, bf16[32,6144]{1,0:T(8,128)(2,1)S(1)}, u32[]{:S(2)}, u32[]{:S(2)}) %collective-permute-start.6) | collective-permute-done | bytes 393248 | tf_op jit(solution)/shard_map/ppermute | solution.py:132
  21.8 2.7 %project_far.1 = (bf16[256,6144]{1,0:T(8,128)(2,1)S(1)}, bf16[128,512]{1,0:T(8,128)(2,1)S(1)}, bf16[128,512]{1,0:T(8,128)(2,1)S(1)}, bf16[4,128,128]{2,1,0:T(8,128)(2,1)S(1)}) custom-call(f32[4]{0:T(128)S(1)} %copy-done, f32[256,1]{1,0:T(8,128)S(1)} %get-tuple-element.30.refs_1_.place_ref, ...), custom_call_target="tpu_custom_call", output_to_operand_aliasing={{0}: (5, {})} | custom-call | flops 1610612736 | bytes 12582912 | tf_op jit(solution)/shard_map/project_far/pallas_call | solution.py:347
  24.5 1.4 %collective-permute-start.7 = (bf16[4,128,128]{2,1,0:T(8,128)(2,1)S(1)}, bf16[4,128,128]{2,1,0:T(8,128)(2,1)S(1)}, u32[]{:S(2)}, u32[]{:S(2)}) collective-permute-start(bf16[4,128,128]{2,1,0:T(8,128)(2,1)S(1)} %get-tuple-element.47), channel_id=1, source_target_pairs={{0,8},{8,16},{16,24},{24,0},{1,9},{9,17},{17,25},{25,1},{2,10},{10... | collective-permute-start | bytes 393224 | tf_op jit(solution)/shard_map/ppermute | solution.py:550
  25.9 2.6 %collective-permute-start.8 = (bf16[4,128,128]{2,1,0:T(8,128)(2,1)S(1)}, bf16[4,128,128]{2,1,0:T(8,128)(2,1)S(1)}, u32[]{:S(2)}, u32[]{:S(2)}) collective-permute-start(bf16[4,128,128]{2,1,0:T(8,128)(2,1)S(1)} %get-tuple-element.47), channel_id=1, source_target_pairs={{0,16},{8,24},{16,0},{24,8},{1,17},{9,25},{17,1},{25,9},{2,18},{10... | collective-permute-start | bytes 393224 | tf_op jit(solution)/shard_map/ppermute | solution.py:550
  28.5 3.4 %collective-permute-start.9 = (bf16[4,128,128]{2,1,0:T(8,128)(2,1)S(1)}, bf16[4,128,128]{2,1,0:T(8,128)(2,1)S(1)}, u32[]{:S(2)}, u32[]{:S(2)}) collective-permute-start(bf16[4,128,128]{2,1,0:T(8,128)(2,1)S(1)} %get-tuple-element.47), channel_id=1, source_target_pairs={{0,24},{1,25},{2,26},{3,27},{4,28},{5,29},{6,30},{7,31}} | collective-permute-start | bytes 393224 | tf_op jit(solution)/shard_map/ppermute | solution.py:552
  31.9 3.5 %gates.1 = (bf16[256,512]{1,0:T(8,128)(2,1)S(1)}, f32[256,512]{1,0:T(8,128)S(1)}, bf16[512,6144]{1,0:T(8,128)(2,1)S(1)}) custom-call(bf16[256,6144]{1,0:T(8,128)(2,1)S(1)} %get-tuple-element.41.x_all, bf16[6144,1024]{1,0:T(8,128)(2,1)S(1)} %get-tuple-element.42.qg, bf16[512,6144]{1,0:T(8,128)(2,1)} %w_hbm.5), custom_call_target="tpu_custom_call" | custom-call | flops 3221225472 | bytes 25165824 | tf_op jit(solution)/shard_map/gates/pallas_call | solution.py:392
  35.5 1.2 %inner.1.in_ref = f32[256,512]{1,0:T(8,128)S(1)} custom-call(f32[4]{0:T(128)S(1)} %copy-done, f32[256,1]{1,0:T(8,128)S(1)} %get-tuple-element.30.refs_1_.place_ref, f32[1,256]{1,0:T(1,128)S(1)} %get-tuple-element.31.across_ref, bf16[256,512]{1,0:T(8,128)(2,1)S(1)} %get-tuple-element.43.q_ref, bf16[128,512]{1,0:T(8,128)(2,1)S(1)} %get-tuple-element.37.refs_1_.k0, ...), custom_call_target="tpu_custom_call" | custom-call | tf_op jit(solution)/shard_map/inner/pallas_call | solution.py:456
  36.7 0.8 %collective-permute-done.8.s2 = bf16[4,128,128]{2,1,0:T(8,128)(2,1)S(1)} collective-permute-done((bf16[4,128,128]{2,1,0:T(8,128)(2,1)S(1)}, bf16[4,128,128]{2,1,0:T(8,128)(2,1)S(1)}, u32[]{:S(2)}, u32[]{:S(2)}) %collective-permute-start.8) | collective-permute-done | bytes 131104 | tf_op jit(solution)/shard_map/ppermute | solution.py:550
  37.5 1.1 %finish.1 = (bf16[128,512]{1,0:T(8,128)(2,1)S(1)}, bf16[128,512]{1,0:T(8,128)(2,1)S(1)}) custom-call(f32[4]{0:T(128)S(1)} %copy-done, f32[256,1]{1,0:T(8,128)S(1)} %get-tuple-element.30.refs_1_.place_ref, f32[1,512]{1,0:T(1,128)S(1)} %bitcast.1, f32[256,512]{1,0:T(8,128)S(1)} %inner.1.in_ref, bf16[256,512]{1,0:T(8,128)(2,1)S(1)} %get-tuple-element.43.q_ref, ...), custom_call_target="tpu_custom_call" | custom-call | tf_op jit(solution)/shard_map/finish/pallas_call | solution.py:456
  38.6 0.1 collective-permute-start.10
  38.7 1.0 %out_own.1.own_ref = f32[128,6144]{1,0:T(8,128)S(1)} custom-call(bf16[128,512]{1,0:T(8,128)(2,1)S(1)} %get-tuple-element.48.y_ref, bf16[512,6144]{1,0:T(8,128)(2,1)S(1)} %get-tuple-element.49.w_ref), custom_call_target="tpu_custom_call" | custom-call | flops 805306368 | bytes 6291456 | tf_op jit(solution)/shard_map/out_own/pallas_call | solution.py:476
  39.7 0.3 collective-permute-done.10.z_ref
  40.0 1.0 %out_rows.1 = (bf16[32,6144]{1,0:T(8,128)(2,1)S(1)}, f32[32,6144]{1,0:T(8,128)S(1)}, bf16[32,6144]{1,0:T(8,128)(2,1)S(1)}, f32[32,6144]{1,0:T(8,128)S(1)}) custom-call(f32[128,6144]{1,0:T(8,128)S(1)} %out_own.1.own_ref, bf16[128,512]{1,0:T(8,128)(2,1)S(1)} %collective-permute-done.10.z_ref, bf16[512,6144]{1,0:T(8,128)(2,1)S(1)} %collective-permute-done.11.u_ref), custom_call_target="tpu_custom_call" | custom-call | flops 805306368 | bytes 6291456 | tf_op jit(solution)/shard_map/out_rows/pallas_call | solution.py:505
  41.0 1.0 %collective-permute-start.13 = (bf16[32,6144]{1,0:T(8,128)(2,1)S(1)}, bf16[32,6144]{1,0:T(8,128)(2,1)S(1)}, u32[]{:S(2)}, u32[]{:S(2)}) collective-permute-start(bf16[32,6144]{1,0:T(8,128)(2,1)S(1)} %get-tuple-element.54), channel_id=1, source_target_pairs={{0,4},{1,3},{2,6},{3,1},{4,0},{5,7},{6,2},{7,5},{8,12},{9,11},{10,... | collective-permute-start | bytes 1179656 | tf_op jit(solution)/shard_map/ppermute | solution.py:132
  42.1 1.1 %collective-permute-start.12 = (bf16[32,6144]{1,0:T(8,128)(2,1)S(1)}, bf16[32,6144]{1,0:T(8,128)(2,1)S(1)}, u32[]{:S(2)}, u32[]{:S(2)}) collective-permute-start(bf16[32,6144]{1,0:T(8,128)(2,1)S(1)} %get-tuple-element.52), channel_id=1, source_target_pairs={{0,4},{1,3},{2,6},{3,1},{4,0},{5,7},{6,2},{7,5},{8,12},{9,11},{10,... | collective-permute-start | bytes 1179656 | tf_op jit(solution)/shard_map/ppermute | solution.py:132
  43.1 5.8 %collective-permute-done.13 = bf16[32,6144]{1,0:T(8,128)(2,1)S(1)} collective-permute-done((bf16[32,6144]{1,0:T(8,128)(2,1)S(1)}, bf16[32,6144]{1,0:T(8,128)(2,1)S(1)}, u32[]{:S(2)}, u32[]{:S(2)}) %collective-permute-start.13) | collective-permute-done | bytes 393248 | tf_op jit(solution)/shard_map/ppermute | solution.py:132
  48.9 0.1 add_convert_fusion.1
  49.0 1.4 %collective-permute-start.14 = (bf16[32,6144]{1,0:T(8,128)(2,1)S(1)}, bf16[32,6144]{1,0:T(8,128)(2,1)S(1)}, u32[]{:S(2)}, u32[]{:S(2)}) collective-permute-start(bf16[32,6144]{1,0:T(8,128)(2,1)S(1)} %add_convert_fusion.1), channel_id=1, source_target_pairs={{0,2},{1,5},{2,0},{3,7},{4,6},{5,1},{6,4},{7,3},{8,10},{9,13},{10,... | collective-permute-start | bytes 1179656 | tf_op jit(solution)/shard_map/ppermute | solution.py:132
  50.4 4.8 %collective-permute-done.12 = bf16[32,6144]{1,0:T(8,128)(2,1)S(1)} collective-permute-done((bf16[32,6144]{1,0:T(8,128)(2,1)S(1)}, bf16[32,6144]{1,0:T(8,128)(2,1)S(1)}, u32[]{:S(2)}, u32[]{:S(2)}) %collective-permute-start.12) | collective-permute-done | bytes 393248 | tf_op jit(solution)/shard_map/ppermute | solution.py:132
  55.2 0.1 convert_add_fusion
  55.3 1.5 %collective-permute-done.14 = bf16[32,6144]{1,0:T(8,128)(2,1)S(1)} collective-permute-done((bf16[32,6144]{1,0:T(8,128)(2,1)S(1)}, bf16[32,6144]{1,0:T(8,128)(2,1)S(1)}, u32[]{:S(2)}, u32[]{:S(2)}) %collective-permute-start.14) | collective-permute-done | bytes 393248 | tf_op jit(solution)/shard_map/ppermute | solution.py:132
  56.8 0.8 %add_convert_fusion = bf16[32,6144]{1,0:T(8,128)(2,1)} fusion(f32[32,6144]{1,0:T(8,128)S(1)} %convert_add_fusion, bf16[32,6144]{1,0:T(8,128)(2,1)S(1)} %collective-permute-done.14), kind=kLoop, calls=%fused_computation | loop fusion | flops 589824 | bytes 1572864 | tf_op jit(solution)/shard_map/convert_element_type | solution.py:570
  (18 shorter events, 0.1 us)
Async XLA Ops:
  0.0 8.9 %copy-start.2 = (bf16[32,6144]{1,0:T(8,128)(2,1)S(1)}, bf16[32,6144]{1,0:T(8,128)(2,1)}, u32[]{:S(2)}) copy-start(bf16[32,6144]{1,0:T(8,128)(2,1)} %pass_ref.3) | copy-start | bytes 1179652
  0.0 40.0 %collective-permute-start.11 = (bf16[512,6144]{1,0:T(8,128)(2,1)}, bf16[512,6144]{1,0:T(8,128)(2,1)S(1)}, u32[]{:S(2)}, u32[]{:S(2)}) collective-permute-start(bf16[512,6144]{1,0:T(8,128)(2,1)} %w_hbm.5), channel_id=1, source_target_pairs={{0,1},{1,0},{2,3},{3,2},{4,5},{5,4},{6,7},{7,6},{8,9},{9,8},{10,11... | collective-permute-start | bytes 18874376 | tf_op jit(solution)/shard_map/ppermute | solution.py:132
  0.5 8.5 %collective-permute-start.1 = (bf16[32,6144]{1,0:T(8,128)(2,1)}, bf16[32,6144]{1,0:T(8,128)(2,1)S(1)}, u32[]{:S(2)}, u32[]{:S(2)}) collective-permute-start(bf16[32,6144]{1,0:T(8,128)(2,1)} %pass_ref.3), channel_id=1, source_target_pairs={{0,2},{1,5},{2,0},{3,7},{4,6},{5,1},{6,4},{7,3},{8,10},{9,13},{10,... | collective-permute-start | bytes 1179656 | tf_op jit(solution)/shard_map/ppermute | solution.py:132
  7.4 8.4 %collective-permute-start.2 = (bf16[32,6144]{1,0:T(8,128)(2,1)S(1)}, bf16[32,6144]{1,0:T(8,128)(2,1)S(1)}, u32[]{:S(2)}, u32[]{:S(2)}) collective-permute-start(bf16[32,6144]{1,0:T(8,128)(2,1)S(1)} %get-tuple-element.32.refs_0_), channel_id=1, source_target_pairs={{0,4},{1,3},{2,6},{3,1},{4,0},{5,7},{6,2},{7,5},{8,12},{9,11},{10,... | collective-permute-start | bytes 1179656 | tf_op jit(solution)/shard_map/ppermute | solution.py:132
  8.9 7.4 %collective-permute-start = (bf16[32,6144]{1,0:T(8,128)(2,1)S(1)}, bf16[32,6144]{1,0:T(8,128)(2,1)S(1)}, u32[]{:S(2)}, u32[]{:S(2)}) collective-permute-start(bf16[32,6144]{1,0:T(8,128)(2,1)S(1)} %copy-done.2), channel_id=1, source_target_pairs={{0,1},{1,0},{2,3},{3,2},{4,5},{5,4},{6,7},{7,6},{8,9},{9,8},{10,11... | collective-permute-start | bytes 1179656 | tf_op jit(solution)/shard_map/ppermute | solution.py:132
  9.0 11.0 %collective-permute-start.5 = (bf16[32,6144]{1,0:T(8,128)(2,1)S(1)}, bf16[32,6144]{1,0:T(8,128)(2,1)S(1)}, u32[]{:S(2)}, u32[]{:S(2)}) collective-permute-start(bf16[32,6144]{1,0:T(8,128)(2,1)S(1)} %tie.2.refs_2_), channel_id=1, source_target_pairs={{0,4},{1,3},{2,6},{3,1},{4,0},{5,7},{6,2},{7,5},{8,12},{9,11},{10,... | collective-permute-start | bytes 1179656 | tf_op jit(solution)/shard_map/ppermute | solution.py:132
  15.7 4.4 %collective-permute-start.3 = (bf16[32,6144]{1,0:T(8,128)(2,1)S(1)}, bf16[32,6144]{1,0:T(8,128)(2,1)S(1)}, u32[]{:S(2)}, u32[]{:S(2)}) collective-permute-start(bf16[32,6144]{1,0:T(8,128)(2,1)S(1)} %tie.2.refs_2_), channel_id=1, source_target_pairs={{0,1},{1,0},{2,3},{3,2},{4,5},{5,4},{6,7},{7,6},{8,9},{9,8},{10,11... | collective-permute-start | bytes 1179656 | tf_op jit(solution)/shard_map/ppermute | solution.py:132
  15.8 4.3 %collective-permute-start.4 = (bf16[32,6144]{1,0:T(8,128)(2,1)S(1)}, bf16[32,6144]{1,0:T(8,128)(2,1)S(1)}, u32[]{:S(2)}, u32[]{:S(2)}) collective-permute-start(bf16[32,6144]{1,0:T(8,128)(2,1)S(1)} %collective-permute-done.2.refs_3_), channel_id=1, source_target_pairs={{0,1},{1,0},{2,3},{3,2},{4,5},{5,4},{6,7},{7,6},{8,9},{9,8},{10,11... | collective-permute-start | bytes 1179656 | tf_op jit(solution)/shard_map/ppermute | solution.py:132
  16.3 5.5 %copy-start = (f32[4]{0:T(128)S(1)}, f32[4]{0:T(128)}, u32[]{:S(2)}) copy-start(f32[4]{0:T(128)} %rate_ref.5) | copy-start | bytes 52
  20.0 1.8 %collective-permute-start.6 = (bf16[32,6144]{1,0:T(8,128)(2,1)S(1)}, bf16[32,6144]{1,0:T(8,128)(2,1)S(1)}, u32[]{:S(2)}, u32[]{:S(2)}) collective-permute-start(bf16[32,6144]{1,0:T(8,128)(2,1)S(1)} %tie.3.refs_2_), channel_id=1, source_target_pairs={{0,1},{1,0},{2,3},{3,2},{4,5},{5,4},{6,7},{7,6},{8,9},{9,8},{10,11... | collective-permute-start | bytes 1179656 | tf_op jit(solution)/shard_map/ppermute | solution.py:132
  24.5 13.0 %copy-start.1 = (f32[512]{0:T(512)S(1)}, f32[512]{0:T(512)}, u32[]{:S(2)}) copy-start(f32[512]{0:T(512)} %param.8) | copy-start | bytes 6148
  24.5 12.2 %collective-permute-start.7 = (bf16[4,128,128]{2,1,0:T(8,128)(2,1)S(1)}, bf16[4,128,128]{2,1,0:T(8,128)(2,1)S(1)}, u32[]{:S(2)}, u32[]{:S(2)}) collective-permute-start(bf16[4,128,128]{2,1,0:T(8,128)(2,1)S(1)} %get-tuple-element.47), channel_id=1, source_target_pairs={{0,8},{8,16},{16,24},{24,0},{1,9},{9,17},{17,25},{25,1},{2,10},{10... | collective-permute-start | bytes 393224 | tf_op jit(solution)/shard_map/ppermute | solution.py:550
  25.9 11.6 %collective-permute-start.8 = (bf16[4,128,128]{2,1,0:T(8,128)(2,1)S(1)}, bf16[4,128,128]{2,1,0:T(8,128)(2,1)S(1)}, u32[]{:S(2)}, u32[]{:S(2)}) collective-permute-start(bf16[4,128,128]{2,1,0:T(8,128)(2,1)S(1)} %get-tuple-element.47), channel_id=1, source_target_pairs={{0,16},{8,24},{16,0},{24,8},{1,17},{9,25},{17,1},{25,9},{2,18},{10... | collective-permute-start | bytes 393224 | tf_op jit(solution)/shard_map/ppermute | solution.py:550
  28.5 9.0 %collective-permute-start.9 = (bf16[4,128,128]{2,1,0:T(8,128)(2,1)S(1)}, bf16[4,128,128]{2,1,0:T(8,128)(2,1)S(1)}, u32[]{:S(2)}, u32[]{:S(2)}) collective-permute-start(bf16[4,128,128]{2,1,0:T(8,128)(2,1)S(1)} %get-tuple-element.47), channel_id=1, source_target_pairs={{0,24},{1,25},{2,26},{3,27},{4,28},{5,29},{6,30},{7,31}} | collective-permute-start | bytes 393224 | tf_op jit(solution)/shard_map/ppermute | solution.py:552
  38.6 1.4 %collective-permute-start.10 = (bf16[128,512]{1,0:T(8,128)(2,1)S(1)}, bf16[128,512]{1,0:T(8,128)(2,1)S(1)}, u32[]{:S(2)}, u32[]{:S(2)}) collective-permute-start(bf16[128,512]{1,0:T(8,128)(2,1)S(1)} %get-tuple-element.50), channel_id=1, source_target_pairs={{0,1},{1,0},{2,3},{3,2},{4,5},{5,4},{6,7},{7,6},{8,9},{9,8},{10,11... | collective-permute-start | bytes 393224 | tf_op jit(solution)/shard_map/ppermute | solution.py:132
  41.0 7.8 %collective-permute-start.13 = (bf16[32,6144]{1,0:T(8,128)(2,1)S(1)}, bf16[32,6144]{1,0:T(8,128)(2,1)S(1)}, u32[]{:S(2)}, u32[]{:S(2)}) collective-permute-start(bf16[32,6144]{1,0:T(8,128)(2,1)S(1)} %get-tuple-element.54), channel_id=1, source_target_pairs={{0,4},{1,3},{2,6},{3,1},{4,0},{5,7},{6,2},{7,5},{8,12},{9,11},{10,... | collective-permute-start | bytes 1179656 | tf_op jit(solution)/shard_map/ppermute | solution.py:132
  42.1 13.1 %collective-permute-start.12 = (bf16[32,6144]{1,0:T(8,128)(2,1)S(1)}, bf16[32,6144]{1,0:T(8,128)(2,1)S(1)}, u32[]{:S(2)}, u32[]{:S(2)}) collective-permute-start(bf16[32,6144]{1,0:T(8,128)(2,1)S(1)} %get-tuple-element.52), channel_id=1, source_target_pairs={{0,4},{1,3},{2,6},{3,1},{4,0},{5,7},{6,2},{7,5},{8,12},{9,11},{10,... | collective-permute-start | bytes 1179656 | tf_op jit(solution)/shard_map/ppermute | solution.py:132
  49.0 7.8 %collective-permute-start.14 = (bf16[32,6144]{1,0:T(8,128)(2,1)S(1)}, bf16[32,6144]{1,0:T(8,128)(2,1)S(1)}, u32[]{:S(2)}, u32[]{:S(2)}) collective-permute-start(bf16[32,6144]{1,0:T(8,128)(2,1)S(1)} %add_convert_fusion.1), channel_id=1, source_target_pairs={{0,2},{1,5},{2,0},{3,7},{4,6},{5,1},{6,4},{7,3},{8,10},{9,13},{10,... | collective-permute-start | bytes 1179656 | tf_op jit(solution)/shard_map/ppermute | solution.py:132

commit v5 on v4

--- a/solution.py
+++ b/solution.py
@@ -376,11 +376,34 @@
         ).astype(BF16)
 
 
+def early_kernel(_, qg, x_all, q_ref):
+    count, width = q_ref.shape
+    q_ref[...] = silu(jnp.dot(x_all[:count], qg[:, :width], preferred_element_type=F32))
+
+
+def early(x_all, qg):
+    count, depth = x_all.shape[0] // 2, x_all.shape[1]
+    width = qg.shape[1] // 2
+
+    return pl.pallas_call(
+        early_kernel,
+        in_specs=[VMEM, VMEM],
+        out_specs=[VMEM, VMEM],
+        out_shape=[pltpu.VMEM(x_all.shape, BF16), pltpu.VMEM((count, width), BF16)],
+        input_output_aliases={0: 0},
+        compiler_params=pltpu.CompilerParams(vmem_limit_bytes=2 * MIB),
+        cost_estimate=pl.CostEstimate(
+            flops=2 * count * depth * width, bytes_accessed=2 * depth * width, transcendentals=0
+        ),
+        name="early",
+    )(pinned(x_all), pinned(qg))
+
+
 def gates_kernel(x_all, qg, w_hbm, q_ref, g_ref, w_ref, sem):
     copy = pltpu.make_async_copy(w_hbm, w_ref, sem)
     copy.start()
-    width = q_ref.shape[1]
-    q_ref[...] = silu(jnp.dot(x_all[...], qg[:, :width], preferred_element_type=F32))
+    count, width = q_ref.shape
+    q_ref[...] = silu(jnp.dot(x_all[count:], qg[:, :width], preferred_element_type=F32))
     mixed = jnp.dot(x_all[...], qg[:, width:], preferred_element_type=F32)
     g_ref[...] = 1.0 / (1.0 + jnp.exp(-mixed))
     copy.wait()
@@ -394,30 +417,29 @@
         in_specs=[VMEM, VMEM, HBM],
         out_specs=[VMEM] * 3,
         out_shape=[
-            pltpu.VMEM((count, width), BF16),
+            pltpu.VMEM((count // 2, width), BF16),
             pltpu.VMEM((count, width), F32),
             pltpu.VMEM(w.shape, w.dtype),
         ],
         scratch_shapes=[pltpu.SemaphoreType.DMA],
         compiler_params=pltpu.CompilerParams(vmem_limit_bytes=2 * MIB),
         cost_estimate=pl.CostEstimate(
-            flops=4 * count * depth * width, bytes_accessed=8 * depth * width, transcendentals=0
+            flops=3 * count * depth * width, bytes_accessed=8 * depth * width, transcendentals=0
         ),
         name="gates",
     )(pinned(x_all), pinned(qg), in_hbm(w))
 
 
-def inner_kernel(rate_ref, place_ref, across_ref, q_ref, k0, k1, v0, v1, o_ref):
+def inner_kernel(rate_ref, place_ref, across_ref, q0, q1, k0, k1, v0, v1, o_ref):
     diff = place_ref[...] - across_ref[...]
     seen = diff >= 0
     diff = jnp.maximum(diff, 0.0)
     for h in range(o_ref.shape[1] // HD):
         cols = slice(h * HD, (h + 1) * HD)
+        q = jnp.concatenate([q0[:, cols], q1[:, cols]], 0)
         k = jnp.concatenate([k0[:, cols], k1[:, cols]], 0)
         v = jnp.concatenate([v0[:, cols], v1[:, cols]], 0)
-        scores = lax.dot_general(
-            q_ref[:, cols], k, (((1,), (1,)), ((), ())), preferred_element_type=F32
-        )
+        scores = lax.dot_general(q, k, (((1,), (1,)), ((), ())), preferred_element_type=F32)
         causal = jnp.where(seen, jnp.exp(-rate_ref[h] * diff), 0.0)
         o_ref[:, cols] = jnp.dot(
             (scores * causal).astype(BF16), v, preferred_element_type=F32
@@ -427,7 +449,7 @@
 TO_SUM = (3, 7, 1, 2, 5, 6, 0, 4)
 
 
-def finish_kernel(rate_ref, place_ref, gain_ref, in_ref, q_ref, g_ref, s1, s2, s3, y_ref, z_ref):
+def finish_kernel(rate_ref, place_ref, gain_ref, in_ref, q0, q1, g_ref, s1, s2, s3, y_ref, z_ref):
     part = in_ref.shape[0] // 8
     block = lax.axis_index("seq")
     for h in range(in_ref.shape[1] // HD):
@@ -440,7 +462,7 @@
         )
         high = state.astype(BF16)
         low = (state - high.astype(F32)).astype(BF16)
-        q = q_ref[:, cols]
+        q = jnp.concatenate([q0[:, cols], q1[:, cols]], 0)
         extra = jnp.dot(q, high, preferred_element_type=F32) + jnp.dot(
             q, low, preferred_element_type=F32
         )
@@ -542,24 +564,26 @@
     first_beside = hop(second, CORE)
     (far,) = tie([far], [k0])
     far_beside = hop(far, CORE)
+    x_all, q0 = early(x_all, qg)
     x_all, k1, v1, states = project_far(
         decay_rate, down, k0, v0, kv, x_all, [second_beside, first_beside, far, far_beside]
     )
 
     came = [
-        lax.ppermute(states, "seq", [(i, (i + k) % 4) for i in range(4)]) for k in (1, 2)
+        lax.ppermute(states, "seq", [(i, (i + 1) % 4) for i in range(4)]),
+        lax.ppermute(states, "seq", [(0, 2), (1, 3)]),
     ]
     came.append(lax.ppermute(states, "seq", [(0, 3)]))
-    q, g, w_own = gates(x_all, qg, out_weight)
+    q1, g, w_own = gates(x_all, qg, out_weight)
     full = jax.ShapeDtypeStruct((8 * rows, heads * HD), F32)
-    inner = small(inner_kernel, 1, full, "inner", decay_rate, down, across, q, k0, k1, v0, v1)
+    inner = small(inner_kernel, 1, full, "inner", decay_rate, down, across, q0, q1, k0, k1, v0, v1)
     split = jax.ShapeDtypeStruct((4 * rows, heads * HD), BF16)
     y, y_other = small(
         finish_kernel,
         1,
         [split, split],
         "finish",
-        decay_rate, down, head_gain[None, :], inner, q, g, *came,
+        decay_rate, down, head_gain[None, :], inner, q0, q1, g, *came,
     )
     z = hop(y_other, CORE)
     a, b, c, d = out_rows(out_own(y, w_own), z, w_other)

time: 57.8 us -> 57.8 us (level)
  the two profiles are of different devices: /device:TPU:0 before, /device:TPU:9 now
where the time goes in v5:
time: 57.8 us; the launch traced here: 56.8 us
  Pallas kernels  23.1 us (40%)
  waiting for transfers between devices  16.5 us (29%)
  starting transfers between devices  16 us (28%)
  other arithmetic  0.95 us (2%)
    ppermute x12, waiting for transfers between devices, hop(): return lax.ppermute(value, 'tp', pairs)  13.8 us
    ppermute x12, starting transfers between devices, hop(): return lax.ppermute(value, 'tp', pairs)  10.8 us
    pallas_call x2, Pallas kernels, prep(): pl.pallas_call(functools.partial(prep_kernel, first, last, bool(turned)),...  8.58 us
    pallas_call x1, Pallas kernels, project_near(): pl.pallas_call(functools.partial(near_kernel, len(rows), first), in_specs...  3.66 us
    ppermute x1, starting transfers between devices, paired_device(): lax.ppermute(states, 'seq', [(0, 2), (1, 3)])  3.08 us
    pallas_call x1, Pallas kernels, gates(): pl.pallas_call(gates_kernel, in_specs=[VMEM, VMEM, HBM], out_specs=[VMEM]...  2.8 us
    ppermute x1, waiting for transfers between devices, paired_device(): lax.ppermute(states, 'seq', [(0, 2), (1, 3)])  2.71 us
    pallas_call x1, Pallas kernels, project_far(): pl.pallas_call(functools.partial(far_kernel, len(rows)), in_specs=[SMEM]...  2.67 us
  transfers between devices with their start and end apart: 15, of which 5 were waited for; matrix products, arithmetic and copies ran while one was open for 0% of the time, Pallas kernels for 39%

profile of v5, /device:TPU:9, one launch (start us, length us, event | category | flops | bytes accessed | tf_op | source)
XLA Modules:
  0.0 56.8 jit_solution(11433408922600494988)
XLA Ops:
  0.0 0.7 %collective-permute-start.11 = (bf16[512,6144]{1,0:T(8,128)(2,1)}, bf16[512,6144]{1,0:T(8,128)(2,1)S(1)}, u32[]{:S(2)}, u32[]{:S(2)}) collective-permute-start(bf16[512,6144]{1,0:T(8,128)(2,1)} %w_hbm.5), channel_id=1, source_target_pairs={{0,1},{1,0},{2,3},{3,2},{4,5},{5,4},{6,7},{7,6},{8,9},{9,8},{10,11... | collective-permute-start | bytes 18874376 | tf_op jit(solution)/shard_map/ppermute | solution.py:132
  0.7 1.2 %collective-permute-start.1 = (bf16[32,6144]{1,0:T(8,128)(2,1)}, bf16[32,6144]{1,0:T(8,128)(2,1)S(1)}, u32[]{:S(2)}, u32[]{:S(2)}) collective-permute-start(bf16[32,6144]{1,0:T(8,128)(2,1)} %pass_ref.3), channel_id=1, source_target_pairs={{0,2},{1,5},{2,0},{3,7},{4,6},{5,1},{6,4},{7,3},{8,10},{9,13},{10,... | collective-permute-start | bytes 1179656 | tf_op jit(solution)/shard_map/ppermute | solution.py:132
  1.9 4.3 %prep_a.1 = (bf16[6144,1024]{1,0:T(8,128)(2,1)S(1)}, bf16[6144,1024]{1,0:T(8,128)(2,1)S(1)}, bf16[32,6144]{1,0:T(8,128)(2,1)S(1)}, f32[256,1]{1,0:T(8,128)S(1)}, f32[1,256]{1,0:T(1,128)S(1)}) custom-call(bf16[6144,4,512]{2,1,0:T(4,128)(2,1)} %refs_4_.1, bf16[32,6144]{1,0:T(8,128)(2,1)} %pass_ref.3), custom_call_target="tpu_custom_call" | custom-call | bytes 18874368 | tf_op jit(solution)/shard_map/prep_a/pallas_call | solution.py:240
  6.3 1.3 %collective-permute-start.2 = (bf16[32,6144]{1,0:T(8,128)(2,1)S(1)}, bf16[32,6144]{1,0:T(8,128)(2,1)S(1)}, u32[]{:S(2)}, u32[]{:S(2)}) collective-permute-start(bf16[32,6144]{1,0:T(8,128)(2,1)S(1)} %get-tuple-element.34.refs_0_), channel_id=1, source_target_pairs={{0,4},{1,3},{2,6},{3,1},{4,0},{5,7},{6,2},{7,5},{8,12},{9,11},{10,... | collective-permute-start | bytes 1179656 | tf_op jit(solution)/shard_map/ppermute | solution.py:132
  7.6 0.6 %collective-permute-start = (bf16[32,6144]{1,0:T(8,128)(2,1)S(1)}, bf16[32,6144]{1,0:T(8,128)(2,1)S(1)}, u32[]{:S(2)}, u32[]{:S(2)}) collective-permute-start(bf16[32,6144]{1,0:T(8,128)(2,1)S(1)} %copy-done.2), channel_id=1, source_target_pairs={{0,1},{1,0},{2,3},{3,2},{4,5},{5,4},{6,7},{7,6},{8,9},{9,8},{10,11... | collective-permute-start | bytes 1179656 | tf_op jit(solution)/shard_map/ppermute | solution.py:132
  8.2 0.8 %collective-permute-start.5 = (bf16[32,6144]{1,0:T(8,128)(2,1)S(1)}, bf16[32,6144]{1,0:T(8,128)(2,1)S(1)}, u32[]{:S(2)}, u32[]{:S(2)}) collective-permute-start(bf16[32,6144]{1,0:T(8,128)(2,1)S(1)} %tie.2.refs_2_), channel_id=1, source_target_pairs={{0,4},{1,3},{2,6},{3,1},{4,0},{5,7},{6,2},{7,5},{8,12},{9,11},{10,... | collective-permute-start | bytes 1179656 | tf_op jit(solution)/shard_map/ppermute | solution.py:132
  9.0 4.2 %prep_b.1 = (bf16[6144,1024]{1,0:T(8,128)(2,1)S(1)}, bf16[6144,1024]{1,0:T(8,128)(2,1)S(1)}) custom-call(bf16[6144,4,512]{2,1,0:T(4,128)(2,1)} %refs_4_.1, bf16[32,6144]{1,0:T(8,128)(2,1)} %pass_ref.3, bf16[6144,1024]{1,0:T(8,128)(2,1)S(1)} %get-tuple-element.35.refs_0_, ...), custom_call_target="tpu_custom_call", output_to_operand_aliasing={{0}: (2, {}), {1}: (3, {})} | custom-call | bytes 18874368 | tf_op jit(solution)/shard_map/prep_b/pallas_call | solution.py:240
  13.3 1.5 %collective-permute-start.3 = (bf16[32,6144]{1,0:T(8,128)(2,1)S(1)}, bf16[32,6144]{1,0:T(8,128)(2,1)S(1)}, u32[]{:S(2)}, u32[]{:S(2)}) collective-permute-start(bf16[32,6144]{1,0:T(8,128)(2,1)S(1)} %tie.2.refs_2_), channel_id=1, source_target_pairs={{0,1},{1,0},{2,3},{3,2},{4,5},{5,4},{6,7},{7,6},{8,9},{9,8},{10,11... | collective-permute-start | bytes 1179656 | tf_op jit(solution)/shard_map/ppermute | solution.py:132
  14.8 0.1 collective-permute-start.4
  14.9 3.7 %project_near.1 = (bf16[6144,1024]{1,0:T(8,128)(2,1)S(1)}, bf16[6144,1024]{1,0:T(8,128)(2,1)S(1)}, bf16[256,6144]{1,0:T(8,128)(2,1)S(1)}, bf16[128,512]{1,0:T(8,128)(2,1)S(1)}, bf16[128,512]{1,0:T(8,128)(2,1)S(1)}) custom-call(bf16[32,6144]{1,0:T(8,128)(2,1)S(1)} %get-tuple-element.34.refs_0_, ...), custom_call_target="tpu_custom_call", output_to_operand_aliasing={{0}: (5, {}), {1}: (6, {})} | custom-call | flops 3221225472 | bytes 50331648 | tf_op jit(solution)/shard_map/project_near/pallas_call | solution.py:299
  18.6 0.5 collective-permute-start.6
  19.1 1.0 %early.1 = (bf16[256,6144]{1,0:T(8,128)(2,1)S(1)}, bf16[128,512]{1,0:T(8,128)(2,1)S(1)}) custom-call(bf16[256,6144]{1,0:T(8,128)(2,1)S(1)} %get-tuple-element.39._, bf16[6144,1024]{1,0:T(8,128)(2,1)S(1)} %get-tuple-element.40.qg), custom_call_target="tpu_custom_call", output_to_operand_aliasing={{0}: (0, {})} | custom-call | flops 805306368 | bytes 6291456 | tf_op jit(solution)/shard_map/early/pallas_call | solution.py:388
  20.1 0.3 collective-permute-done.6.refs_3_
  20.4 2.7 %project_far.1 = (bf16[256,6144]{1,0:T(8,128)(2,1)S(1)}, bf16[128,512]{1,0:T(8,128)(2,1)S(1)}, bf16[128,512]{1,0:T(8,128)(2,1)S(1)}, bf16[4,128,128]{2,1,0:T(8,128)(2,1)S(1)}) custom-call(f32[4]{0:T(128)S(1)} %copy-done, f32[256,1]{1,0:T(8,128)S(1)} %get-tuple-element.32.refs_1_.place_ref, ...), custom_call_target="tpu_custom_call", output_to_operand_aliasing={{0}: (5, {})} | custom-call | flops 1610612736 | bytes 12582912 | tf_op jit(solution)/shard_map/project_far/pallas_call | solution.py:347
  23.1 1.3 %collective-permute-start.7 = (bf16[4,128,128]{2,1,0:T(8,128)(2,1)S(1)}, bf16[4,128,128]{2,1,0:T(8,128)(2,1)S(1)}, u32[]{:S(2)}, u32[]{:S(2)}) collective-permute-start(bf16[4,128,128]{2,1,0:T(8,128)(2,1)S(1)} %get-tuple-element.51), channel_id=1, source_target_pairs={{0,8},{8,16},{16,24},{24,0},{1,9},{9,17},{17,25},{25,1},{2,10},{10... | collective-permute-start | bytes 393224 | tf_op jit(solution)/shard_map/ppermute | solution.py:573
  24.5 3.1 %collective-permute-start.8 = (bf16[4,128,128]{2,1,0:T(8,128)(2,1)S(1)}, bf16[4,128,128]{2,1,0:T(8,128)(2,1)S(1)}, u32[]{:S(2)}, u32[]{:S(2)}) collective-permute-start(bf16[4,128,128]{2,1,0:T(8,128)(2,1)S(1)} %get-tuple-element.51), channel_id=1, source_target_pairs={{0,16},{8,24},{1,17},{9,25},{2,18},{10,26},{3,19},{11,27},{4,20},{... | collective-permute-start | bytes 393224 | tf_op jit(solution)/shard_map/ppermute | solution.py:574
  27.5 0.8 %collective-permute-start.9 = (bf16[4,128,128]{2,1,0:T(8,128)(2,1)S(1)}, bf16[4,128,128]{2,1,0:T(8,128)(2,1)S(1)}, u32[]{:S(2)}, u32[]{:S(2)}) collective-permute-start(bf16[4,128,128]{2,1,0:T(8,128)(2,1)S(1)} %get-tuple-element.51), channel_id=1, source_target_pairs={{0,24},{1,25},{2,26},{3,27},{4,28},{5,29},{6,30},{7,31}} | collective-permute-start | bytes 393224 | tf_op jit(solution)/shard_map/ppermute | solution.py:576
  28.4 2.8 %gates.1 = (bf16[128,512]{1,0:T(8,128)(2,1)S(1)}, f32[256,512]{1,0:T(8,128)S(1)}, bf16[512,6144]{1,0:T(8,128)(2,1)S(1)}) custom-call(bf16[256,6144]{1,0:T(8,128)(2,1)S(1)} %get-tuple-element.46.x_all, bf16[6144,1024]{1,0:T(8,128)(2,1)S(1)} %get-tuple-element.40.qg, bf16[512,6144]{1,0:T(8,128)(2,1)} %w_hbm.5), custom_call_target="tpu_custom_call" | custom-call | flops 2415919104 | bytes 25165824 | tf_op jit(solution)/shard_map/gates/pallas_call | solution.py:415
  31.2 1.2 %inner.1.in_ref = f32[256,512]{1,0:T(8,128)S(1)} custom-call(f32[4]{0:T(128)S(1)} %copy-done, f32[256,1]{1,0:T(8,128)S(1)} %get-tuple-element.32.refs_1_.place_ref, f32[1,256]{1,0:T(1,128)S(1)} %get-tuple-element.33.across_ref, bf16[128,512]{1,0:T(8,128)(2,1)S(1)} %get-tuple-element.41.q0, bf16[128,512]{1,0:T(8,128)(2,1)S(1)} %get-tuple-element.47.q1, ...), custom_call_target="tpu_custom_call" | custom-call | tf_op jit(solution)/shard_map/inner/pallas_call | solution.py:478
  32.5 2.7 %collective-permute-done.8.s2 = bf16[4,128,128]{2,1,0:T(8,128)(2,1)S(1)} collective-permute-done((bf16[4,128,128]{2,1,0:T(8,128)(2,1)S(1)}, bf16[4,128,128]{2,1,0:T(8,128)(2,1)S(1)}, u32[]{:S(2)}, u32[]{:S(2)}) %collective-permute-start.8) | collective-permute-done | bytes 131104 | tf_op jit(solution)/shard_map/ppermute | solution.py:574
  35.2 1.1 %finish.1 = (bf16[128,512]{1,0:T(8,128)(2,1)S(1)}, bf16[128,512]{1,0:T(8,128)(2,1)S(1)}) custom-call(f32[4]{0:T(128)S(1)} %copy-done, f32[256,1]{1,0:T(8,128)S(1)} %get-tuple-element.32.refs_1_.place_ref, f32[1,512]{1,0:T(1,128)S(1)} %bitcast.1, f32[256,512]{1,0:T(8,128)S(1)} %inner.1.in_ref, bf16[128,512]{1,0:T(8,128)(2,1)S(1)} %get-tuple-element.41.q0, ...), custom_call_target="tpu_custom_call" | custom-call | tf_op jit(solution)/shard_map/finish/pallas_call | solution.py:478
  36.3 1.7 %collective-permute-start.10 = (bf16[128,512]{1,0:T(8,128)(2,1)S(1)}, bf16[128,512]{1,0:T(8,128)(2,1)S(1)}, u32[]{:S(2)}, u32[]{:S(2)}) collective-permute-start(bf16[128,512]{1,0:T(8,128)(2,1)S(1)} %get-tuple-element.54), channel_id=1, source_target_pairs={{0,1},{1,0},{2,3},{3,2},{4,5},{5,4},{6,7},{7,6},{8,9},{9,8},{10,11... | collective-permute-start | bytes 393224 | tf_op jit(solution)/shard_map/ppermute | solution.py:132
  38.1 1.0 %out_own.1.own_ref = f32[128,6144]{1,0:T(8,128)S(1)} custom-call(bf16[128,512]{1,0:T(8,128)(2,1)S(1)} %get-tuple-element.52.y_ref, bf16[512,6144]{1,0:T(8,128)(2,1)S(1)} %get-tuple-element.53.w_ref), custom_call_target="tpu_custom_call" | custom-call | flops 805306368 | bytes 6291456 | tf_op jit(solution)/shard_map/out_own/pallas_call | solution.py:498
  39.1 1.0 %out_rows.1 = (bf16[32,6144]{1,0:T(8,128)(2,1)S(1)}, f32[32,6144]{1,0:T(8,128)S(1)}, bf16[32,6144]{1,0:T(8,128)(2,1)S(1)}, f32[32,6144]{1,0:T(8,128)S(1)}) custom-call(f32[128,6144]{1,0:T(8,128)S(1)} %out_own.1.own_ref, bf16[128,512]{1,0:T(8,128)(2,1)S(1)} %collective-permute-done.10.z_ref, bf16[512,6144]{1,0:T(8,128)(2,1)S(1)} %collective-permute-done.11.u_ref), custom_call_target="tpu_custom_call" | custom-call | flops 805306368 | bytes 6291456 | tf_op jit(solution)/shard_map/out_rows/pallas_call | solution.py:527
  40.1 1.2 %collective-permute-start.13 = (bf16[32,6144]{1,0:T(8,128)(2,1)S(1)}, bf16[32,6144]{1,0:T(8,128)(2,1)S(1)}, u32[]{:S(2)}, u32[]{:S(2)}) collective-permute-start(bf16[32,6144]{1,0:T(8,128)(2,1)S(1)} %get-tuple-element.58), channel_id=1, source_target_pairs={{0,4},{1,3},{2,6},{3,1},{4,0},{5,7},{6,2},{7,5},{8,12},{9,11},{10,... | collective-permute-start | bytes 1179656 | tf_op jit(solution)/shard_map/ppermute | solution.py:132
  41.2 0.4 collective-permute-start.12
  41.6 5.5 %collective-permute-done.13 = bf16[32,6144]{1,0:T(8,128)(2,1)S(1)} collective-permute-done((bf16[32,6144]{1,0:T(8,128)(2,1)S(1)}, bf16[32,6144]{1,0:T(8,128)(2,1)S(1)}, u32[]{:S(2)}, u32[]{:S(2)}) %collective-permute-start.13) | collective-permute-done | bytes 393248 | tf_op jit(solution)/shard_map/ppermute | solution.py:132
  47.1 0.1 add_convert_fusion.1
  47.1 0.8 %collective-permute-start.14 = (bf16[32,6144]{1,0:T(8,128)(2,1)S(1)}, bf16[32,6144]{1,0:T(8,128)(2,1)S(1)}, u32[]{:S(2)}, u32[]{:S(2)}) collective-permute-start(bf16[32,6144]{1,0:T(8,128)(2,1)S(1)} %add_convert_fusion.1), channel_id=1, source_target_pairs={{0,2},{1,5},{2,0},{3,7},{4,6},{5,1},{6,4},{7,3},{8,10},{9,13},{10,... | collective-permute-start | bytes 1179656 | tf_op jit(solution)/shard_map/ppermute | solution.py:132
  47.9 3.4 %collective-permute-done.12 = bf16[32,6144]{1,0:T(8,128)(2,1)S(1)} collective-permute-done((bf16[32,6144]{1,0:T(8,128)(2,1)S(1)}, bf16[32,6144]{1,0:T(8,128)(2,1)S(1)}, u32[]{:S(2)}, u32[]{:S(2)}) %collective-permute-start.12) | collective-permute-done | bytes 393248 | tf_op jit(solution)/shard_map/ppermute | solution.py:132
  51.3 4.6 %collective-permute-done.14 = bf16[32,6144]{1,0:T(8,128)(2,1)S(1)} collective-permute-done((bf16[32,6144]{1,0:T(8,128)(2,1)S(1)}, bf16[32,6144]{1,0:T(8,128)(2,1)S(1)}, u32[]{:S(2)}, u32[]{:S(2)}) %collective-permute-start.14) | collective-permute-done | bytes 393248 | tf_op jit(solution)/shard_map/ppermute | solution.py:132
  56.0 0.8 %add_convert_fusion = bf16[32,6144]{1,0:T(8,128)(2,1)} fusion(f32[32,6144]{1,0:T(8,128)S(1)} %convert_add_fusion, bf16[32,6144]{1,0:T(8,128)(2,1)S(1)} %collective-permute-done.14), kind=kLoop, calls=%fused_computation | loop fusion | flops 589824 | bytes 1572864 | tf_op jit(solution)/shard_map/convert_element_type | solution.py:594
  (19 shorter events, 0.1 us)
Async XLA Ops:
  0.0 7.6 %copy-start.2 = (bf16[32,6144]{1,0:T(8,128)(2,1)S(1)}, bf16[32,6144]{1,0:T(8,128)(2,1)}, u32[]{:S(2)}) copy-start(bf16[32,6144]{1,0:T(8,128)(2,1)} %pass_ref.3) | copy-start | bytes 1179652
  0.0 39.1 %collective-permute-start.11 = (bf16[512,6144]{1,0:T(8,128)(2,1)}, bf16[512,6144]{1,0:T(8,128)(2,1)S(1)}, u32[]{:S(2)}, u32[]{:S(2)}) collective-permute-start(bf16[512,6144]{1,0:T(8,128)(2,1)} %w_hbm.5), channel_id=1, source_target_pairs={{0,1},{1,0},{2,3},{3,2},{4,5},{5,4},{6,7},{7,6},{8,9},{9,8},{10,11... | collective-permute-start | bytes 18874376 | tf_op jit(solution)/shard_map/ppermute | solution.py:132
  0.7 7.5 %collective-permute-start.1 = (bf16[32,6144]{1,0:T(8,128)(2,1)}, bf16[32,6144]{1,0:T(8,128)(2,1)S(1)}, u32[]{:S(2)}, u32[]{:S(2)}) collective-permute-start(bf16[32,6144]{1,0:T(8,128)(2,1)} %pass_ref.3), channel_id=1, source_target_pairs={{0,2},{1,5},{2,0},{3,7},{4,6},{5,1},{6,4},{7,3},{8,10},{9,13},{10,... | collective-permute-start | bytes 1179656 | tf_op jit(solution)/shard_map/ppermute | solution.py:132
  6.3 8.5 %collective-permute-start.2 = (bf16[32,6144]{1,0:T(8,128)(2,1)S(1)}, bf16[32,6144]{1,0:T(8,128)(2,1)S(1)}, u32[]{:S(2)}, u32[]{:S(2)}) collective-permute-start(bf16[32,6144]{1,0:T(8,128)(2,1)S(1)} %get-tuple-element.34.refs_0_), channel_id=1, source_target_pairs={{0,4},{1,3},{2,6},{3,1},{4,0},{5,7},{6,2},{7,5},{8,12},{9,11},{10,... | collective-permute-start | bytes 1179656 | tf_op jit(solution)/shard_map/ppermute | solution.py:132
  7.6 7.3 %collective-permute-start = (bf16[32,6144]{1,0:T(8,128)(2,1)S(1)}, bf16[32,6144]{1,0:T(8,128)(2,1)S(1)}, u32[]{:S(2)}, u32[]{:S(2)}) collective-permute-start(bf16[32,6144]{1,0:T(8,128)(2,1)S(1)} %copy-done.2), channel_id=1, source_target_pairs={{0,1},{1,0},{2,3},{3,2},{4,5},{5,4},{6,7},{7,6},{8,9},{9,8},{10,11... | collective-permute-start | bytes 1179656 | tf_op jit(solution)/shard_map/ppermute | solution.py:132
  8.2 10.4 %collective-permute-start.5 = (bf16[32,6144]{1,0:T(8,128)(2,1)S(1)}, bf16[32,6144]{1,0:T(8,128)(2,1)S(1)}, u32[]{:S(2)}, u32[]{:S(2)}) collective-permute-start(bf16[32,6144]{1,0:T(8,128)(2,1)S(1)} %tie.2.refs_2_), channel_id=1, source_target_pairs={{0,4},{1,3},{2,6},{3,1},{4,0},{5,7},{6,2},{7,5},{8,12},{9,11},{10,... | collective-permute-start | bytes 1179656 | tf_op jit(solution)/shard_map/ppermute | solution.py:132
  13.3 6.8 %collective-permute-start.3 = (bf16[32,6144]{1,0:T(8,128)(2,1)S(1)}, bf16[32,6144]{1,0:T(8,128)(2,1)S(1)}, u32[]{:S(2)}, u32[]{:S(2)}) collective-permute-start(bf16[32,6144]{1,0:T(8,128)(2,1)S(1)} %tie.2.refs_2_), channel_id=1, source_target_pairs={{0,1},{1,0},{2,3},{3,2},{4,5},{5,4},{6,7},{7,6},{8,9},{9,8},{10,11... | collective-permute-start | bytes 1179656 | tf_op jit(solution)/shard_map/ppermute | solution.py:132
  14.8 5.3 %collective-permute-start.4 = (bf16[32,6144]{1,0:T(8,128)(2,1)S(1)}, bf16[32,6144]{1,0:T(8,128)(2,1)S(1)}, u32[]{:S(2)}, u32[]{:S(2)}) collective-permute-start(bf16[32,6144]{1,0:T(8,128)(2,1)S(1)} %collective-permute-done.2.refs_3_), channel_id=1, source_target_pairs={{0,1},{1,0},{2,3},{3,2},{4,5},{5,4},{6,7},{7,6},{8,9},{9,8},{10,11... | collective-permute-start | bytes 1179656 | tf_op jit(solution)/shard_map/ppermute | solution.py:132
  18.5 1.9 %copy-start = (f32[4]{0:T(128)S(1)}, f32[4]{0:T(128)}, u32[]{:S(2)}) copy-start(f32[4]{0:T(128)} %rate_ref.5) | copy-start | bytes 52
  18.6 1.8 %collective-permute-start.6 = (bf16[32,6144]{1,0:T(8,128)(2,1)S(1)}, bf16[32,6144]{1,0:T(8,128)(2,1)S(1)}, u32[]{:S(2)}, u32[]{:S(2)}) collective-permute-start(bf16[32,6144]{1,0:T(8,128)(2,1)S(1)} %tie.3.refs_2_), channel_id=1, source_target_pairs={{0,1},{1,0},{2,3},{3,2},{4,5},{5,4},{6,7},{7,6},{8,9},{9,8},{10,11... | collective-permute-start | bytes 1179656 | tf_op jit(solution)/shard_map/ppermute | solution.py:132
  23.1 12.1 %copy-start.1 = (f32[512]{0:T(512)S(1)}, f32[512]{0:T(512)}, u32[]{:S(2)}) copy-start(f32[512]{0:T(512)} %param.8) | copy-start | bytes 6148
  23.1 9.3 %collective-permute-start.7 = (bf16[4,128,128]{2,1,0:T(8,128)(2,1)S(1)}, bf16[4,128,128]{2,1,0:T(8,128)(2,1)S(1)}, u32[]{:S(2)}, u32[]{:S(2)}) collective-permute-start(bf16[4,128,128]{2,1,0:T(8,128)(2,1)S(1)} %get-tuple-element.51), channel_id=1, source_target_pairs={{0,8},{8,16},{16,24},{24,0},{1,9},{9,17},{17,25},{25,1},{2,10},{10... | collective-permute-start | bytes 393224 | tf_op jit(solution)/shard_map/ppermute | solution.py:573
  24.5 10.7 %collective-permute-start.8 = (bf16[4,128,128]{2,1,0:T(8,128)(2,1)S(1)}, bf16[4,128,128]{2,1,0:T(8,128)(2,1)S(1)}, u32[]{:S(2)}, u32[]{:S(2)}) collective-permute-start(bf16[4,128,128]{2,1,0:T(8,128)(2,1)S(1)} %get-tuple-element.51), channel_id=1, source_target_pairs={{0,16},{8,24},{1,17},{9,25},{2,18},{10,26},{3,19},{11,27},{4,20},{... | collective-permute-start | bytes 393224 | tf_op jit(solution)/shard_map/ppermute | solution.py:574
  27.5 7.6 %collective-permute-start.9 = (bf16[4,128,128]{2,1,0:T(8,128)(2,1)S(1)}, bf16[4,128,128]{2,1,0:T(8,128)(2,1)S(1)}, u32[]{:S(2)}, u32[]{:S(2)}) collective-permute-start(bf16[4,128,128]{2,1,0:T(8,128)(2,1)S(1)} %get-tuple-element.51), channel_id=1, source_target_pairs={{0,24},{1,25},{2,26},{3,27},{4,28},{5,29},{6,30},{7,31}} | collective-permute-start | bytes 393224 | tf_op jit(solution)/shard_map/ppermute | solution.py:576
  36.3 2.7 %collective-permute-start.10 = (bf16[128,512]{1,0:T(8,128)(2,1)S(1)}, bf16[128,512]{1,0:T(8,128)(2,1)S(1)}, u32[]{:S(2)}, u32[]{:S(2)}) collective-permute-start(bf16[128,512]{1,0:T(8,128)(2,1)S(1)} %get-tuple-element.54), channel_id=1, source_target_pairs={{0,1},{1,0},{2,3},{3,2},{4,5},{5,4},{6,7},{7,6},{8,9},{9,8},{10,11... | collective-permute-start | bytes 393224 | tf_op jit(solution)/shard_map/ppermute | solution.py:132
  40.1 7.0 %collective-permute-start.13 = (bf16[32,6144]{1,0:T(8,128)(2,1)S(1)}, bf16[32,6144]{1,0:T(8,128)(2,1)S(1)}, u32[]{:S(2)}, u32[]{:S(2)}) collective-permute-start(bf16[32,6144]{1,0:T(8,128)(2,1)S(1)} %get-tuple-element.58), channel_id=1, source_target_pairs={{0,4},{1,3},{2,6},{3,1},{4,0},{5,7},{6,2},{7,5},{8,12},{9,11},{10,... | collective-permute-start | bytes 1179656 | tf_op jit(solution)/shard_map/ppermute | solution.py:132
  41.2 10.0 %collective-permute-start.12 = (bf16[32,6144]{1,0:T(8,128)(2,1)S(1)}, bf16[32,6144]{1,0:T(8,128)(2,1)S(1)}, u32[]{:S(2)}, u32[]{:S(2)}) collective-permute-start(bf16[32,6144]{1,0:T(8,128)(2,1)S(1)} %get-tuple-element.56), channel_id=1, source_target_pairs={{0,4},{1,3},{2,6},{3,1},{4,0},{5,7},{6,2},{7,5},{8,12},{9,11},{10,... | collective-permute-start | bytes 1179656 | tf_op jit(solution)/shard_map/ppermute | solution.py:132
  47.1 8.9 %collective-permute-start.14 = (bf16[32,6144]{1,0:T(8,128)(2,1)S(1)}, bf16[32,6144]{1,0:T(8,128)(2,1)S(1)}, u32[]{:S(2)}, u32[]{:S(2)}) collective-permute-start(bf16[32,6144]{1,0:T(8,128)(2,1)S(1)} %add_convert_fusion.1), channel_id=1, source_target_pairs={{0,2},{1,5},{2,0},{3,7},{4,6},{5,1},{6,4},{7,3},{8,10},{9,13},{10,... | collective-permute-start | bytes 1179656 | tf_op jit(solution)/shard_map/ppermute | solution.py:132

commit v6 on v5

--- a/solution.py
+++ b/solution.py
@@ -543,7 +543,7 @@
     rows = tokens.shape[0]
     heads = decay_rate.shape[0]
 
-    cuts = [proj_weight.shape[0] // STEP * part // 8 * STEP for part in (0, 3, 6)]
+    cuts = [proj_weight.shape[0] // STEP * part // 24 * STEP for part in (0, 10, 18)]
     w_other = hop(out_weight, CORE)
     first = hop(tokens, FIRST)
     outs = [

time: 57.8 us -> 57.5 us (level)
    ppermute x12, starting transfers between devices: 10.8 us -> 11.4 us  [hop(): return lax.ppermute(value, 'tp', pairs)]
where the time goes in v6:
time: 57.5 us; the launch traced here: 56.5 us
  Pallas kernels  22.9 us (40%)
  starting transfers between devices  16.5 us (29%)
  waiting for transfers between devices  16 us (28%)
  other arithmetic  0.95 us (2%)
    ppermute x12, waiting for transfers between devices, hop(): return lax.ppermute(value, 'tp', pairs)  13.2 us
    ppermute x12, starting transfers between devices, hop(): return lax.ppermute(value, 'tp', pairs)  11.4 us
    pallas_call x2, Pallas kernels, prep(): pl.pallas_call(functools.partial(prep_kernel, first, last, bool(turned)),...  8.35 us
    pallas_call x1, Pallas kernels, project_near(): pl.pallas_call(functools.partial(near_kernel, len(rows), first), in_specs...  3.65 us
    ppermute x1, starting transfers between devices, paired_device(): lax.ppermute(states, 'seq', [(0, 2), (1, 3)])  2.93 us
    ppermute x1, waiting for transfers between devices, paired_device(): lax.ppermute(states, 'seq', [(0, 2), (1, 3)])  2.8 us
    pallas_call x1, Pallas kernels, gates(): pl.pallas_call(gates_kernel, in_specs=[VMEM, VMEM, HBM], out_specs=[VMEM]...  2.8 us
    pallas_call x1, Pallas kernels, project_far(): pl.pallas_call(functools.partial(far_kernel, len(rows)), in_specs=[SMEM]...  2.67 us
  transfers between devices with their start and end apart: 15, of which 5 were waited for; matrix products, arithmetic and copies ran while one was open for 0% of the time, Pallas kernels for 39%

profile of v6, /device:TPU:9, one launch (start us, length us, event | category | flops | bytes accessed | tf_op | source)
XLA Modules:
  0.0 56.5 jit_solution(5661699253310557086)
XLA Ops:
  0.0 0.7 %collective-permute-start.11 = (bf16[512,6144]{1,0:T(8,128)(2,1)}, bf16[512,6144]{1,0:T(8,128)(2,1)S(1)}, u32[]{:S(2)}, u32[]{:S(2)}) collective-permute-start(bf16[512,6144]{1,0:T(8,128)(2,1)} %w_hbm.5), channel_id=1, source_target_pairs={{0,1},{1,0},{2,3},{3,2},{4,5},{5,4},{6,7},{7,6},{8,9},{9,8},{10,11... | collective-permute-start | bytes 18874376 | tf_op jit(solution)/shard_map/ppermute | solution.py:132
  0.7 1.2 %collective-permute-start.1 = (bf16[32,6144]{1,0:T(8,128)(2,1)}, bf16[32,6144]{1,0:T(8,128)(2,1)S(1)}, u32[]{:S(2)}, u32[]{:S(2)}) collective-permute-start(bf16[32,6144]{1,0:T(8,128)(2,1)} %pass_ref.3), channel_id=1, source_target_pairs={{0,2},{1,5},{2,0},{3,7},{4,6},{5,1},{6,4},{7,3},{8,10},{9,13},{10,... | collective-permute-start | bytes 1179656 | tf_op jit(solution)/shard_map/ppermute | solution.py:132
  1.9 4.6 %prep_a.1 = (bf16[6144,1024]{1,0:T(8,128)(2,1)S(1)}, bf16[6144,1024]{1,0:T(8,128)(2,1)S(1)}, bf16[32,6144]{1,0:T(8,128)(2,1)S(1)}, f32[256,1]{1,0:T(8,128)S(1)}, f32[1,256]{1,0:T(1,128)S(1)}) custom-call(bf16[6144,4,512]{2,1,0:T(4,128)(2,1)} %refs_4_.1, bf16[32,6144]{1,0:T(8,128)(2,1)} %pass_ref.3), custom_call_target="tpu_custom_call" | custom-call | bytes 20971520 | tf_op jit(solution)/shard_map/prep_a/pallas_call | solution.py:240
  6.6 1.3 %collective-permute-start.2 = (bf16[32,6144]{1,0:T(8,128)(2,1)S(1)}, bf16[32,6144]{1,0:T(8,128)(2,1)S(1)}, u32[]{:S(2)}, u32[]{:S(2)}) collective-permute-start(bf16[32,6144]{1,0:T(8,128)(2,1)S(1)} %get-tuple-element.34.refs_0_), channel_id=1, source_target_pairs={{0,4},{1,3},{2,6},{3,1},{4,0},{5,7},{6,2},{7,5},{8,12},{9,11},{10,... | collective-permute-start | bytes 1179656 | tf_op jit(solution)/shard_map/ppermute | solution.py:132
  7.8 0.6 %collective-permute-start = (bf16[32,6144]{1,0:T(8,128)(2,1)S(1)}, bf16[32,6144]{1,0:T(8,128)(2,1)S(1)}, u32[]{:S(2)}, u32[]{:S(2)}) collective-permute-start(bf16[32,6144]{1,0:T(8,128)(2,1)S(1)} %copy-done.2), channel_id=1, source_target_pairs={{0,1},{1,0},{2,3},{3,2},{4,5},{5,4},{6,7},{7,6},{8,9},{9,8},{10,11... | collective-permute-start | bytes 1179656 | tf_op jit(solution)/shard_map/ppermute | solution.py:132
  8.5 0.5 collective-permute-start.5
  9.0 3.7 %prep_b.1 = (bf16[6144,1024]{1,0:T(8,128)(2,1)S(1)}, bf16[6144,1024]{1,0:T(8,128)(2,1)S(1)}) custom-call(bf16[6144,4,512]{2,1,0:T(4,128)(2,1)} %refs_4_.1, bf16[32,6144]{1,0:T(8,128)(2,1)} %pass_ref.3, bf16[6144,1024]{1,0:T(8,128)(2,1)S(1)} %get-tuple-element.35.refs_0_, ...), custom_call_target="tpu_custom_call", output_to_operand_aliasing={{0}: (2, {}), {1}: (3, {})} | custom-call | bytes 16777216 | tf_op jit(solution)/shard_map/prep_b/pallas_call | solution.py:240
  12.7 1.3 %collective-permute-start.3 = (bf16[32,6144]{1,0:T(8,128)(2,1)S(1)}, bf16[32,6144]{1,0:T(8,128)(2,1)S(1)}, u32[]{:S(2)}, u32[]{:S(2)}) collective-permute-start(bf16[32,6144]{1,0:T(8,128)(2,1)S(1)} %tie.2.refs_2_), channel_id=1, source_target_pairs={{0,1},{1,0},{2,3},{3,2},{4,5},{5,4},{6,7},{7,6},{8,9},{9,8},{10,11... | collective-permute-start | bytes 1179656 | tf_op jit(solution)/shard_map/ppermute | solution.py:132
  14.0 0.7 %collective-permute-start.4 = (bf16[32,6144]{1,0:T(8,128)(2,1)S(1)}, bf16[32,6144]{1,0:T(8,128)(2,1)S(1)}, u32[]{:S(2)}, u32[]{:S(2)}) collective-permute-start(bf16[32,6144]{1,0:T(8,128)(2,1)S(1)} %collective-permute-done.2.refs_3_), channel_id=1, source_target_pairs={{0,1},{1,0},{2,3},{3,2},{4,5},{5,4},{6,7},{7,6},{8,9},{9,8},{10,11... | collective-permute-start | bytes 1179656 | tf_op jit(solution)/shard_map/ppermute | solution.py:132
  14.7 3.6 %project_near.1 = (bf16[6144,1024]{1,0:T(8,128)(2,1)S(1)}, bf16[6144,1024]{1,0:T(8,128)(2,1)S(1)}, bf16[256,6144]{1,0:T(8,128)(2,1)S(1)}, bf16[128,512]{1,0:T(8,128)(2,1)S(1)}, bf16[128,512]{1,0:T(8,128)(2,1)S(1)}) custom-call(bf16[32,6144]{1,0:T(8,128)(2,1)S(1)} %get-tuple-element.34.refs_0_, ...), custom_call_target="tpu_custom_call", output_to_operand_aliasing={{0}: (5, {}), {1}: (6, {})} | custom-call | flops 3221225472 | bytes 50331648 | tf_op jit(solution)/shard_map/project_near/pallas_call | solution.py:299
  18.4 0.5 collective-permute-start.6
  18.9 1.0 %early.1 = (bf16[256,6144]{1,0:T(8,128)(2,1)S(1)}, bf16[128,512]{1,0:T(8,128)(2,1)S(1)}) custom-call(bf16[256,6144]{1,0:T(8,128)(2,1)S(1)} %get-tuple-element.39._, bf16[6144,1024]{1,0:T(8,128)(2,1)S(1)} %get-tuple-element.40.qg), custom_call_target="tpu_custom_call", output_to_operand_aliasing={{0}: (0, {})} | custom-call | flops 805306368 | bytes 6291456 | tf_op jit(solution)/shard_map/early/pallas_call | solution.py:388
  20.0 0.3 collective-permute-done.6.refs_3_
  20.3 2.7 %project_far.1 = (bf16[256,6144]{1,0:T(8,128)(2,1)S(1)}, bf16[128,512]{1,0:T(8,128)(2,1)S(1)}, bf16[128,512]{1,0:T(8,128)(2,1)S(1)}, bf16[4,128,128]{2,1,0:T(8,128)(2,1)S(1)}) custom-call(f32[4]{0:T(128)S(1)} %copy-done, f32[256,1]{1,0:T(8,128)S(1)} %get-tuple-element.32.refs_1_.place_ref, ...), custom_call_target="tpu_custom_call", output_to_operand_aliasing={{0}: (5, {})} | custom-call | flops 1610612736 | bytes 12582912 | tf_op jit(solution)/shard_map/project_far/pallas_call | solution.py:347
  23.0 1.4 %collective-permute-start.7 = (bf16[4,128,128]{2,1,0:T(8,128)(2,1)S(1)}, bf16[4,128,128]{2,1,0:T(8,128)(2,1)S(1)}, u32[]{:S(2)}, u32[]{:S(2)}) collective-permute-start(bf16[4,128,128]{2,1,0:T(8,128)(2,1)S(1)} %get-tuple-element.51), channel_id=1, source_target_pairs={{0,8},{8,16},{16,24},{24,0},{1,9},{9,17},{17,25},{25,1},{2,10},{10... | collective-permute-start | bytes 393224 | tf_op jit(solution)/shard_map/ppermute | solution.py:573
  24.3 2.9 %collective-permute-start.8 = (bf16[4,128,128]{2,1,0:T(8,128)(2,1)S(1)}, bf16[4,128,128]{2,1,0:T(8,128)(2,1)S(1)}, u32[]{:S(2)}, u32[]{:S(2)}) collective-permute-start(bf16[4,128,128]{2,1,0:T(8,128)(2,1)S(1)} %get-tuple-element.51), channel_id=1, source_target_pairs={{0,16},{8,24},{1,17},{9,25},{2,18},{10,26},{3,19},{11,27},{4,20},{... | collective-permute-start | bytes 393224 | tf_op jit(solution)/shard_map/ppermute | solution.py:574
  27.3 0.8 %collective-permute-start.9 = (bf16[4,128,128]{2,1,0:T(8,128)(2,1)S(1)}, bf16[4,128,128]{2,1,0:T(8,128)(2,1)S(1)}, u32[]{:S(2)}, u32[]{:S(2)}) collective-permute-start(bf16[4,128,128]{2,1,0:T(8,128)(2,1)S(1)} %get-tuple-element.51), channel_id=1, source_target_pairs={{0,24},{1,25},{2,26},{3,27},{4,28},{5,29},{6,30},{7,31}} | collective-permute-start | bytes 393224 | tf_op jit(solution)/shard_map/ppermute | solution.py:576
  28.1 2.8 %gates.1 = (bf16[128,512]{1,0:T(8,128)(2,1)S(1)}, f32[256,512]{1,0:T(8,128)S(1)}, bf16[512,6144]{1,0:T(8,128)(2,1)S(1)}) custom-call(bf16[256,6144]{1,0:T(8,128)(2,1)S(1)} %get-tuple-element.46.x_all, bf16[6144,1024]{1,0:T(8,128)(2,1)S(1)} %get-tuple-element.40.qg, bf16[512,6144]{1,0:T(8,128)(2,1)} %w_hbm.5), custom_call_target="tpu_custom_call" | custom-call | flops 2415919104 | bytes 25165824 | tf_op jit(solution)/shard_map/gates/pallas_call | solution.py:415
  30.9 1.2 %inner.1.in_ref = f32[256,512]{1,0:T(8,128)S(1)} custom-call(f32[4]{0:T(128)S(1)} %copy-done, f32[256,1]{1,0:T(8,128)S(1)} %get-tuple-element.32.refs_1_.place_ref, f32[1,256]{1,0:T(1,128)S(1)} %get-tuple-element.33.across_ref, bf16[128,512]{1,0:T(8,128)(2,1)S(1)} %get-tuple-element.41.q0, bf16[128,512]{1,0:T(8,128)(2,1)S(1)} %get-tuple-element.47.q1, ...), custom_call_target="tpu_custom_call" | custom-call | tf_op jit(solution)/shard_map/inner/pallas_call | solution.py:478
  32.2 2.8 %collective-permute-done.8.s2 = bf16[4,128,128]{2,1,0:T(8,128)(2,1)S(1)} collective-permute-done((bf16[4,128,128]{2,1,0:T(8,128)(2,1)S(1)}, bf16[4,128,128]{2,1,0:T(8,128)(2,1)S(1)}, u32[]{:S(2)}, u32[]{:S(2)}) %collective-permute-start.8) | collective-permute-done | bytes 131104 | tf_op jit(solution)/shard_map/ppermute | solution.py:574
  35.0 1.1 %finish.1 = (bf16[128,512]{1,0:T(8,128)(2,1)S(1)}, bf16[128,512]{1,0:T(8,128)(2,1)S(1)}) custom-call(f32[4]{0:T(128)S(1)} %copy-done, f32[256,1]{1,0:T(8,128)S(1)} %get-tuple-element.32.refs_1_.place_ref, f32[1,512]{1,0:T(1,128)S(1)} %bitcast.1, f32[256,512]{1,0:T(8,128)S(1)} %inner.1.in_ref, bf16[128,512]{1,0:T(8,128)(2,1)S(1)} %get-tuple-element.41.q0, ...), custom_call_target="tpu_custom_call" | custom-call | tf_op jit(solution)/shard_map/finish/pallas_call | solution.py:478
  36.1 1.6 %collective-permute-start.10 = (bf16[128,512]{1,0:T(8,128)(2,1)S(1)}, bf16[128,512]{1,0:T(8,128)(2,1)S(1)}, u32[]{:S(2)}, u32[]{:S(2)}) collective-permute-start(bf16[128,512]{1,0:T(8,128)(2,1)S(1)} %get-tuple-element.54), channel_id=1, source_target_pairs={{0,1},{1,0},{2,3},{3,2},{4,5},{5,4},{6,7},{7,6},{8,9},{9,8},{10,11... | collective-permute-start | bytes 393224 | tf_op jit(solution)/shard_map/ppermute | solution.py:132
  37.8 1.0 %out_own.1.own_ref = f32[128,6144]{1,0:T(8,128)S(1)} custom-call(bf16[128,512]{1,0:T(8,128)(2,1)S(1)} %get-tuple-element.52.y_ref, bf16[512,6144]{1,0:T(8,128)(2,1)S(1)} %get-tuple-element.53.w_ref), custom_call_target="tpu_custom_call" | custom-call | flops 805306368 | bytes 6291456 | tf_op jit(solution)/shard_map/out_own/pallas_call | solution.py:498
  38.8 1.0 %out_rows.1 = (bf16[32,6144]{1,0:T(8,128)(2,1)S(1)}, f32[32,6144]{1,0:T(8,128)S(1)}, bf16[32,6144]{1,0:T(8,128)(2,1)S(1)}, f32[32,6144]{1,0:T(8,128)S(1)}) custom-call(f32[128,6144]{1,0:T(8,128)S(1)} %out_own.1.own_ref, bf16[128,512]{1,0:T(8,128)(2,1)S(1)} %collective-permute-done.10.z_ref, bf16[512,6144]{1,0:T(8,128)(2,1)S(1)} %collective-permute-done.11.u_ref), custom_call_target="tpu_custom_call" | custom-call | flops 805306368 | bytes 6291456 | tf_op jit(solution)/shard_map/out_rows/pallas_call | solution.py:527
  39.8 0.7 %collective-permute-start.13 = (bf16[32,6144]{1,0:T(8,128)(2,1)S(1)}, bf16[32,6144]{1,0:T(8,128)(2,1)S(1)}, u32[]{:S(2)}, u32[]{:S(2)}) collective-permute-start(bf16[32,6144]{1,0:T(8,128)(2,1)S(1)} %get-tuple-element.58), channel_id=1, source_target_pairs={{0,4},{1,3},{2,6},{3,1},{4,0},{5,7},{6,2},{7,5},{8,12},{9,11},{10,... | collective-permute-start | bytes 1179656 | tf_op jit(solution)/shard_map/ppermute | solution.py:132
  40.5 0.9 %collective-permute-start.12 = (bf16[32,6144]{1,0:T(8,128)(2,1)S(1)}, bf16[32,6144]{1,0:T(8,128)(2,1)S(1)}, u32[]{:S(2)}, u32[]{:S(2)}) collective-permute-start(bf16[32,6144]{1,0:T(8,128)(2,1)S(1)} %get-tuple-element.56), channel_id=1, source_target_pairs={{0,4},{1,3},{2,6},{3,1},{4,0},{5,7},{6,2},{7,5},{8,12},{9,11},{10,... | collective-permute-start | bytes 1179656 | tf_op jit(solution)/shard_map/ppermute | solution.py:132
  41.3 5.5 %collective-permute-done.13 = bf16[32,6144]{1,0:T(8,128)(2,1)S(1)} collective-permute-done((bf16[32,6144]{1,0:T(8,128)(2,1)S(1)}, bf16[32,6144]{1,0:T(8,128)(2,1)S(1)}, u32[]{:S(2)}, u32[]{:S(2)}) %collective-permute-start.13) | collective-permute-done | bytes 393248 | tf_op jit(solution)/shard_map/ppermute | solution.py:132
  46.8 0.1 add_convert_fusion.1
  46.9 1.3 %collective-permute-start.14 = (bf16[32,6144]{1,0:T(8,128)(2,1)S(1)}, bf16[32,6144]{1,0:T(8,128)(2,1)S(1)}, u32[]{:S(2)}, u32[]{:S(2)}) collective-permute-start(bf16[32,6144]{1,0:T(8,128)(2,1)S(1)} %add_convert_fusion.1), channel_id=1, source_target_pairs={{0,2},{1,5},{2,0},{3,7},{4,6},{5,1},{6,4},{7,3},{8,10},{9,13},{10,... | collective-permute-start | bytes 1179656 | tf_op jit(solution)/shard_map/ppermute | solution.py:132
  48.2 2.8 %collective-permute-done.12 = bf16[32,6144]{1,0:T(8,128)(2,1)S(1)} collective-permute-done((bf16[32,6144]{1,0:T(8,128)(2,1)S(1)}, bf16[32,6144]{1,0:T(8,128)(2,1)S(1)}, u32[]{:S(2)}, u32[]{:S(2)}) %collective-permute-start.12) | collective-permute-done | bytes 393248 | tf_op jit(solution)/shard_map/ppermute | solution.py:132
  51.1 4.6 %collective-permute-done.14 = bf16[32,6144]{1,0:T(8,128)(2,1)S(1)} collective-permute-done((bf16[32,6144]{1,0:T(8,128)(2,1)S(1)}, bf16[32,6144]{1,0:T(8,128)(2,1)S(1)}, u32[]{:S(2)}, u32[]{:S(2)}) %collective-permute-start.14) | collective-permute-done | bytes 393248 | tf_op jit(solution)/shard_map/ppermute | solution.py:132
  55.7 0.8 %add_convert_fusion = bf16[32,6144]{1,0:T(8,128)(2,1)} fusion(f32[32,6144]{1,0:T(8,128)S(1)} %convert_add_fusion, bf16[32,6144]{1,0:T(8,128)(2,1)S(1)} %collective-permute-done.14), kind=kLoop, calls=%fused_computation | loop fusion | flops 589824 | bytes 1572864 | tf_op jit(solution)/shard_map/convert_element_type | solution.py:594
  (19 shorter events, 0.1 us)
Async XLA Ops:
  0.0 7.8 %copy-start.2 = (bf16[32,6144]{1,0:T(8,128)(2,1)S(1)}, bf16[32,6144]{1,0:T(8,128)(2,1)}, u32[]{:S(2)}) copy-start(bf16[32,6144]{1,0:T(8,128)(2,1)} %pass_ref.3) | copy-start | bytes 1179652
  0.0 38.8 %collective-permute-start.11 = (bf16[512,6144]{1,0:T(8,128)(2,1)}, bf16[512,6144]{1,0:T(8,128)(2,1)S(1)}, u32[]{:S(2)}, u32[]{:S(2)}) collective-permute-start(bf16[512,6144]{1,0:T(8,128)(2,1)} %w_hbm.5), channel_id=1, source_target_pairs={{0,1},{1,0},{2,3},{3,2},{4,5},{5,4},{6,7},{7,6},{8,9},{9,8},{10,11... | collective-permute-start | bytes 18874376 | tf_op jit(solution)/shard_map/ppermute | solution.py:132
  0.7 7.8 %collective-permute-start.1 = (bf16[32,6144]{1,0:T(8,128)(2,1)}, bf16[32,6144]{1,0:T(8,128)(2,1)S(1)}, u32[]{:S(2)}, u32[]{:S(2)}) collective-permute-start(bf16[32,6144]{1,0:T(8,128)(2,1)} %pass_ref.3), channel_id=1, source_target_pairs={{0,2},{1,5},{2,0},{3,7},{4,6},{5,1},{6,4},{7,3},{8,10},{9,13},{10,... | collective-permute-start | bytes 1179656 | tf_op jit(solution)/shard_map/ppermute | solution.py:132
  6.6 7.5 %collective-permute-start.2 = (bf16[32,6144]{1,0:T(8,128)(2,1)S(1)}, bf16[32,6144]{1,0:T(8,128)(2,1)S(1)}, u32[]{:S(2)}, u32[]{:S(2)}) collective-permute-start(bf16[32,6144]{1,0:T(8,128)(2,1)S(1)} %get-tuple-element.34.refs_0_), channel_id=1, source_target_pairs={{0,4},{1,3},{2,6},{3,1},{4,0},{5,7},{6,2},{7,5},{8,12},{9,11},{10,... | collective-permute-start | bytes 1179656 | tf_op jit(solution)/shard_map/ppermute | solution.py:132
  7.8 6.9 %collective-permute-start = (bf16[32,6144]{1,0:T(8,128)(2,1)S(1)}, bf16[32,6144]{1,0:T(8,128)(2,1)S(1)}, u32[]{:S(2)}, u32[]{:S(2)}) collective-permute-start(bf16[32,6144]{1,0:T(8,128)(2,1)S(1)} %copy-done.2), channel_id=1, source_target_pairs={{0,1},{1,0},{2,3},{3,2},{4,5},{5,4},{6,7},{7,6},{8,9},{9,8},{10,11... | collective-permute-start | bytes 1179656 | tf_op jit(solution)/shard_map/ppermute | solution.py:132
  8.5 9.9 %collective-permute-start.5 = (bf16[32,6144]{1,0:T(8,128)(2,1)S(1)}, bf16[32,6144]{1,0:T(8,128)(2,1)S(1)}, u32[]{:S(2)}, u32[]{:S(2)}) collective-permute-start(bf16[32,6144]{1,0:T(8,128)(2,1)S(1)} %tie.2.refs_2_), channel_id=1, source_target_pairs={{0,4},{1,3},{2,6},{3,1},{4,0},{5,7},{6,2},{7,5},{8,12},{9,11},{10,... | collective-permute-start | bytes 1179656 | tf_op jit(solution)/shard_map/ppermute | solution.py:132
  12.7 7.2 %collective-permute-start.3 = (bf16[32,6144]{1,0:T(8,128)(2,1)S(1)}, bf16[32,6144]{1,0:T(8,128)(2,1)S(1)}, u32[]{:S(2)}, u32[]{:S(2)}) collective-permute-start(bf16[32,6144]{1,0:T(8,128)(2,1)S(1)} %tie.2.refs_2_), channel_id=1, source_target_pairs={{0,1},{1,0},{2,3},{3,2},{4,5},{5,4},{6,7},{7,6},{8,9},{9,8},{10,11... | collective-permute-start | bytes 1179656 | tf_op jit(solution)/shard_map/ppermute | solution.py:132
  14.0 6.0 %collective-permute-start.4 = (bf16[32,6144]{1,0:T(8,128)(2,1)S(1)}, bf16[32,6144]{1,0:T(8,128)(2,1)S(1)}, u32[]{:S(2)}, u32[]{:S(2)}) collective-permute-start(bf16[32,6144]{1,0:T(8,128)(2,1)S(1)} %collective-permute-done.2.refs_3_), channel_id=1, source_target_pairs={{0,1},{1,0},{2,3},{3,2},{4,5},{5,4},{6,7},{7,6},{8,9},{9,8},{10,11... | collective-permute-start | bytes 1179656 | tf_op jit(solution)/shard_map/ppermute | solution.py:132
  18.4 1.9 %copy-start = (f32[4]{0:T(128)S(1)}, f32[4]{0:T(128)}, u32[]{:S(2)}) copy-start(f32[4]{0:T(128)} %rate_ref.5) | copy-start | bytes 52
  18.4 1.9 %collective-permute-start.6 = (bf16[32,6144]{1,0:T(8,128)(2,1)S(1)}, bf16[32,6144]{1,0:T(8,128)(2,1)S(1)}, u32[]{:S(2)}, u32[]{:S(2)}) collective-permute-start(bf16[32,6144]{1,0:T(8,128)(2,1)S(1)} %tie.3.refs_2_), channel_id=1, source_target_pairs={{0,1},{1,0},{2,3},{3,2},{4,5},{5,4},{6,7},{7,6},{8,9},{9,8},{10,11... | collective-permute-start | bytes 1179656 | tf_op jit(solution)/shard_map/ppermute | solution.py:132
  23.0 12.0 %copy-start.1 = (f32[512]{0:T(512)S(1)}, f32[512]{0:T(512)}, u32[]{:S(2)}) copy-start(f32[512]{0:T(512)} %param.8) | copy-start | bytes 6148
  23.0 9.2 %collective-permute-start.7 = (bf16[4,128,128]{2,1,0:T(8,128)(2,1)S(1)}, bf16[4,128,128]{2,1,0:T(8,128)(2,1)S(1)}, u32[]{:S(2)}, u32[]{:S(2)}) collective-permute-start(bf16[4,128,128]{2,1,0:T(8,128)(2,1)S(1)} %get-tuple-element.51), channel_id=1, source_target_pairs={{0,8},{8,16},{16,24},{24,0},{1,9},{9,17},{17,25},{25,1},{2,10},{10... | collective-permute-start | bytes 393224 | tf_op jit(solution)/shard_map/ppermute | solution.py:573
  24.3 10.7 %collective-permute-start.8 = (bf16[4,128,128]{2,1,0:T(8,128)(2,1)S(1)}, bf16[4,128,128]{2,1,0:T(8,128)(2,1)S(1)}, u32[]{:S(2)}, u32[]{:S(2)}) collective-permute-start(bf16[4,128,128]{2,1,0:T(8,128)(2,1)S(1)} %get-tuple-element.51), channel_id=1, source_target_pairs={{0,16},{8,24},{1,17},{9,25},{2,18},{10,26},{3,19},{11,27},{4,20},{... | collective-permute-start | bytes 393224 | tf_op jit(solution)/shard_map/ppermute | solution.py:574
  27.3 7.7 %collective-permute-start.9 = (bf16[4,128,128]{2,1,0:T(8,128)(2,1)S(1)}, bf16[4,128,128]{2,1,0:T(8,128)(2,1)S(1)}, u32[]{:S(2)}, u32[]{:S(2)}) collective-permute-start(bf16[4,128,128]{2,1,0:T(8,128)(2,1)S(1)} %get-tuple-element.51), channel_id=1, source_target_pairs={{0,24},{1,25},{2,26},{3,27},{4,28},{5,29},{6,30},{7,31}} | collective-permute-start | bytes 393224 | tf_op jit(solution)/shard_map/ppermute | solution.py:576
  36.1 2.6 %collective-permute-start.10 = (bf16[128,512]{1,0:T(8,128)(2,1)S(1)}, bf16[128,512]{1,0:T(8,128)(2,1)S(1)}, u32[]{:S(2)}, u32[]{:S(2)}) collective-permute-start(bf16[128,512]{1,0:T(8,128)(2,1)S(1)} %get-tuple-element.54), channel_id=1, source_target_pairs={{0,1},{1,0},{2,3},{3,2},{4,5},{5,4},{6,7},{7,6},{8,9},{9,8},{10,11... | collective-permute-start | bytes 393224 | tf_op jit(solution)/shard_map/ppermute | solution.py:132
  39.8 7.0 %collective-permute-start.13 = (bf16[32,6144]{1,0:T(8,128)(2,1)S(1)}, bf16[32,6144]{1,0:T(8,128)(2,1)S(1)}, u32[]{:S(2)}, u32[]{:S(2)}) collective-permute-start(bf16[32,6144]{1,0:T(8,128)(2,1)S(1)} %get-tuple-element.58), channel_id=1, source_target_pairs={{0,4},{1,3},{2,6},{3,1},{4,0},{5,7},{6,2},{7,5},{8,12},{9,11},{10,... | collective-permute-start | bytes 1179656 | tf_op jit(solution)/shard_map/ppermute | solution.py:132
  40.5 10.5 %collective-permute-start.12 = (bf16[32,6144]{1,0:T(8,128)(2,1)S(1)}, bf16[32,6144]{1,0:T(8,128)(2,1)S(1)}, u32[]{:S(2)}, u32[]{:S(2)}) collective-permute-start(bf16[32,6144]{1,0:T(8,128)(2,1)S(1)} %get-tuple-element.56), channel_id=1, source_target_pairs={{0,4},{1,3},{2,6},{3,1},{4,0},{5,7},{6,2},{7,5},{8,12},{9,11},{10,... | collective-permute-start | bytes 1179656 | tf_op jit(solution)/shard_map/ppermute | solution.py:132
  46.9 8.9 %collective-permute-start.14 = (bf16[32,6144]{1,0:T(8,128)(2,1)S(1)}, bf16[32,6144]{1,0:T(8,128)(2,1)S(1)}, u32[]{:S(2)}, u32[]{:S(2)}) collective-permute-start(bf16[32,6144]{1,0:T(8,128)(2,1)S(1)} %add_convert_fusion.1), channel_id=1, source_target_pairs={{0,2},{1,5},{2,0},{3,7},{4,6},{5,1},{6,4},{7,3},{8,10},{9,13},{10,... | collective-permute-start | bytes 1179656 | tf_op jit(solution)/shard_map/ppermute | solution.py:132

commit v7 on v6

--- a/solution.py
+++ b/solution.py
@@ -543,7 +543,7 @@
     rows = tokens.shape[0]
     heads = decay_rate.shape[0]
 
-    cuts = [proj_weight.shape[0] // STEP * part // 24 * STEP for part in (0, 10, 18)]
+    cuts = [proj_weight.shape[0] // STEP * part // 24 * STEP for part in (0, 10, 19)]
     w_other = hop(out_weight, CORE)
     first = hop(tokens, FIRST)
     outs = [

time: 57.5 us -> 57.5 us (level)
  transfers between devices with their start and end apart: 15 -> 15, of which waited for: 5 -> 5; matrix products, arithmetic and copies ran while one was open for 0% -> 0% of each run, Pallas kernels for 39% -> 40%
where the time goes in v7:
time: 57.5 us; the launch traced here: 56.5 us
  Pallas kernels  23.3 us (41%)
  starting transfers between devices  16 us (28%)
  waiting for transfers between devices  16 us (28%)
  other arithmetic  0.95 us (2%)
    ppermute x12, waiting for transfers between devices, hop(): return lax.ppermute(value, 'tp', pairs)  13.2 us
    ppermute x12, starting transfers between devices, hop(): return lax.ppermute(value, 'tp', pairs)  10.9 us
    pallas_call x2, Pallas kernels, prep(): pl.pallas_call(functools.partial(prep_kernel, first, last, bool(turned)),...  8.87 us
    pallas_call x1, Pallas kernels, project_near(): pl.pallas_call(functools.partial(near_kernel, len(rows), first), in_specs...  3.6 us
    ppermute x1, starting transfers between devices, paired_device(): lax.ppermute(states, 'seq', [(0, 2), (1, 3)])  2.93 us
    ppermute x1, waiting for transfers between devices, paired_device(): lax.ppermute(states, 'seq', [(0, 2), (1, 3)])  2.8 us
    pallas_call x1, Pallas kernels, gates(): pl.pallas_call(gates_kernel, in_specs=[VMEM, VMEM, HBM], out_specs=[VMEM]...  2.8 us
    pallas_call x1, Pallas kernels, project_far(): pl.pallas_call(functools.partial(far_kernel, len(rows)), in_specs=[SMEM]...  2.67 us
  transfers between devices with their start and end apart: 15, of which 5 were waited for; matrix products, arithmetic and copies ran while one was open for 0% of the time, Pallas kernels for 40%

profile of v7, /device:TPU:9, one launch (start us, length us, event | category | flops | bytes accessed | tf_op | source)
XLA Modules:
  0.0 56.5 jit_solution(8010927346311692079)
XLA Ops:
  0.0 0.7 %collective-permute-start.11 = (bf16[512,6144]{1,0:T(8,128)(2,1)}, bf16[512,6144]{1,0:T(8,128)(2,1)S(1)}, u32[]{:S(2)}, u32[]{:S(2)}) collective-permute-start(bf16[512,6144]{1,0:T(8,128)(2,1)} %w_hbm.5), channel_id=1, source_target_pairs={{0,1},{1,0},{2,3},{3,2},{4,5},{5,4},{6,7},{7,6},{8,9},{9,8},{10,11... | collective-permute-start | bytes 18874376 | tf_op jit(solution)/shard_map/ppermute | solution.py:132
  0.7 1.2 %collective-permute-start.1 = (bf16[32,6144]{1,0:T(8,128)(2,1)}, bf16[32,6144]{1,0:T(8,128)(2,1)S(1)}, u32[]{:S(2)}, u32[]{:S(2)}) collective-permute-start(bf16[32,6144]{1,0:T(8,128)(2,1)} %pass_ref.3), channel_id=1, source_target_pairs={{0,2},{1,5},{2,0},{3,7},{4,6},{5,1},{6,4},{7,3},{8,10},{9,13},{10,... | collective-permute-start | bytes 1179656 | tf_op jit(solution)/shard_map/ppermute | solution.py:132
  1.9 4.6 %prep_a.1 = (bf16[6144,1024]{1,0:T(8,128)(2,1)S(1)}, bf16[6144,1024]{1,0:T(8,128)(2,1)S(1)}, bf16[32,6144]{1,0:T(8,128)(2,1)S(1)}, f32[256,1]{1,0:T(8,128)S(1)}, f32[1,256]{1,0:T(1,128)S(1)}) custom-call(bf16[6144,4,512]{2,1,0:T(4,128)(2,1)} %refs_4_.1, bf16[32,6144]{1,0:T(8,128)(2,1)} %pass_ref.3), custom_call_target="tpu_custom_call" | custom-call | bytes 20971520 | tf_op jit(solution)/shard_map/prep_a/pallas_call | solution.py:240
  6.6 1.3 %collective-permute-start.2 = (bf16[32,6144]{1,0:T(8,128)(2,1)S(1)}, bf16[32,6144]{1,0:T(8,128)(2,1)S(1)}, u32[]{:S(2)}, u32[]{:S(2)}) collective-permute-start(bf16[32,6144]{1,0:T(8,128)(2,1)S(1)} %get-tuple-element.34.refs_0_), channel_id=1, source_target_pairs={{0,4},{1,3},{2,6},{3,1},{4,0},{5,7},{6,2},{7,5},{8,12},{9,11},{10,... | collective-permute-start | bytes 1179656 | tf_op jit(solution)/shard_map/ppermute | solution.py:132
  7.8 0.6 %collective-permute-start = (bf16[32,6144]{1,0:T(8,128)(2,1)S(1)}, bf16[32,6144]{1,0:T(8,128)(2,1)S(1)}, u32[]{:S(2)}, u32[]{:S(2)}) collective-permute-start(bf16[32,6144]{1,0:T(8,128)(2,1)S(1)} %copy-done.2), channel_id=1, source_target_pairs={{0,1},{1,0},{2,3},{3,2},{4,5},{5,4},{6,7},{7,6},{8,9},{9,8},{10,11... | collective-permute-start | bytes 1179656 | tf_op jit(solution)/shard_map/ppermute | solution.py:132
  8.5 0.5 collective-permute-start.5
  9.0 4.2 %prep_b.1 = (bf16[6144,1024]{1,0:T(8,128)(2,1)S(1)}, bf16[6144,1024]{1,0:T(8,128)(2,1)S(1)}) custom-call(bf16[6144,4,512]{2,1,0:T(4,128)(2,1)} %refs_4_.1, bf16[32,6144]{1,0:T(8,128)(2,1)} %pass_ref.3, bf16[6144,1024]{1,0:T(8,128)(2,1)S(1)} %get-tuple-element.35.refs_0_, ...), custom_call_target="tpu_custom_call", output_to_operand_aliasing={{0}: (2, {}), {1}: (3, {})} | custom-call | bytes 18874368 | tf_op jit(solution)/shard_map/prep_b/pallas_call | solution.py:240
  13.3 1.3 %collective-permute-start.3 = (bf16[32,6144]{1,0:T(8,128)(2,1)S(1)}, bf16[32,6144]{1,0:T(8,128)(2,1)S(1)}, u32[]{:S(2)}, u32[]{:S(2)}) collective-permute-start(bf16[32,6144]{1,0:T(8,128)(2,1)S(1)} %tie.2.refs_2_), channel_id=1, source_target_pairs={{0,1},{1,0},{2,3},{3,2},{4,5},{5,4},{6,7},{7,6},{8,9},{9,8},{10,11... | collective-permute-start | bytes 1179656 | tf_op jit(solution)/shard_map/ppermute | solution.py:132
  14.6 0.2 collective-permute-start.4
  14.7 3.6 %project_near.1 = (bf16[6144,1024]{1,0:T(8,128)(2,1)S(1)}, bf16[6144,1024]{1,0:T(8,128)(2,1)S(1)}, bf16[256,6144]{1,0:T(8,128)(2,1)S(1)}, bf16[128,512]{1,0:T(8,128)(2,1)S(1)}, bf16[128,512]{1,0:T(8,128)(2,1)S(1)}) custom-call(bf16[32,6144]{1,0:T(8,128)(2,1)S(1)} %get-tuple-element.34.refs_0_, ...), custom_call_target="tpu_custom_call", output_to_operand_aliasing={{0}: (5, {}), {1}: (6, {})} | custom-call | flops 3221225472 | bytes 50331648 | tf_op jit(solution)/shard_map/project_near/pallas_call | solution.py:299
  18.4 0.6 %collective-permute-start.6 = (bf16[32,6144]{1,0:T(8,128)(2,1)S(1)}, bf16[32,6144]{1,0:T(8,128)(2,1)S(1)}, u32[]{:S(2)}, u32[]{:S(2)}) collective-permute-start(bf16[32,6144]{1,0:T(8,128)(2,1)S(1)} %tie.3.refs_2_), channel_id=1, source_target_pairs={{0,1},{1,0},{2,3},{3,2},{4,5},{5,4},{6,7},{7,6},{8,9},{9,8},{10,11... | collective-permute-start | bytes 1179656 | tf_op jit(solution)/shard_map/ppermute | solution.py:132
  18.9 1.0 %early.1 = (bf16[256,6144]{1,0:T(8,128)(2,1)S(1)}, bf16[128,512]{1,0:T(8,128)(2,1)S(1)}) custom-call(bf16[256,6144]{1,0:T(8,128)(2,1)S(1)} %get-tuple-element.39._, bf16[6144,1024]{1,0:T(8,128)(2,1)S(1)} %get-tuple-element.40.qg), custom_call_target="tpu_custom_call", output_to_operand_aliasing={{0}: (0, {})} | custom-call | flops 805306368 | bytes 6291456 | tf_op jit(solution)/shard_map/early/pallas_call | solution.py:388
  20.0 0.3 collective-permute-done.6.refs_3_
  20.3 2.7 %project_far.1 = (bf16[256,6144]{1,0:T(8,128)(2,1)S(1)}, bf16[128,512]{1,0:T(8,128)(2,1)S(1)}, bf16[128,512]{1,0:T(8,128)(2,1)S(1)}, bf16[4,128,128]{2,1,0:T(8,128)(2,1)S(1)}) custom-call(f32[4]{0:T(128)S(1)} %copy-done, f32[256,1]{1,0:T(8,128)S(1)} %get-tuple-element.32.refs_1_.place_ref, ...), custom_call_target="tpu_custom_call", output_to_operand_aliasing={{0}: (5, {})} | custom-call | flops 1610612736 | bytes 12582912 | tf_op jit(solution)/shard_map/project_far/pallas_call | solution.py:347
  23.0 1.4 %collective-permute-start.7 = (bf16[4,128,128]{2,1,0:T(8,128)(2,1)S(1)}, bf16[4,128,128]{2,1,0:T(8,128)(2,1)S(1)}, u32[]{:S(2)}, u32[]{:S(2)}) collective-permute-start(bf16[4,128,128]{2,1,0:T(8,128)(2,1)S(1)} %get-tuple-element.51), channel_id=1, source_target_pairs={{0,8},{8,16},{16,24},{24,0},{1,9},{9,17},{17,25},{25,1},{2,10},{10... | collective-permute-start | bytes 393224 | tf_op jit(solution)/shard_map/ppermute | solution.py:573
  24.3 2.9 %collective-permute-start.8 = (bf16[4,128,128]{2,1,0:T(8,128)(2,1)S(1)}, bf16[4,128,128]{2,1,0:T(8,128)(2,1)S(1)}, u32[]{:S(2)}, u32[]{:S(2)}) collective-permute-start(bf16[4,128,128]{2,1,0:T(8,128)(2,1)S(1)} %get-tuple-element.51), channel_id=1, source_target_pairs={{0,16},{8,24},{1,17},{9,25},{2,18},{10,26},{3,19},{11,27},{4,20},{... | collective-permute-start | bytes 393224 | tf_op jit(solution)/shard_map/ppermute | solution.py:574
  27.3 0.8 %collective-permute-start.9 = (bf16[4,128,128]{2,1,0:T(8,128)(2,1)S(1)}, bf16[4,128,128]{2,1,0:T(8,128)(2,1)S(1)}, u32[]{:S(2)}, u32[]{:S(2)}) collective-permute-start(bf16[4,128,128]{2,1,0:T(8,128)(2,1)S(1)} %get-tuple-element.51), channel_id=1, source_target_pairs={{0,24},{1,25},{2,26},{3,27},{4,28},{5,29},{6,30},{7,31}} | collective-permute-start | bytes 393224 | tf_op jit(solution)/shard_map/ppermute | solution.py:576
  28.1 2.8 %gates.1 = (bf16[128,512]{1,0:T(8,128)(2,1)S(1)}, f32[256,512]{1,0:T(8,128)S(1)}, bf16[512,6144]{1,0:T(8,128)(2,1)S(1)}) custom-call(bf16[256,6144]{1,0:T(8,128)(2,1)S(1)} %get-tuple-element.46.x_all, bf16[6144,1024]{1,0:T(8,128)(2,1)S(1)} %get-tuple-element.40.qg, bf16[512,6144]{1,0:T(8,128)(2,1)} %w_hbm.5), custom_call_target="tpu_custom_call" | custom-call | flops 2415919104 | bytes 25165824 | tf_op jit(solution)/shard_map/gates/pallas_call | solution.py:415
  30.9 1.2 %inner.1.in_ref = f32[256,512]{1,0:T(8,128)S(1)} custom-call(f32[4]{0:T(128)S(1)} %copy-done, f32[256,1]{1,0:T(8,128)S(1)} %get-tuple-element.32.refs_1_.place_ref, f32[1,256]{1,0:T(1,128)S(1)} %get-tuple-element.33.across_ref, bf16[128,512]{1,0:T(8,128)(2,1)S(1)} %get-tuple-element.41.q0, bf16[128,512]{1,0:T(8,128)(2,1)S(1)} %get-tuple-element.47.q1, ...), custom_call_target="tpu_custom_call" | custom-call | tf_op jit(solution)/shard_map/inner/pallas_call | solution.py:478
  32.2 2.8 %collective-permute-done.8.s2 = bf16[4,128,128]{2,1,0:T(8,128)(2,1)S(1)} collective-permute-done((bf16[4,128,128]{2,1,0:T(8,128)(2,1)S(1)}, bf16[4,128,128]{2,1,0:T(8,128)(2,1)S(1)}, u32[]{:S(2)}, u32[]{:S(2)}) %collective-permute-start.8) | collective-permute-done | bytes 131104 | tf_op jit(solution)/shard_map/ppermute | solution.py:574
  35.0 1.1 %finish.1 = (bf16[128,512]{1,0:T(8,128)(2,1)S(1)}, bf16[128,512]{1,0:T(8,128)(2,1)S(1)}) custom-call(f32[4]{0:T(128)S(1)} %copy-done, f32[256,1]{1,0:T(8,128)S(1)} %get-tuple-element.32.refs_1_.place_ref, f32[1,512]{1,0:T(1,128)S(1)} %bitcast.1, f32[256,512]{1,0:T(8,128)S(1)} %inner.1.in_ref, bf16[128,512]{1,0:T(8,128)(2,1)S(1)} %get-tuple-element.41.q0, ...), custom_call_target="tpu_custom_call" | custom-call | tf_op jit(solution)/shard_map/finish/pallas_call | solution.py:478
  36.1 1.6 %collective-permute-start.10 = (bf16[128,512]{1,0:T(8,128)(2,1)S(1)}, bf16[128,512]{1,0:T(8,128)(2,1)S(1)}, u32[]{:S(2)}, u32[]{:S(2)}) collective-permute-start(bf16[128,512]{1,0:T(8,128)(2,1)S(1)} %get-tuple-element.54), channel_id=1, source_target_pairs={{0,1},{1,0},{2,3},{3,2},{4,5},{5,4},{6,7},{7,6},{8,9},{9,8},{10,11... | collective-permute-start | bytes 393224 | tf_op jit(solution)/shard_map/ppermute | solution.py:132
  37.8 1.0 %out_own.1.own_ref = f32[128,6144]{1,0:T(8,128)S(1)} custom-call(bf16[128,512]{1,0:T(8,128)(2,1)S(1)} %get-tuple-element.52.y_ref, bf16[512,6144]{1,0:T(8,128)(2,1)S(1)} %get-tuple-element.53.w_ref), custom_call_target="tpu_custom_call" | custom-call | flops 805306368 | bytes 6291456 | tf_op jit(solution)/shard_map/out_own/pallas_call | solution.py:498
  38.8 1.0 %out_rows.1 = (bf16[32,6144]{1,0:T(8,128)(2,1)S(1)}, f32[32,6144]{1,0:T(8,128)S(1)}, bf16[32,6144]{1,0:T(8,128)(2,1)S(1)}, f32[32,6144]{1,0:T(8,128)S(1)}) custom-call(f32[128,6144]{1,0:T(8,128)S(1)} %out_own.1.own_ref, bf16[128,512]{1,0:T(8,128)(2,1)S(1)} %collective-permute-done.10.z_ref, bf16[512,6144]{1,0:T(8,128)(2,1)S(1)} %collective-permute-done.11.u_ref), custom_call_target="tpu_custom_call" | custom-call | flops 805306368 | bytes 6291456 | tf_op jit(solution)/shard_map/out_rows/pallas_call | solution.py:527
  39.8 1.1 %collective-permute-start.13 = (bf16[32,6144]{1,0:T(8,128)(2,1)S(1)}, bf16[32,6144]{1,0:T(8,128)(2,1)S(1)}, u32[]{:S(2)}, u32[]{:S(2)}) collective-permute-start(bf16[32,6144]{1,0:T(8,128)(2,1)S(1)} %get-tuple-element.58), channel_id=1, source_target_pairs={{0,4},{1,3},{2,6},{3,1},{4,0},{5,7},{6,2},{7,5},{8,12},{9,11},{10,... | collective-permute-start | bytes 1179656 | tf_op jit(solution)/shard_map/ppermute | solution.py:132
  40.9 0.4 collective-permute-start.12
  41.3 5.5 %collective-permute-done.13 = bf16[32,6144]{1,0:T(8,128)(2,1)S(1)} collective-permute-done((bf16[32,6144]{1,0:T(8,128)(2,1)S(1)}, bf16[32,6144]{1,0:T(8,128)(2,1)S(1)}, u32[]{:S(2)}, u32[]{:S(2)}) %collective-permute-start.13) | collective-permute-done | bytes 393248 | tf_op jit(solution)/shard_map/ppermute | solution.py:132
  46.8 0.1 add_convert_fusion.1
  46.9 1.3 %collective-permute-start.14 = (bf16[32,6144]{1,0:T(8,128)(2,1)S(1)}, bf16[32,6144]{1,0:T(8,128)(2,1)S(1)}, u32[]{:S(2)}, u32[]{:S(2)}) collective-permute-start(bf16[32,6144]{1,0:T(8,128)(2,1)S(1)} %add_convert_fusion.1), channel_id=1, source_target_pairs={{0,2},{1,5},{2,0},{3,7},{4,6},{5,1},{6,4},{7,3},{8,10},{9,13},{10,... | collective-permute-start | bytes 1179656 | tf_op jit(solution)/shard_map/ppermute | solution.py:132
  48.2 2.8 %collective-permute-done.12 = bf16[32,6144]{1,0:T(8,128)(2,1)S(1)} collective-permute-done((bf16[32,6144]{1,0:T(8,128)(2,1)S(1)}, bf16[32,6144]{1,0:T(8,128)(2,1)S(1)}, u32[]{:S(2)}, u32[]{:S(2)}) %collective-permute-start.12) | collective-permute-done | bytes 393248 | tf_op jit(solution)/shard_map/ppermute | solution.py:132
  51.1 4.6 %collective-permute-done.14 = bf16[32,6144]{1,0:T(8,128)(2,1)S(1)} collective-permute-done((bf16[32,6144]{1,0:T(8,128)(2,1)S(1)}, bf16[32,6144]{1,0:T(8,128)(2,1)S(1)}, u32[]{:S(2)}, u32[]{:S(2)}) %collective-permute-start.14) | collective-permute-done | bytes 393248 | tf_op jit(solution)/shard_map/ppermute | solution.py:132
  55.7 0.8 %add_convert_fusion = bf16[32,6144]{1,0:T(8,128)(2,1)} fusion(f32[32,6144]{1,0:T(8,128)S(1)} %convert_add_fusion, bf16[32,6144]{1,0:T(8,128)(2,1)S(1)} %collective-permute-done.14), kind=kLoop, calls=%fused_computation | loop fusion | flops 589824 | bytes 1572864 | tf_op jit(solution)/shard_map/convert_element_type | solution.py:594
  (19 shorter events, 0.1 us)
Async XLA Ops:
  0.0 7.8 %copy-start.2 = (bf16[32,6144]{1,0:T(8,128)(2,1)S(1)}, bf16[32,6144]{1,0:T(8,128)(2,1)}, u32[]{:S(2)}) copy-start(bf16[32,6144]{1,0:T(8,128)(2,1)} %pass_ref.3) | copy-start | bytes 1179652
  0.0 38.8 %collective-permute-start.11 = (bf16[512,6144]{1,0:T(8,128)(2,1)}, bf16[512,6144]{1,0:T(8,128)(2,1)S(1)}, u32[]{:S(2)}, u32[]{:S(2)}) collective-permute-start(bf16[512,6144]{1,0:T(8,128)(2,1)} %w_hbm.5), channel_id=1, source_target_pairs={{0,1},{1,0},{2,3},{3,2},{4,5},{5,4},{6,7},{7,6},{8,9},{9,8},{10,11... | collective-permute-start | bytes 18874376 | tf_op jit(solution)/shard_map/ppermute | solution.py:132
  0.7 7.8 %collective-permute-start.1 = (bf16[32,6144]{1,0:T(8,128)(2,1)}, bf16[32,6144]{1,0:T(8,128)(2,1)S(1)}, u32[]{:S(2)}, u32[]{:S(2)}) collective-permute-start(bf16[32,6144]{1,0:T(8,128)(2,1)} %pass_ref.3), channel_id=1, source_target_pairs={{0,2},{1,5},{2,0},{3,7},{4,6},{5,1},{6,4},{7,3},{8,10},{9,13},{10,... | collective-permute-start | bytes 1179656 | tf_op jit(solution)/shard_map/ppermute | solution.py:132
  6.6 8.0 %collective-permute-start.2 = (bf16[32,6144]{1,0:T(8,128)(2,1)S(1)}, bf16[32,6144]{1,0:T(8,128)(2,1)S(1)}, u32[]{:S(2)}, u32[]{:S(2)}) collective-permute-start(bf16[32,6144]{1,0:T(8,128)(2,1)S(1)} %get-tuple-element.34.refs_0_), channel_id=1, source_target_pairs={{0,4},{1,3},{2,6},{3,1},{4,0},{5,7},{6,2},{7,5},{8,12},{9,11},{10,... | collective-permute-start | bytes 1179656 | tf_op jit(solution)/shard_map/ppermute | solution.py:132
  7.8 6.9 %collective-permute-start = (bf16[32,6144]{1,0:T(8,128)(2,1)S(1)}, bf16[32,6144]{1,0:T(8,128)(2,1)S(1)}, u32[]{:S(2)}, u32[]{:S(2)}) collective-permute-start(bf16[32,6144]{1,0:T(8,128)(2,1)S(1)} %copy-done.2), channel_id=1, source_target_pairs={{0,1},{1,0},{2,3},{3,2},{4,5},{5,4},{6,7},{7,6},{8,9},{9,8},{10,11... | collective-permute-start | bytes 1179656 | tf_op jit(solution)/shard_map/ppermute | solution.py:132
  8.5 9.9 %collective-permute-start.5 = (bf16[32,6144]{1,0:T(8,128)(2,1)S(1)}, bf16[32,6144]{1,0:T(8,128)(2,1)S(1)}, u32[]{:S(2)}, u32[]{:S(2)}) collective-permute-start(bf16[32,6144]{1,0:T(8,128)(2,1)S(1)} %tie.2.refs_2_), channel_id=1, source_target_pairs={{0,4},{1,3},{2,6},{3,1},{4,0},{5,7},{6,2},{7,5},{8,12},{9,11},{10,... | collective-permute-start | bytes 1179656 | tf_op jit(solution)/shard_map/ppermute | solution.py:132
  13.3 6.7 %collective-permute-start.3 = (bf16[32,6144]{1,0:T(8,128)(2,1)S(1)}, bf16[32,6144]{1,0:T(8,128)(2,1)S(1)}, u32[]{:S(2)}, u32[]{:S(2)}) collective-permute-start(bf16[32,6144]{1,0:T(8,128)(2,1)S(1)} %tie.2.refs_2_), channel_id=1, source_target_pairs={{0,1},{1,0},{2,3},{3,2},{4,5},{5,4},{6,7},{7,6},{8,9},{9,8},{10,11... | collective-permute-start | bytes 1179656 | tf_op jit(solution)/shard_map/ppermute | solution.py:132
  14.6 5.4 %collective-permute-start.4 = (bf16[32,6144]{1,0:T(8,128)(2,1)S(1)}, bf16[32,6144]{1,0:T(8,128)(2,1)S(1)}, u32[]{:S(2)}, u32[]{:S(2)}) collective-permute-start(bf16[32,6144]{1,0:T(8,128)(2,1)S(1)} %collective-permute-done.2.refs_3_), channel_id=1, source_target_pairs={{0,1},{1,0},{2,3},{3,2},{4,5},{5,4},{6,7},{7,6},{8,9},{9,8},{10,11... | collective-permute-start | bytes 1179656 | tf_op jit(solution)/shard_map/ppermute | solution.py:132
  18.3 2.0 %copy-start = (f32[4]{0:T(128)S(1)}, f32[4]{0:T(128)}, u32[]{:S(2)}) copy-start(f32[4]{0:T(128)} %rate_ref.5) | copy-start | bytes 52
  18.4 1.9 %collective-permute-start.6 = (bf16[32,6144]{1,0:T(8,128)(2,1)S(1)}, bf16[32,6144]{1,0:T(8,128)(2,1)S(1)}, u32[]{:S(2)}, u32[]{:S(2)}) collective-permute-start(bf16[32,6144]{1,0:T(8,128)(2,1)S(1)} %tie.3.refs_2_), channel_id=1, source_target_pairs={{0,1},{1,0},{2,3},{3,2},{4,5},{5,4},{6,7},{7,6},{8,9},{9,8},{10,11... | collective-permute-start | bytes 1179656 | tf_op jit(solution)/shard_map/ppermute | solution.py:132
  23.0 12.0 %copy-start.1 = (f32[512]{0:T(512)S(1)}, f32[512]{0:T(512)}, u32[]{:S(2)}) copy-start(f32[512]{0:T(512)} %param.8) | copy-start | bytes 6148
  23.0 9.2 %collective-permute-start.7 = (bf16[4,128,128]{2,1,0:T(8,128)(2,1)S(1)}, bf16[4,128,128]{2,1,0:T(8,128)(2,1)S(1)}, u32[]{:S(2)}, u32[]{:S(2)}) collective-permute-start(bf16[4,128,128]{2,1,0:T(8,128)(2,1)S(1)} %get-tuple-element.51), channel_id=1, source_target_pairs={{0,8},{8,16},{16,24},{24,0},{1,9},{9,17},{17,25},{25,1},{2,10},{10... | collective-permute-start | bytes 393224 | tf_op jit(solution)/shard_map/ppermute | solution.py:573
  24.3 10.7 %collective-permute-start.8 = (bf16[4,128,128]{2,1,0:T(8,128)(2,1)S(1)}, bf16[4,128,128]{2,1,0:T(8,128)(2,1)S(1)}, u32[]{:S(2)}, u32[]{:S(2)}) collective-permute-start(bf16[4,128,128]{2,1,0:T(8,128)(2,1)S(1)} %get-tuple-element.51), channel_id=1, source_target_pairs={{0,16},{8,24},{1,17},{9,25},{2,18},{10,26},{3,19},{11,27},{4,20},{... | collective-permute-start | bytes 393224 | tf_op jit(solution)/shard_map/ppermute | solution.py:574
  27.3 7.7 %collective-permute-start.9 = (bf16[4,128,128]{2,1,0:T(8,128)(2,1)S(1)}, bf16[4,128,128]{2,1,0:T(8,128)(2,1)S(1)}, u32[]{:S(2)}, u32[]{:S(2)}) collective-permute-start(bf16[4,128,128]{2,1,0:T(8,128)(2,1)S(1)} %get-tuple-element.51), channel_id=1, source_target_pairs={{0,24},{1,25},{2,26},{3,27},{4,28},{5,29},{6,30},{7,31}} | collective-permute-start | bytes 393224 | tf_op jit(solution)/shard_map/ppermute | solution.py:576
  36.1 2.6 %collective-permute-start.10 = (bf16[128,512]{1,0:T(8,128)(2,1)S(1)}, bf16[128,512]{1,0:T(8,128)(2,1)S(1)}, u32[]{:S(2)}, u32[]{:S(2)}) collective-permute-start(bf16[128,512]{1,0:T(8,128)(2,1)S(1)} %get-tuple-element.54), channel_id=1, source_target_pairs={{0,1},{1,0},{2,3},{3,2},{4,5},{5,4},{6,7},{7,6},{8,9},{9,8},{10,11... | collective-permute-start | bytes 393224 | tf_op jit(solution)/shard_map/ppermute | solution.py:132
  39.8 7.0 %collective-permute-start.13 = (bf16[32,6144]{1,0:T(8,128)(2,1)S(1)}, bf16[32,6144]{1,0:T(8,128)(2,1)S(1)}, u32[]{:S(2)}, u32[]{:S(2)}) collective-permute-start(bf16[32,6144]{1,0:T(8,128)(2,1)S(1)} %get-tuple-element.58), channel_id=1, source_target_pairs={{0,4},{1,3},{2,6},{3,1},{4,0},{5,7},{6,2},{7,5},{8,12},{9,11},{10,... | collective-permute-start | bytes 1179656 | tf_op jit(solution)/shard_map/ppermute | solution.py:132
  40.9 10.1 %collective-permute-start.12 = (bf16[32,6144]{1,0:T(8,128)(2,1)S(1)}, bf16[32,6144]{1,0:T(8,128)(2,1)S(1)}, u32[]{:S(2)}, u32[]{:S(2)}) collective-permute-start(bf16[32,6144]{1,0:T(8,128)(2,1)S(1)} %get-tuple-element.56), channel_id=1, source_target_pairs={{0,4},{1,3},{2,6},{3,1},{4,0},{5,7},{6,2},{7,5},{8,12},{9,11},{10,... | collective-permute-start | bytes 1179656 | tf_op jit(solution)/shard_map/ppermute | solution.py:132
  46.9 8.9 %collective-permute-start.14 = (bf16[32,6144]{1,0:T(8,128)(2,1)S(1)}, bf16[32,6144]{1,0:T(8,128)(2,1)S(1)}, u32[]{:S(2)}, u32[]{:S(2)}) collective-permute-start(bf16[32,6144]{1,0:T(8,128)(2,1)S(1)} %add_convert_fusion.1), channel_id=1, source_target_pairs={{0,2},{1,5},{2,0},{3,7},{4,6},{5,1},{6,4},{7,3},{8,10},{9,13},{10,... | collective-permute-start | bytes 1179656 | tf_op jit(solution)/shard_map/ppermute | solution.py:132
